TPU v7x, 256 devices: a whole 4x4x8 slice. The times are simulated.
256 devices in a mesh: vgroup: 8 (over x, core), feat: 32 (over z, y).
Axes of the slice: x: 4, y: 4, z: 8, core: 2. Of those that a mesh axis runs over, the one named last changes fastest.
Arguments:
- features_t: bfloat16 [8, 1024, 32768], P('vgroup', 'feat'), may hold values from -6 to 6
- tile_weights: bfloat16 [8, 1024, 128, 128], P('vgroup'), may hold values from -0.1875 to 0.1875
- tile_dst: int32 [8, 1024], P('vgroup'), may hold values from 0 to 127
- tile_src: int32 [8, 1024], P('vgroup'), may hold values from 0 to 255
- tile_count: int32 [8], P('vgroup'), may hold values from 256 to 1024, as said below
- w_self: bfloat16 [1024, 256], P('feat'), may hold values from -0.1875 to 0.1875
- w_neigh: bfloat16 [1024, 256], P('feat'), may hold values from -0.1875 to 0.1875
- bias: float32 [256], replicated, may hold values from -4 to 4
- grad_hidden: bfloat16 [131072, 256], P(('vgroup', 'feat')), may hold values from -1 to 1
Outputs:
- hidden: bfloat16 [131072, 256], P(('vgroup', 'feat'))
- grad_self: float32 [1024, 256], P('feat')
- grad_neigh: float32 [1024, 256], P('feat')
- grad_bias: float32 [256], replicated
Inputs may be any that keep to these rules, and one draw needn't show every extreme that they name: `tile_count`: slots at or past a group's count are ignored; at least one group has all 1024 slots live.
All inputs are finite; a program needn't handle non-finite values.
Results may differ from a plain program's by a relative error of at most 0.0075.
Values may be sent and summed in bfloat16 or wider, within the bound.
No kernel may reach another device: no remote copies, remote signals or barrier semaphores. Data moves between devices by JAX's collectives and lax.ppermute only.
A program may use at most 192 MiB of HBM per device.

v0:
```python
import jax
import jax.numpy as jnp
from jax import lax
from jax.sharding import PartitionSpec as P


def activate(pre):
    return jax.nn.gelu(pre, approximate=True)


def left_product(columns, weights):
    return lax.dot_general(
        columns, weights, (((0,), (0,)), ((), ())), preferred_element_type=jnp.float32
    )


def gathered_grads(delta, target_columns, aggregated):
    piece = lax.all_gather(delta, "feat", axis=0, tiled=True)
    grad_s = jnp.dot(target_columns, piece, preferred_element_type=jnp.float32)
    grad_n = jnp.dot(aggregated, piece, preferred_element_type=jnp.float32)
    grad_self, grad_neigh = lax.psum((grad_s, grad_n), "vgroup")
    grad_bias = lax.psum(jnp.sum(delta, axis=0, dtype=jnp.float32), ("vgroup", "feat"))
    return (grad_self, grad_neigh, grad_bias)


def body(
    features_t, tile_weights, tile_dst, tile_src, tile_count, w_self, w_neigh, bias, grad_hidden
):
    feats = features_t[0]
    tile_list = tile_weights[0]
    dsts = tile_dst[0]
    srcs = tile_src[0]
    count = tile_count[0]
    fcols, nsrc = feats.shape
    slot_total, tile_extent = (tile_list.shape[0], tile_list.shape[1])
    nfeat = lax.axis_size("feat")
    rows_dev = grad_hidden.shape[0]
    ndst = rows_dev * nfeat
    dtiles = ndst // tile_extent
    stiles = nsrc // tile_extent
    source_blocks = feats.reshape(fcols, stiles, tile_extent)
    picked = jnp.take(source_blocks, srcs, axis=1)
    product = jnp.einsum("ftk,tjk->ftj", picked, tile_list, preferred_element_type=jnp.float32)
    slot_indices = jnp.arange(slot_total)
    live = (slot_indices < count).astype(jnp.float32)
    onehot = (dsts[None, :] == jnp.arange(dtiles)[:, None]).astype(jnp.float32) * live[None, :]
    summed = jnp.einsum("dt,ftj->fdj", onehot, product, precision=lax.Precision.HIGHEST)
    aggregated = summed.reshape(fcols, ndst).astype(jnp.bfloat16)
    target_columns = feats[:, :ndst]
    pre = (
        lax.psum_scatter(
            left_product(target_columns, w_self) + left_product(aggregated, w_neigh),
            "feat",
            scatter_dimension=0,
            tiled=True,
        )
        + bias
    )
    output, pullback = jax.vjp(activate, pre)
    delta = pullback(grad_hidden.astype(jnp.float32))[0].astype(jnp.bfloat16)
    grad_self, grad_neigh, grad_bias = gathered_grads(delta, target_columns, aggregated)
    hidden = output.astype(jnp.bfloat16)
    return (hidden, grad_self, grad_neigh, grad_bias)


def solution(mesh):
    return jax.shard_map(
        body,
        mesh=mesh,
        in_specs=(
            P("vgroup", "feat", None),
            P("vgroup", None, None, None),
            P("vgroup", None),
            P("vgroup", None),
            P("vgroup"),
            P("feat", None),
            P("feat", None),
            P(),
            P(("vgroup", "feat"), None),
        ),
        out_specs=(P(("vgroup", "feat"), None), P("feat", None), P("feat", None), P()),
        check_vma=False,
    )
```

profile of v0, /device:TPU:1, one launch (start us, length us, event | category | flops | bytes accessed | tf_op | source)
XLA Modules:
  0.0 531.9 jit_solution(14090146914875210003)
XLA Ops:
  7.2 0.0 copy-start
  7.2 0.0 copy-start.5
  7.2 0.0 reduce-scatter.2.cloned.1.call-start
  7.2 2.1 copy.17
  9.3 1.4 copy.14
  10.7 0.0 copy-done.5
  11.4 9.8 %gather_fusion = bf16[1024,32,128]{2,1,0:T(8,128)(2,1)} fusion(bf16[32,256,128]{2,0,1:T(8,128)(2,1)S(1)} %copy.14, s32[1024]{0:T(1024)S(1)} %broadcast_clamp_fusion), kind=kCustom, calls=%fused_computation | custom fusion | bytes 16781312 | tf_op jit(solution)/shard_map/jit(_take)/gather | solution.py:42
  21.2 25.3 %fusion.4 = f32[32,1024,128]{2,0,1:T(8,128)} fusion(bf16[1,1024,128,128]{3,2,1,0:T(8,128)(2,1)} %param.10, bf16[1024,32,128]{2,1,0:T(8,128)(2,1)} %gather_fusion, pred[1024]{0:T(1024)(128)(4,1)S(1)} %compare_and_fusion), kind=kOutput, calls=%fused_computation.6 | convolution fusion | flops 1077936128 | bytes 58721280 | tf_op jit(solution)/shard_map/ftk,tjk->ftj/dot_general | solution.py:43
  46.5 0.0 copy-done.7
  46.5 31.9 %fusion.14 = bf16[32,128,128]{1,2,0:T(8,128)(2,1)} fusion(f32[32,1024,128]{2,0,1:T(8,128)} %fusion.4, f32[1024]{0:T(1024)S(1)} %fusion.40, s32[1024]{0:T(1024)S(1)} %bitcast.46), kind=kOutput, calls=%fused_computation.12 | convolution fusion | flops 6443237376 | bytes 17833984 | tf_op jit(solution)/shard_map/dt,ftj->fdj/dot_general | solution.py:47
  78.4 1.8 copy.16
  80.2 0.0 copy-done
  80.2 0.0 copy-done.3
  80.3 0.0 copy-start.6
  80.3 2.4 fusion.23
  82.7 0.0 copy-done.6
  82.7 8.4 %convolution_add_fusion = f32[16384,256]{1,0:T(8,128)} fusion(f32[16384,256]{1,0:T(8,128)S(1)} %fusion.23, bf16[32,256]{1,0:T(8,128)(2,1)S(1)} %copy-done.6, bf16[4,8,128,128]{3,2,1,0:T(8,128)(2,1)S(1)} %bitcast.38), kind=kOutput, calls=%fused_computation.3 | convolution fusion | flops 272629760 | bytes 34619392 | tf_op jit(solution)/shard_map/dot_general | solution.py:12
  91.1 0.0 reduce-scatter.2.cloned.1.call-update
  91.1 0.0 all-gather.2.cloned.1.call-start
  91.1 245.3 %reduce-scatter.2.cloned.1.call-done = f32[512,256]{1,0:T(8,128)} async-done(((f32[16384,256]{1,0:T(8,128)}), f32[512,256]{1,0:T(8,128)}) %reduce-scatter.2.cloned.1.call-update) | async-done | bytes 524304 | tf_op jit(solution)/shard_map/reduce_scatter | solution.py:51
  336.4 0.0 copy-done.4
  336.4 2.3 convert_reduce_fusion
  338.7 0.0 all-gather.2.cloned.1.call-update
  338.7 0.0 all-reduce.3.cloned.1.call-start
  338.8 100.9 %all-gather.2.cloned.1.call-done = bf16[16384,256]{1,0:T(8,128)(2,1)} async-done(((bf16[512,256]{1,0:T(8,128)(2,1)}), bf16[16384,256]{1,0:T(8,128)(2,1)}) %all-gather.2.cloned.1.call-update) | async-done | bytes 8388624 | tf_op jit(solution)/shard_map/all_gather | solution.py:18
  439.7 5.6 %fusion.17 = f32[32,256]{1,0:T(8,128)} fusion(bf16[16384,256]{1,0:T(8,128)(2,1)} %all-gather.2.cloned.1.call-done, bf16[4,8,128,128]{3,2,1,0:T(8,128)(2,1)S(1)} %bitcast.39), kind=kOutput, calls=%fused_computation.14 | convolution fusion | flops 268435456 | bytes 9469952 | tf_op jit(solution)/shard_map/dot_general | solution.py:20
  445.3 0.1 copy-done.2
  445.4 2.2 convolution_bitcast_fusion
  447.6 0.0 all-reduce.3.cloned.1.call-update
  447.6 75.0 %psum.23 = f32[256]{0:T(256)} all-reduce(f32[256]{0:T(256)S(1)} %get-tuple-element.6), channel_id=1, replica_groups=mesh['vgroup'=8,'feat'=32] {'vgroup','feat'}, use_global_device_ids=true, to_apply=%region_4.5 | all-reduce | flops 256 | bytes 2048 | tf_op jit(solution)/shard_map/psum | solution.py:22
  522.6 1.4 copy.36
  524.0 1.4 copy.37
  (13 shorter events, 0.0 us)
Async XLA Ops:
  7.2 73.1 %copy-start = (bf16[32,256]{1,0:T(8,128)(2,1)S(1)}, bf16[32,256]{1,0:T(8,128)(2,1)}, u32[]{:S(2)}) copy-start(bf16[32,256]{1,0:T(8,128)(2,1)} %param.14) | copy-start | bytes 49156
  7.2 3.5 copy-start.5
  7.2 329.2 %reduce-scatter.2.cloned.1.call-start = ((), (), s32[]{:S(2)}) async-start(), calls=%async_computation.1 | async-start | bytes 17301504 | tf_op jit(solution)/shard_map/reduce_scatter | solution.py:51
  21.2 25.3 %copy-start.7 = (s32[1,1024]{1,0:T(1,128)S(1)}, s32[1,1024]{1,0:T(1,128)}, u32[]{:S(2)}) copy-start(s32[1,1024]{1,0:T(1,128)} %param.11) | copy-start | bytes 12292
  46.5 33.7 %copy-start.3 = (bf16[1,32,32768]{2,1,0:T(8,128)(2,1)S(1)}, bf16[1,32,32768]{2,1,0:T(8,128)(2,1)}, u32[]{:S(2)}) copy-start(bf16[1,32,32768]{2,1,0:T(8,128)(2,1)} %param.9) | copy-start | bytes 6291460
  80.3 2.4 copy-start.6
  91.0 245.4 %copy-start.4 = (bf16[512,256]{1,0:T(8,128)(2,1)S(1)}, bf16[512,256]{1,0:T(8,128)(2,1)}, u32[]{:S(2)}) copy-start(bf16[512,256]{1,0:T(8,128)(2,1)} %param.17) | copy-start | bytes 786436
  91.1 245.4 %copy-start.8 = (f32[256]{0:T(256)S(1)}, f32[256]{0:T(256)}, u32[]{:S(2)}) copy-start(f32[256]{0:T(256)} %param.16) | copy-start | bytes 3076
  91.1 348.6 %all-gather.2.cloned.1.call-start = ((), (), s32[]{:S(2)}) async-start(), calls=%async_computation.2 | async-start | bytes 8650752 | tf_op jit(solution)/shard_map/all_gather | solution.py:18
  338.7 183.9 %all-reduce.3.cloned.1.call-start = ((), (), s32[]{:S(2)}) async-start(), calls=%async_computation.3 | async-start | bytes 131072 | tf_op jit(solution)/shard_map/psum | solution.py:21
  439.7 5.8 %copy-start.2 = (bf16[16384,256]{1,0:T(8,128)(2,1)S(1)}, bf16[16384,256]{1,0:T(8,128)(2,1)}, u32[]{:S(2)}) copy-start(bf16[16384,256]{1,0:T(8,128)(2,1)} %all-gather.2.cloned.1.call-done) | copy-start | bytes 25165828
  439.7 85.7 %copy-start.1 = (bf16[32,256]{1,0:T(8,128)(2,1)S(1)}, bf16[32,256]{1,0:T(8,128)(2,1)}, u32[]{:S(2)}) copy-start(bf16[32,256]{1,0:T(8,128)(2,1)} %param.14) | copy-start | bytes 49156
Sparse Core Ops, SparseCore 0:
  91.2 245.1 reduce-scatter.1
  339.0 100.6 all-gather.1
  447.8 59.5 all-reduce.2
where the time goes:
time: 532 us
  waiting for transfers between devices  346 us (65%)
  matrix products  75.8 us (14%)
  blocking collectives  75 us (14%)
  local copies, waits for them, and re-layouts  18 us (3%)
  between operations  14.5 us (3%)
    reduce_scatter x1, waiting for transfers between devices, body(): lax.psum_scatter(left_product(target_columns, w_self) + left_product(aggr...  245 us
    all_gather x1, waiting for transfers between devices, gathered_grads(): piece = lax.all_gather(delta, 'feat', axis=0, tiled=True)  101 us
    psum x1, blocking collectives, gathered_grads(): lax.psum(jnp.sum(delta, axis=0, dtype=jnp.float32), ('vgroup', 'feat'))  75 us
    dot_general x1, matrix products, body(): jnp.einsum('dt,ftj->fdj', onehot, product, precision=lax.Precision.HIGHEST)  31.9 us
    dot_general x1, matrix products, body(): jnp.einsum('ftk,tjk->ftj', picked, tile_list, preferred_element_type=jnp....  25.3 us
    dot_general x2, matrix products, left_product(): lax.dot_general(columns, weights, (((0,), (0,)), ((), ())), preferred_ele...  10.8 us
  transfers between devices with their start and end apart: 3, of which 2 were waited for; matrix products, arithmetic and copies ran while one was open for 0% of the time, Pallas kernels for 0%

commit v1 on v0

v1 whole, which is shorter than its diff:
```python
import jax
import jax.numpy as jnp
from jax import lax
from jax.experimental import pallas as pl
from jax.experimental.pallas import tpu as pltpu
from jax.sharding import PartitionSpec as P

TILE = 128
SLOTS_STEP = 128
UNROLL = 32
GELU_A = 0.7978845608
GELU_B = 0.044715
BF16 = jnp.bfloat16
F32 = jnp.float32


def aggregate(dsts, srcs, count, feats, weights, nfeat):
    fcols, nsrc = feats.shape
    slots = weights.shape[0]
    dtiles = nsrc // TILE // 2
    per_owner = dtiles // nfeat
    steps = slots // SLOTS_STEP

    def kernel(dst, src, cnt, x_ref, w_ref, o_ref, acc):
        i = pl.program_id(0)

        @pl.when(i == 0)
        def _():
            acc[...] = jnp.zeros_like(acc)

        base = i * SLOTS_STEP
        live = jnp.clip(cnt[0] - base, 0, SLOTS_STEP)
        zero = jnp.zeros((fcols, TILE), BF16)

        def source(slot):
            return x_ref[:, pl.ds(pl.multiple_of(src[slot] * TILE, TILE), TILE)]

        def group(g, carry):
            first = g * UNROLL
            products = []
            for u in range(0, UNROLL, 2):
                slot = base + first + u
                left = jnp.concatenate(
                    [
                        jnp.concatenate([source(slot), zero], 1),
                        jnp.concatenate([zero, source(slot + 1)], 1),
                    ],
                    0,
                )
                right = jnp.concatenate([w_ref[first + u], w_ref[first + u + 1]], 1)
                both = lax.dot_general(
                    left, right, (((1,), (1,)), ((), ())), preferred_element_type=F32
                )
                products += [both[:fcols], both[fcols:]]
            for u in range(UNROLL):
                slot = base + first + u
                acc[dst[slot]] += jnp.where(slot < cnt[0], products[u], 0.0)
            return carry

        lax.fori_loop(0, pl.cdiv(live, UNROLL), group, 0)

        @pl.when(i == steps - 1)
        def _():
            for c in range(nfeat):
                for q in range(per_owner):
                    o_ref[c, :, q * TILE : (q + 1) * TILE] = acc[c * per_owner + q].astype(BF16)

    return pl.pallas_call(
        kernel,
        grid_spec=pltpu.PrefetchScalarGridSpec(
            num_scalar_prefetch=3,
            grid=(steps,),
            in_specs=[
                pl.BlockSpec((fcols, nsrc), lambda i, *_: (0, 0)),
                pl.BlockSpec((SLOTS_STEP, TILE, TILE), lambda i, *_: (i, 0, 0)),
            ],
            out_specs=pl.BlockSpec((nfeat, fcols, per_owner * TILE), lambda i, *_: (0, 0, 0)),
            scratch_shapes=[pltpu.VMEM((dtiles, fcols, TILE), F32)],
        ),
        out_shape=jax.ShapeDtypeStruct((nfeat, fcols, per_owner * TILE), BF16),
        name="aggregate",
        compiler_params=pltpu.CompilerParams(vmem_limit_bytes=40 << 20),
        cost_estimate=pl.CostEstimate(
            flops=2 * slots * fcols * TILE * TILE,
            bytes_accessed=slots * TILE * TILE * 2 + fcols * nsrc * 2,
            transcendentals=0,
        ),
    )(dsts, srcs, count, feats, weights)


def contract_rows(a, b):
    return lax.dot_general(a, b, (((0,), (0,)), ((), ())), preferred_element_type=F32)


def own_part(place, w_rel, x_rows, bias):
    ny, nv, two_f, hid = w_rel.shape
    fcols = two_f // 2
    feats, rows = x_rows.shape

    def kernel(at, w_ref, x_ref, b_ref, pre_ref, wn_ref, ws):
        for j in range(ny):
            for k in range(nv):
                z = lax.rem(at[1] + lax.bitwise_xor(at[0], k), nv)
                y = lax.bitwise_xor(at[2], j)
                start = pl.multiple_of((z * ny + y) * fcols, fcols)
                ws[pl.ds(start, fcols), :] = w_ref[j, k, :fcols, :]
                wn_ref[pl.ds(start, fcols), :] = w_ref[j, k, fcols:, :]
        pre_ref[...] = contract_rows(x_ref[...], ws[...]) + b_ref[...]

    return pl.pallas_call(
        kernel,
        in_specs=[pl.BlockSpec(memory_space=pltpu.SMEM)]
        + [pl.BlockSpec(memory_space=pltpu.VMEM)] * 3,
        out_specs=[pl.BlockSpec(memory_space=pltpu.VMEM)] * 2,
        out_shape=[
            jax.ShapeDtypeStruct((rows, hid), F32),
            jax.ShapeDtypeStruct((feats, hid), BF16),
        ],
        scratch_shapes=[pltpu.VMEM((feats, hid), BF16)],
        name="own_part",
        compiler_params=pltpu.CompilerParams(vmem_limit_bytes=40 << 20),
        cost_estimate=pl.CostEstimate(
            flops=2 * feats * rows * hid, bytes_accessed=4 << 20, transcendentals=0
        ),
    )(place, w_rel, x_rows, bias)


def layer(place, pre_own, a_rows, w_neigh, x_rows, upstream):
    feats, rows = x_rows.shape
    hid = upstream.shape[1]

    def kernel(at, pre_ref, a_ref, wn_ref, x_ref, up_ref, hid_ref, g_ref, gb_ref):
        v = pre_ref[...] + contract_rows(a_ref[...], wn_ref[...])
        sq = v * v
        t = jnp.tanh(GELU_A * (v + GELU_B * sq * v))
        half = 0.5 * (1.0 + t)
        hid_ref[...] = (v * half).astype(BF16)
        slope = half + 0.5 * v * (1.0 - t * t) * (GELU_A * (1.0 + 3.0 * GELU_B * sq))
        delta = (up_ref[...].astype(F32) * slope).astype(BF16)
        gb_ref[...] = jnp.sum(delta.astype(F32), axis=0, keepdims=True)
        core = lax.rem(at[0], 2)
        g_ref[core] = jnp.dot(x_ref[...], delta, preferred_element_type=F32).astype(BF16)
        g_ref[1 - core] = jnp.dot(a_ref[...], delta, preferred_element_type=F32).astype(BF16)

    return pl.pallas_call(
        kernel,
        in_specs=[pl.BlockSpec(memory_space=pltpu.SMEM)]
        + [pl.BlockSpec(memory_space=pltpu.VMEM)] * 5,
        out_specs=[pl.BlockSpec(memory_space=pltpu.VMEM)] * 3,
        out_shape=[
            jax.ShapeDtypeStruct((rows, hid), BF16),
            jax.ShapeDtypeStruct((2, feats, hid), BF16),
            jax.ShapeDtypeStruct((1, hid), F32),
        ],
        name="layer",
        compiler_params=pltpu.CompilerParams(vmem_limit_bytes=40 << 20),
        cost_estimate=pl.CostEstimate(
            flops=6 * feats * rows * hid, bytes_accessed=6 << 20, transcendentals=rows * hid
        ),
    )(place, pre_own, a_rows, w_neigh, x_rows, upstream)


def body(nz, ny, features_t, tile_weights, tile_dst, tile_src, tile_count, w_self, w_neigh, bias, grad_hidden):
    feats = features_t[0]
    fcols, nsrc = feats.shape
    nv = lax.axis_size("vgroup")
    nfeat = lax.axis_size("feat")
    rows_dev, hid = grad_hidden.shape
    ndst = rows_dev * nfeat
    v = lax.axis_index("vgroup")
    f = lax.axis_index("feat")
    place = jnp.stack([v, f // ny, f % ny]).astype(jnp.int32)

    with jax.named_scope("send_features"):
        x_out = feats[:, :ndst].reshape(fcols, nfeat, rows_dev).transpose(1, 0, 2)
        x_rows = lax.all_to_all(x_out, "feat", 0, 0, tiled=True).reshape(nfeat * fcols, rows_dev)

    with jax.named_scope("gather_weights"):
        own = jnp.concatenate([w_self, w_neigh], axis=0)
        shift = [
            (a * nfeat + z * ny + y, a * nfeat + ((z - a) % nz) * ny + y)
            for a in range(nv)
            for z in range(nz)
            for y in range(ny)
        ]
        one = lax.ppermute(own, ("vgroup", "feat"), shift)
        column = jnp.stack(
            [one]
            + [lax.ppermute(one, "vgroup", [(a, a ^ k) for a in range(nv)]) for k in range(1, nv)]
        )
        w_rel = jnp.stack(
            [column]
            + [
                lax.ppermute(column, "feat", [(a, (a // ny) * ny + ((a % ny) ^ j)) for a in range(nfeat)])
                for j in range(1, ny)
            ]
        )

    agg = aggregate(tile_dst[0], tile_src[0], tile_count, feats, tile_weights[0], nfeat)
    with jax.named_scope("send_aggregated"):
        a_rows = lax.all_to_all(agg, "feat", 0, 0, tiled=True).reshape(nfeat * fcols, rows_dev)

    pre_own, wn = own_part(place, w_rel, x_rows, bias[None, :])
    hidden, grads, gb = layer(place, pre_own, a_rows, wn, x_rows, grad_hidden)

    with jax.named_scope("reduce_grads"):
        other_core = [(a, a ^ 1) for a in range(nv)]
        got = lax.ppermute(grads[1], "vgroup", other_core)
        pair = (grads[0].astype(F32) + got.astype(F32)).astype(BF16).reshape(nfeat, fcols, hid)
        gb = gb + lax.ppermute(gb, "vgroup", other_core)
        high = lax.reduce_precision(gb, 8, 7)
        mid = lax.reduce_precision(gb - high, 8, 7)
        low = gb - high - mid
        split = jnp.concatenate([high, mid, low, jnp.zeros((5, hid), F32)], 0).astype(BF16)
        outgoing = jnp.concatenate([pair, jnp.broadcast_to(split[None], (nfeat, 8, hid))], axis=1)
        arrived = lax.all_to_all(outgoing, "feat", 0, 0, tiled=True)
        total = jnp.sum(arrived.astype(F32), axis=0)
        parts = [total] + [
            lax.ppermute(total, "vgroup", [(a, a ^ (2 * k)) for a in range(nv)]) for k in range(1, nv // 2)
        ]
        total = sum(parts[1:], parts[0])
        other = lax.ppermute(total[:fcols], "vgroup", other_core)
        first = v % 2 == 0
        mine = total[:fcols]
        grad_self = jnp.where(first, mine, other)
        grad_neigh = jnp.where(first, other, mine)
        grad_bias = jnp.sum(total[fcols:], axis=0)
    return (hidden, grad_self, grad_neigh, grad_bias)


def solution(mesh):
    ny = 4
    nz = mesh.shape["feat"] // ny

    def run(*args):
        return body(nz, ny, *args)

    return jax.shard_map(
        run,
        mesh=mesh,
        in_specs=(
            P("vgroup", "feat", None),
            P("vgroup", None, None, None),
            P("vgroup", None),
            P("vgroup", None),
            P("vgroup"),
            P("feat", None),
            P("feat", None),
            P(),
            P(("vgroup", "feat"), None),
        ),
        out_specs=(P(("vgroup", "feat"), None), P("feat", None), P("feat", None), P()),
        check_vma=False,
    )
```

time: 532 us -> 130 us (0.24)
  waiting for transfers between devices: 346 us -> 27.2 us
  matrix products: 75.8 us -> 0 us
  blocking collectives: 75 us -> 23.9 us
  starting transfers between devices: 0.12 us -> 48.7 us
  Pallas kernels: 0 us -> 22.8 us
  local copies, waits for them, and re-layouts: 18 us -> 3.58 us
  between operations: 14.5 us -> 1.52 us
    reduce_scatter x1 -> x0, waiting for transfers between devices: 245 us -> none  [body(): lax.psum_scatter(left_product(target_columns, w_self) + left_product(aggr...]
    all_gather x1 -> x0, waiting for transfers between devices: 101 us -> none  [gathered_grads(): piece = lax.all_gather(delta, 'feat', axis=0, tiled=True)]
    dot_general x6 -> x0, matrix products: 75.8 us -> none  [the longest x1 31.9 us: body(): jnp.einsum('dt,ftj->fdj', onehot, product, precision=lax.Precision.HIGHEST)]
    psum x1 -> x0, blocking collectives: 75 us -> none  [gathered_grads(): lax.psum(jnp.sum(delta, axis=0, dtype=jnp.float32), ('vgroup', 'feat'))]
    ppermute x0 -> x17, starting transfers between devices: none -> 30.1 us  [the longest x7 11.4 us: body(): lax.ppermute(one, 'vgroup', [(a, a ^ k) for a in range(nv)])]
    ppermute x0 -> x17, waiting for transfers between devices: none -> 25.9 us  [the longest x3 16.6 us: body(): lax.ppermute(column, 'feat', [(a, a // ny * ny + (a % ny ^ j)) for a in r...]
    all_to_all x0 -> x1, blocking collectives: none -> 23.9 us  [body(): arrived = lax.all_to_all(outgoing, 'feat', 0, 0, tiled=True)]
    pallas_call x0 -> x3, Pallas kernels: none -> 22.8 us  [the longest x1 18.8 us: aggregate(): pl.pallas_call(kernel, grid_spec=pltpu.PrefetchScalarGridSpec(num_scalar_...]
  transfers between devices with their start and end apart: 3 -> 19, of which waited for: 2 -> 10; matrix products, arithmetic and copies ran while one was open for 0% -> 1% of each run, Pallas kernels for 0% -> 15%
where the time goes in v1:
time: 130 us
  starting transfers between devices  48.7 us (37%)
  waiting for transfers between devices  27.2 us (21%)
  blocking collectives  23.9 us (18%)
  Pallas kernels  22.8 us (18%)
  local copies, waits for them, and re-layouts  3.58 us (3%)
  other arithmetic  1.79 us (1%)
  between operations  1.52 us (1%)
    all_to_all x1, blocking collectives, body(): arrived = lax.all_to_all(outgoing, 'feat', 0, 0, tiled=True)  23.9 us
    pallas_call x1, Pallas kernels, aggregate(): pl.pallas_call(kernel, grid_spec=pltpu.PrefetchScalarGridSpec(num_scalar_...  18.8 us
    ppermute x3, waiting for transfers between devices, body(): lax.ppermute(column, 'feat', [(a, a // ny * ny + (a % ny ^ j)) for a in r...  16.6 us
    all_to_all x1, starting transfers between devices, body(): lax.all_to_all(x_out, 'feat', 0, 0, tiled=True)  12.2 us
    ppermute x7, starting transfers between devices, body(): lax.ppermute(one, 'vgroup', [(a, a ^ k) for a in range(nv)])  11.4 us
    all_to_all x1, starting transfers between devices, body(): lax.all_to_all(agg, 'feat', 0, 0, tiled=True)  6.47 us
    ppermute x3, starting transfers between devices, body(): lax.ppermute(total, 'vgroup', [(a, a ^ 2 * k) for a in range(nv)])  4.62 us
    ppermute x1, starting transfers between devices, body(): one = lax.ppermute(own, ('vgroup', 'feat'), shift)  4.42 us
  transfers between devices with their start and end apart: 19, of which 10 were waited for; matrix products, arithmetic and copies ran while one was open for 1% of the time, Pallas kernels for 15%

profile of v1, /device:TPU:1, one launch (start us, length us, event | category | flops | bytes accessed | tf_op | source)
XLA Modules:
  0.0 129.6 jit_solution(5285891456583297455)
XLA Ops:
  0.6 1.3 slice.21
  2.0 1.2 copy.16
  3.1 12.2 %all-to-all-start = ((bf16[32,32,512]{2,1,0:T(8,128)(2,1)}), bf16[32,32,512]{2,1,0:T(8,128)(2,1)S(1)}, u32[]{:S(2)}, u32[]{:S(2)}) async-start(bf16[32,32,512]{2,1,0:T(8,128)(2,1)} %bitcast.52), calls=%async_computation | async-start | bytes 2097152 | tf_op jit(solution)/shard_map/send_features/all_to_all | solution.py:176
  15.3 4.4 %collective-permute-start = (bf16[64,256]{1,0:T(8,128)(2,1)S(1)}, bf16[64,256]{1,0:T(8,128)(2,1)S(1)}, u32[]{:S(2)}, u32[]{:S(2)}) collective-permute-start(bf16[64,256]{1,0:T(8,128)(2,1)S(1)} %pad_maximum_fusion.2), channel_id=1, source_target_pairs={{0,0},{1,1},{2,2},{3,3},{4,4},{5,5},{6,6},{7,7},{8,8},{9,9},{10,10... | collective-permute-start | bytes 98312 | tf_op jit(solution)/shard_map/gather_weights/ppermute | solution.py:186
  20.4 18.8 %aggregate.1 = bf16[32,32,512]{2,1,0:T(8,128)(2,1)S(1)} custom-call(s32[1024]{0:T(1024)S(1)} %bitcast.48, s32[1024]{0:T(1024)S(1)} %bitcast.49, s32[1]{0:T(128)S(6)} %copy.24.cnt, bf16[32,32768]{1,0:T(8,128)(2,1)S(1)} %bitcast.46, bf16[1024,128,128]{2,1,0:T(8,128)(2,1)} %bitcast.51), custom_call_target="tpu_custom_call" | custom-call | flops 1073741824 | bytes 35651584 | tf_op jit(solution)/shard_map/aggregate/pallas_call | solution.py:68
  39.3 0.9 copy-done.1
  40.2 1.3 all-to-all-done
  41.5 6.5 %all-to-all-start.1 = ((bf16[32,32,512]{2,1,0:T(8,128)(2,1)}), bf16[32,32,512]{2,1,0:T(8,128)(2,1)S(1)}, u32[]{:S(2)}, u32[]{:S(2)}) async-start(bf16[32,32,512]{2,1,0:T(8,128)(2,1)} %copy-done.1), calls=%async_computation.1 | async-start | bytes 2097152 | tf_op jit(solution)/shard_map/send_aggregated/all_to_all | solution.py:201
  48.0 4.1 %collective-permute-start.2 = (bf16[64,256]{1,0:T(8,128)(2,1)S(1)}, bf16[64,256]{1,0:T(8,128)(2,1)S(1)}, u32[]{:S(2)}, u32[]{:S(2)}) collective-permute-start(bf16[64,256]{1,0:T(8,128)(2,1)S(1)} %collective-permute-done), channel_id=1, source_target_pairs={{0,64},{32,96},{64,0},{96,32},{128,192},{160,224},{192,128},{224,1... | collective-permute-start | bytes 98312 | tf_op jit(solution)/shard_map/gather_weights/ppermute | solution.py:189
  52.4 3.8 %collective-permute-start.4 = (bf16[64,256]{1,0:T(8,128)(2,1)S(1)}, bf16[64,256]{1,0:T(8,128)(2,1)S(1)}, u32[]{:S(2)}, u32[]{:S(2)}) collective-permute-start(bf16[64,256]{1,0:T(8,128)(2,1)S(1)} %collective-permute-done), channel_id=1, source_target_pairs={{0,128},{32,160},{64,192},{96,224},{128,0},{160,32},{192,64},{224,... | collective-permute-start | bytes 98312 | tf_op jit(solution)/shard_map/gather_weights/ppermute | solution.py:189
  56.1 2.1 %collective-permute-start.6 = (bf16[64,256]{1,0:T(8,128)(2,1)S(1)}, bf16[64,256]{1,0:T(8,128)(2,1)S(1)}, u32[]{:S(2)}, u32[]{:S(2)}) collective-permute-start(bf16[64,256]{1,0:T(8,128)(2,1)S(1)} %collective-permute-done), channel_id=1, source_target_pairs={{0,192},{32,224},{64,128},{96,160},{128,64},{160,96},{192,0},{224,... | collective-permute-start | bytes 98312 | tf_op jit(solution)/shard_map/gather_weights/ppermute | solution.py:189
  58.2 1.2 collective-permute-start.7
  59.4 1.8 %collective-permute-done.5 = bf16[64,256]{1,0:T(8,128)(2,1)S(1)} collective-permute-done((bf16[64,256]{1,0:T(8,128)(2,1)S(1)}, bf16[64,256]{1,0:T(8,128)(2,1)S(1)}, u32[]{:S(2)}, u32[]{:S(2)}) %collective-permute-start.5) | collective-permute-done | bytes 32800 | tf_op jit(solution)/shard_map/gather_weights/ppermute | solution.py:189
  61.3 1.8 %collective-permute-done.7 = bf16[64,256]{1,0:T(8,128)(2,1)S(1)} collective-permute-done((bf16[64,256]{1,0:T(8,128)(2,1)S(1)}, bf16[64,256]{1,0:T(8,128)(2,1)S(1)}, u32[]{:S(2)}, u32[]{:S(2)}) %collective-permute-start.7) | collective-permute-done | bytes 32800 | tf_op jit(solution)/shard_map/gather_weights/ppermute | solution.py:189
  63.1 1.5 %collective-permute-start.8 = (bf16[8,64,256]{2,1,0:T(8,128)(2,1)S(1)}, bf16[8,64,256]{2,1,0:T(8,128)(2,1)S(1)}, u32[]{:S(2)}, u32[]{:S(2)}) collective-permute-start(bf16[8,64,256]{2,1,0:T(8,128)(2,1)S(1)} %bitcast_dynamic-update-slice_fusion), channel_id=1, source_target_pairs={{0,1},{1,0},{2,3},{3,2},{4,5},{5,4},{6,7},{7,6},{8,9},{9,8},{10,11... | collective-permute-start | bytes 786440 | tf_op jit(solution)/shard_map/gather_weights/ppermute | solution.py:194
  64.6 2.4 %collective-permute-start.9 = (bf16[8,64,256]{2,1,0:T(8,128)(2,1)S(1)}, bf16[8,64,256]{2,1,0:T(8,128)(2,1)S(1)}, u32[]{:S(2)}, u32[]{:S(2)}) collective-permute-start(bf16[8,64,256]{2,1,0:T(8,128)(2,1)S(1)} %bitcast_dynamic-update-slice_fusion), channel_id=1, source_target_pairs={{0,2},{1,3},{2,0},{3,1},{4,6},{5,7},{6,4},{7,5},{8,10},{9,11},{10,... | collective-permute-start | bytes 786440 | tf_op jit(solution)/shard_map/gather_weights/ppermute | solution.py:194
  67.0 7.6 %collective-permute-done.8 = bf16[8,64,256]{2,1,0:T(8,128)(2,1)S(1)} collective-permute-done((bf16[8,64,256]{2,1,0:T(8,128)(2,1)S(1)}, bf16[8,64,256]{2,1,0:T(8,128)(2,1)S(1)}, u32[]{:S(2)}, u32[]{:S(2)}) %collective-permute-start.8) | collective-permute-done | bytes 262176 | tf_op jit(solution)/shard_map/gather_weights/ppermute | solution.py:194
  74.6 7.9 %collective-permute-done.9 = bf16[8,64,256]{2,1,0:T(8,128)(2,1)S(1)} collective-permute-done((bf16[8,64,256]{2,1,0:T(8,128)(2,1)S(1)}, bf16[8,64,256]{2,1,0:T(8,128)(2,1)S(1)}, u32[]{:S(2)}, u32[]{:S(2)}) %collective-permute-start.9) | collective-permute-done | bytes 262176 | tf_op jit(solution)/shard_map/gather_weights/ppermute | solution.py:194
  82.5 1.1 collective-permute-done.10
  83.8 1.1 own_part.1
  84.9 2.9 %layer.1 = (bf16[512,256]{1,0:T(8,128)(2,1)}, bf16[2,1024,256]{2,1,0:T(8,128)(2,1)S(1)}, f32[1,256]{1,0:T(1,128)S(1)}) custom-call(s32[3]{0:T(128)S(1)} %pad_add_fusion.at, f32[512,256]{1,0:T(8,128)S(1)} %get-tuple-element.9.pre_ref, bf16[1024,512]{1,0:T(8,128)(2,1)S(1)} %bitcast.47, bf16[1024,256]{1,0:T(8,128)(2,1)S(1)} %get-tuple-element.10.wn_ref, ...), custom_call_target="tpu_custom_call" | custom-call | flops 805306368 | bytes 6291456 | tf_op jit(solution)/shard_map/layer/pallas_call | solution.py:145
  87.9 1.4 %collective-permute-start.11 = (bf16[1024,256]{1,0:T(8,128)(2,1)S(1)}, bf16[1024,256]{1,0:T(8,128)(2,1)S(1)}, u32[]{:S(2)}, u32[]{:S(2)}) collective-permute-start(bf16[1024,256]{1,0:T(8,128)(2,1)S(1)} %slice_bitcast_fusion), channel_id=1, source_target_pairs={{0,32},{32,0},{64,96},{96,64},{128,160},{160,128},{192,224},{224,1... | collective-permute-start | bytes 1572872 | tf_op jit(solution)/shard_map/reduce_grads/ppermute | solution.py:208
  89.5 1.4 %collective-permute-done.12 = f32[1,256]{1,0:T(1,128)S(1)} collective-permute-done((f32[1,256]{1,0:T(1,128)S(1)}, f32[1,256]{1,0:T(1,128)S(1)}, u32[]{:S(2)}, u32[]{:S(2)}) %collective-permute-start.12) | collective-permute-done | bytes 1056 | tf_op jit(solution)/shard_map/reduce_grads/ppermute | solution.py:210
  91.1 23.9 %all_to_all.15 = bf16[32,40,256]{2,1,0:T(8,128)(2,1)S(1)} all-to-all(bf16[32,40,256]{2,1,0:T(8,128)(2,1)S(1)} %pad_maximum_fusion.1), channel_id=1, replica_groups=mesh['vgroup'=8,'feat'=32] {'feat'}, dimensions={0} | all-to-all | bytes 1310720 | tf_op jit(solution)/shard_map/reduce_grads/all_to_all | solution.py:216
  115.2 2.0 %collective-permute-start.13 = (f32[40,256]{1,0:T(8,128)S(1)}, f32[40,256]{1,0:T(8,128)S(1)}, u32[]{:S(2)}, u32[]{:S(2)}) collective-permute-start(f32[40,256]{1,0:T(8,128)S(1)} %convert_reduce_fusion), channel_id=1, source_target_pairs={{0,64},{32,96},{64,0},{96,32},{128,192},{160,224},{192,128},{224,1... | collective-permute-start | bytes 122888 | tf_op jit(solution)/shard_map/reduce_grads/ppermute | solution.py:219
  117.1 2.6 %collective-permute-start.14 = (f32[40,256]{1,0:T(8,128)S(1)}, f32[40,256]{1,0:T(8,128)S(1)}, u32[]{:S(2)}, u32[]{:S(2)}) collective-permute-start(f32[40,256]{1,0:T(8,128)S(1)} %convert_reduce_fusion), channel_id=1, source_target_pairs={{0,128},{32,160},{64,192},{96,224},{128,0},{160,32},{192,64},{224,... | collective-permute-start | bytes 122888 | tf_op jit(solution)/shard_map/reduce_grads/ppermute | solution.py:219
  119.8 1.8 %collective-permute-done.14 = f32[40,256]{1,0:T(8,128)S(1)} collective-permute-done((f32[40,256]{1,0:T(8,128)S(1)}, f32[40,256]{1,0:T(8,128)S(1)}, u32[]{:S(2)}, u32[]{:S(2)}) %collective-permute-start.14) | collective-permute-done | bytes 40992 | tf_op jit(solution)/shard_map/reduce_grads/ppermute | solution.py:219
  121.6 2.2 %collective-permute-done.15 = f32[40,256]{1,0:T(8,128)S(1)} collective-permute-done((f32[40,256]{1,0:T(8,128)S(1)}, f32[40,256]{1,0:T(8,128)S(1)}, u32[]{:S(2)}, u32[]{:S(2)}) %collective-permute-start.15) | collective-permute-done | bytes 40992 | tf_op jit(solution)/shard_map/reduce_grads/ppermute | solution.py:219
  123.9 4.2 %collective-permute-start.16 = (f32[32,256]{1,0:T(8,128)S(1)}, f32[32,256]{1,0:T(8,128)S(1)}, u32[]{:S(2)}, u32[]{:S(2)}) collective-permute-start(f32[32,256]{1,0:T(8,128)S(1)} %slice.22), channel_id=1, source_target_pairs={{0,32},{32,0},{64,96},{96,64},{128,160},{160,128},{192,224},{224,1... | collective-permute-start | bytes 98312 | tf_op jit(solution)/shard_map/reduce_grads/ppermute | solution.py:222
  128.1 0.6 slice_reduce_fusion
  128.7 0.3 collective-permute-done.16
  129.0 0.6 broadcast_select_fusion
  (52 shorter events, 1.2 us)
Async XLA Ops:
  1.9 13.4 %copy-start.6 = (bf16[32,256]{1,0:T(8,128)(2,1)S(1)}, bf16[32,256]{1,0:T(8,128)(2,1)}, u32[]{:S(2)}) copy-start(bf16[32,256]{1,0:T(8,128)(2,1)} %param.15) | copy-start | bytes 49156
  1.9 13.4 %copy-start.7 = (bf16[32,256]{1,0:T(8,128)(2,1)S(1)}, bf16[32,256]{1,0:T(8,128)(2,1)}, u32[]{:S(2)}) copy-start(bf16[32,256]{1,0:T(8,128)(2,1)} %param.14) | copy-start | bytes 49156
  3.1 17.3 %copy-start = (bf16[1,32,32768]{2,1,0:T(8,128)(2,1)S(1)}, bf16[1,32,32768]{2,1,0:T(8,128)(2,1)}, u32[]{:S(2)}) copy-start(bf16[1,32,32768]{2,1,0:T(8,128)(2,1)} %param.9) | copy-start | bytes 6291460
  3.1 17.3 %copy-start.3 = (s32[1,1024]{1,0:T(1,128)S(1)}, s32[1,1024]{1,0:T(1,128)}, u32[]{:S(2)}) copy-start(s32[1,1024]{1,0:T(1,128)} %param.11) | copy-start | bytes 12292
  3.1 17.3 %copy-start.4 = (s32[1,1024]{1,0:T(1,128)S(1)}, s32[1,1024]{1,0:T(1,128)}, u32[]{:S(2)}) copy-start(s32[1,1024]{1,0:T(1,128)} %param.12) | copy-start | bytes 12292
  3.1 38.4 %all-to-all-start = ((bf16[32,32,512]{2,1,0:T(8,128)(2,1)}), bf16[32,32,512]{2,1,0:T(8,128)(2,1)S(1)}, u32[]{:S(2)}, u32[]{:S(2)}) async-start(bf16[32,32,512]{2,1,0:T(8,128)(2,1)} %bitcast.52), calls=%async_computation | async-start | bytes 2097152 | tf_op jit(solution)/shard_map/send_features/all_to_all | solution.py:176
  15.3 24.9 %collective-permute-start = (bf16[64,256]{1,0:T(8,128)(2,1)S(1)}, bf16[64,256]{1,0:T(8,128)(2,1)S(1)}, u32[]{:S(2)}, u32[]{:S(2)}) collective-permute-start(bf16[64,256]{1,0:T(8,128)(2,1)S(1)} %pad_maximum_fusion.2), channel_id=1, source_target_pairs={{0,0},{1,1},{2,2},{3,3},{4,4},{5,5},{6,6},{7,7},{8,8},{9,9},{10,10... | collective-permute-start | bytes 98312 | tf_op jit(solution)/shard_map/gather_weights/ppermute | solution.py:186
  39.3 0.9 copy-start.1
  40.2 15.9 %collective-permute-start.1 = (bf16[64,256]{1,0:T(8,128)(2,1)S(1)}, bf16[64,256]{1,0:T(8,128)(2,1)S(1)}, u32[]{:S(2)}, u32[]{:S(2)}) collective-permute-start(bf16[64,256]{1,0:T(8,128)(2,1)S(1)} %collective-permute-done), channel_id=1, source_target_pairs={{0,32},{32,0},{64,96},{96,64},{128,160},{160,128},{192,224},{224,1... | collective-permute-start | bytes 98312 | tf_op jit(solution)/shard_map/gather_weights/ppermute | solution.py:189
  41.5 43.4 %all-to-all-start.1 = ((bf16[32,32,512]{2,1,0:T(8,128)(2,1)}), bf16[32,32,512]{2,1,0:T(8,128)(2,1)S(1)}, u32[]{:S(2)}, u32[]{:S(2)}) async-start(bf16[32,32,512]{2,1,0:T(8,128)(2,1)} %copy-done.1), calls=%async_computation.1 | async-start | bytes 2097152 | tf_op jit(solution)/shard_map/send_aggregated/all_to_all | solution.py:201
  48.0 35.8 %copy-start.5 = (f32[256]{0:T(256)S(1)}, f32[256]{0:T(256)}, u32[]{:S(2)}) copy-start(f32[256]{0:T(256)} %param.16) | copy-start | bytes 3076
  48.0 10.2 %collective-permute-start.2 = (bf16[64,256]{1,0:T(8,128)(2,1)S(1)}, bf16[64,256]{1,0:T(8,128)(2,1)S(1)}, u32[]{:S(2)}, u32[]{:S(2)}) collective-permute-start(bf16[64,256]{1,0:T(8,128)(2,1)S(1)} %collective-permute-done), channel_id=1, source_target_pairs={{0,64},{32,96},{64,0},{96,32},{128,192},{160,224},{192,128},{224,1... | collective-permute-start | bytes 98312 | tf_op jit(solution)/shard_map/gather_weights/ppermute | solution.py:189
  52.1 7.3 %collective-permute-start.3 = (bf16[64,256]{1,0:T(8,128)(2,1)S(1)}, bf16[64,256]{1,0:T(8,128)(2,1)S(1)}, u32[]{:S(2)}, u32[]{:S(2)}) collective-permute-start(bf16[64,256]{1,0:T(8,128)(2,1)S(1)} %collective-permute-done), channel_id=1, source_target_pairs={{0,96},{32,64},{64,32},{96,0},{128,224},{160,192},{192,160},{224,1... | collective-permute-start | bytes 98312 | tf_op jit(solution)/shard_map/gather_weights/ppermute | solution.py:189
  52.4 7.0 %collective-permute-start.4 = (bf16[64,256]{1,0:T(8,128)(2,1)S(1)}, bf16[64,256]{1,0:T(8,128)(2,1)S(1)}, u32[]{:S(2)}, u32[]{:S(2)}) collective-permute-start(bf16[64,256]{1,0:T(8,128)(2,1)S(1)} %collective-permute-done), channel_id=1, source_target_pairs={{0,128},{32,160},{64,192},{96,224},{128,0},{160,32},{192,64},{224,... | collective-permute-start | bytes 98312 | tf_op jit(solution)/shard_map/gather_weights/ppermute | solution.py:189
  56.1 5.1 %collective-permute-start.5 = (bf16[64,256]{1,0:T(8,128)(2,1)S(1)}, bf16[64,256]{1,0:T(8,128)(2,1)S(1)}, u32[]{:S(2)}, u32[]{:S(2)}) collective-permute-start(bf16[64,256]{1,0:T(8,128)(2,1)S(1)} %collective-permute-done), channel_id=1, source_target_pairs={{0,160},{32,128},{64,224},{96,192},{128,32},{160,0},{192,96},{224,... | collective-permute-start | bytes 98312 | tf_op jit(solution)/shard_map/gather_weights/ppermute | solution.py:189
  56.1 5.1 %collective-permute-start.6 = (bf16[64,256]{1,0:T(8,128)(2,1)S(1)}, bf16[64,256]{1,0:T(8,128)(2,1)S(1)}, u32[]{:S(2)}, u32[]{:S(2)}) collective-permute-start(bf16[64,256]{1,0:T(8,128)(2,1)S(1)} %collective-permute-done), channel_id=1, source_target_pairs={{0,192},{32,224},{64,128},{96,160},{128,64},{160,96},{192,0},{224,... | collective-permute-start | bytes 98312 | tf_op jit(solution)/shard_map/gather_weights/ppermute | solution.py:189
  58.2 4.8 %collective-permute-start.7 = (bf16[64,256]{1,0:T(8,128)(2,1)S(1)}, bf16[64,256]{1,0:T(8,128)(2,1)S(1)}, u32[]{:S(2)}, u32[]{:S(2)}) collective-permute-start(bf16[64,256]{1,0:T(8,128)(2,1)S(1)} %collective-permute-done), channel_id=1, source_target_pairs={{0,224},{32,192},{64,160},{96,128},{128,96},{160,64},{192,32},{224... | collective-permute-start | bytes 98312 | tf_op jit(solution)/shard_map/gather_weights/ppermute | solution.py:189
  63.1 11.6 %collective-permute-start.8 = (bf16[8,64,256]{2,1,0:T(8,128)(2,1)S(1)}, bf16[8,64,256]{2,1,0:T(8,128)(2,1)S(1)}, u32[]{:S(2)}, u32[]{:S(2)}) collective-permute-start(bf16[8,64,256]{2,1,0:T(8,128)(2,1)S(1)} %bitcast_dynamic-update-slice_fusion), channel_id=1, source_target_pairs={{0,1},{1,0},{2,3},{3,2},{4,5},{5,4},{6,7},{7,6},{8,9},{9,8},{10,11... | collective-permute-start | bytes 786440 | tf_op jit(solution)/shard_map/gather_weights/ppermute | solution.py:194
  64.6 18.0 %collective-permute-start.9 = (bf16[8,64,256]{2,1,0:T(8,128)(2,1)S(1)}, bf16[8,64,256]{2,1,0:T(8,128)(2,1)S(1)}, u32[]{:S(2)}, u32[]{:S(2)}) collective-permute-start(bf16[8,64,256]{2,1,0:T(8,128)(2,1)S(1)} %bitcast_dynamic-update-slice_fusion), channel_id=1, source_target_pairs={{0,2},{1,3},{2,0},{3,1},{4,6},{5,7},{6,4},{7,5},{8,10},{9,11},{10,... | collective-permute-start | bytes 786440 | tf_op jit(solution)/shard_map/gather_weights/ppermute | solution.py:194
  67.0 16.7 %collective-permute-start.10 = (bf16[8,64,256]{2,1,0:T(8,128)(2,1)S(1)}, bf16[8,64,256]{2,1,0:T(8,128)(2,1)S(1)}, u32[]{:S(2)}, u32[]{:S(2)}) collective-permute-start(bf16[8,64,256]{2,1,0:T(8,128)(2,1)S(1)} %bitcast_dynamic-update-slice_fusion), channel_id=1, source_target_pairs={{0,3},{1,2},{2,1},{3,0},{4,7},{5,6},{6,5},{7,4},{8,11},{9,10},{10,... | collective-permute-start | bytes 786440 | tf_op jit(solution)/shard_map/gather_weights/ppermute | solution.py:194
  83.8 1.1 copy-start.2
  87.9 3.0 %collective-permute-start.11 = (bf16[1024,256]{1,0:T(8,128)(2,1)S(1)}, bf16[1024,256]{1,0:T(8,128)(2,1)S(1)}, u32[]{:S(2)}, u32[]{:S(2)}) collective-permute-start(bf16[1024,256]{1,0:T(8,128)(2,1)S(1)} %slice_bitcast_fusion), channel_id=1, source_target_pairs={{0,32},{32,0},{64,96},{96,64},{128,160},{160,128},{192,224},{224,1... | collective-permute-start | bytes 1572872 | tf_op jit(solution)/shard_map/reduce_grads/ppermute | solution.py:208
  89.3 1.5 %collective-permute-start.12 = (f32[1,256]{1,0:T(1,128)S(1)}, f32[1,256]{1,0:T(1,128)S(1)}, u32[]{:S(2)}, u32[]{:S(2)}) collective-permute-start(f32[1,256]{1,0:T(1,128)S(1)} %get-tuple-element.13), channel_id=1, source_target_pairs={{0,32},{32,0},{64,96},{96,64},{128,160},{160,128},{192,224},{224,1... | collective-permute-start | bytes 3080 | tf_op jit(solution)/shard_map/reduce_grads/ppermute | solution.py:210
  115.2 4.6 %collective-permute-start.13 = (f32[40,256]{1,0:T(8,128)S(1)}, f32[40,256]{1,0:T(8,128)S(1)}, u32[]{:S(2)}, u32[]{:S(2)}) collective-permute-start(f32[40,256]{1,0:T(8,128)S(1)} %convert_reduce_fusion), channel_id=1, source_target_pairs={{0,64},{32,96},{64,0},{96,32},{128,192},{160,224},{192,128},{224,1... | collective-permute-start | bytes 122888 | tf_op jit(solution)/shard_map/reduce_grads/ppermute | solution.py:219
  117.1 4.5 %collective-permute-start.14 = (f32[40,256]{1,0:T(8,128)S(1)}, f32[40,256]{1,0:T(8,128)S(1)}, u32[]{:S(2)}, u32[]{:S(2)}) collective-permute-start(f32[40,256]{1,0:T(8,128)S(1)} %convert_reduce_fusion), channel_id=1, source_target_pairs={{0,128},{32,160},{64,192},{96,224},{128,0},{160,32},{192,64},{224,... | collective-permute-start | bytes 122888 | tf_op jit(solution)/shard_map/reduce_grads/ppermute | solution.py:219
  119.8 4.1 %collective-permute-start.15 = (f32[40,256]{1,0:T(8,128)S(1)}, f32[40,256]{1,0:T(8,128)S(1)}, u32[]{:S(2)}, u32[]{:S(2)}) collective-permute-start(f32[40,256]{1,0:T(8,128)S(1)} %convert_reduce_fusion), channel_id=1, source_target_pairs={{0,192},{32,224},{64,128},{96,160},{128,64},{160,96},{192,0},{224,... | collective-permute-start | bytes 122888 | tf_op jit(solution)/shard_map/reduce_grads/ppermute | solution.py:219
  123.9 5.1 %collective-permute-start.16 = (f32[32,256]{1,0:T(8,128)S(1)}, f32[32,256]{1,0:T(8,128)S(1)}, u32[]{:S(2)}, u32[]{:S(2)}) collective-permute-start(f32[32,256]{1,0:T(8,128)S(1)} %slice.22), channel_id=1, source_target_pairs={{0,32},{32,0},{64,96},{96,64},{128,160},{160,128},{192,224},{224,1... | collective-permute-start | bytes 98312 | tf_op jit(solution)/shard_map/reduce_grads/ppermute | solution.py:222

commit v2 on v1

v2 whole, which is shorter than its diff:
```python
import jax
import jax.numpy as jnp
from jax import lax
from jax.experimental import pallas as pl
from jax.experimental.pallas import tpu as pltpu
from jax.sharding import PartitionSpec as P

TILE = 128
SLOTS_STEP = 128
UNROLL = 32
GELU_A = 0.7978845608
GELU_B = 0.044715
BF16 = jnp.bfloat16
F32 = jnp.float32


def aggregate(dsts, srcs, count, feats, weights, nfeat):
    fcols, nsrc = feats.shape
    slots = weights.shape[0]
    dtiles = nsrc // TILE // 2
    per_owner = dtiles // nfeat
    steps = slots // SLOTS_STEP

    def kernel(dst, src, cnt, x_ref, w_ref, o_ref, acc, out, sem):
        i = pl.program_id(0)

        @pl.when(i == 0)
        def _():
            acc[...] = jnp.zeros_like(acc)

        base = i * SLOTS_STEP
        live = jnp.clip(cnt[0] - base, 0, SLOTS_STEP)
        zero = jnp.zeros((fcols, TILE), BF16)

        def source(slot):
            return x_ref[:, pl.ds(pl.multiple_of(src[slot] * TILE, TILE), TILE)]

        def group(g, carry):
            first = g * UNROLL
            products = []
            for u in range(0, UNROLL, 2):
                slot = base + first + u
                left = jnp.concatenate(
                    [
                        jnp.concatenate([source(slot), zero], 1),
                        jnp.concatenate([zero, source(slot + 1)], 1),
                    ],
                    0,
                )
                right = jnp.concatenate([w_ref[first + u], w_ref[first + u + 1]], 1)
                both = lax.dot_general(
                    left, right, (((1,), (1,)), ((), ())), preferred_element_type=F32
                )
                products += [both[:fcols], both[fcols:]]
            for u in range(UNROLL):
                slot = base + first + u
                acc[dst[slot]] += jnp.where(slot < cnt[0], products[u], 0.0)
            return carry

        lax.fori_loop(0, pl.cdiv(live, UNROLL), group, 0)

        @pl.when(i == steps - 1)
        def _():
            part = nfeat // 4
            copies = []
            for p in range(4):
                tiles = acc[p * part * per_owner : (p + 1) * part * per_owner]
                out[p * part : (p + 1) * part] = tiles.reshape(part, per_owner * fcols, TILE).astype(BF16)
                copies.append(
                    pltpu.make_async_copy(
                        out.at[pl.ds(p * part, part)], o_ref.at[pl.ds(p * part, part)], sem.at[p]
                    )
                )
                copies[-1].start()
            for c in copies:
                c.wait()

    return pl.pallas_call(
        kernel,
        grid_spec=pltpu.PrefetchScalarGridSpec(
            num_scalar_prefetch=3,
            grid=(steps,),
            in_specs=[
                pl.BlockSpec((fcols, nsrc), lambda i, *_: (0, 0)),
                pl.BlockSpec((SLOTS_STEP, TILE, TILE), lambda i, *_: (i, 0, 0)),
            ],
            out_specs=pl.BlockSpec(memory_space=pltpu.HBM),
            scratch_shapes=[
                pltpu.VMEM((dtiles, fcols, TILE), F32),
                pltpu.VMEM((nfeat, per_owner * fcols, TILE), BF16),
                pltpu.SemaphoreType.DMA((4,)),
            ],
        ),
        out_shape=jax.ShapeDtypeStruct((nfeat, per_owner * fcols, TILE), BF16),
        name="aggregate",
        compiler_params=pltpu.CompilerParams(vmem_limit_bytes=40 << 20),
        cost_estimate=pl.CostEstimate(
            flops=2 * slots * fcols * TILE * TILE,
            bytes_accessed=slots * TILE * TILE * 2 + fcols * nsrc * 2,
            transcendentals=0,
        ),
    )(dsts, srcs, count, feats, weights)


def contract_rows(a, b):
    return lax.dot_general(a, b, (((0,), (0,)), ((), ())), preferred_element_type=F32)


def in_vmem(n):
    return [pl.BlockSpec(memory_space=pltpu.VMEM)] * n


def pack(place, feats, w_self, w_neigh, nfeat, rows_dev):
    fcols = feats.shape[0]
    hid = w_self.shape[1]
    per_owner = rows_dev // TILE
    share = fcols // 2

    def kernel(at, x_ref, ws_ref, wn_ref, o_ref, both):
        both[:, :hid] = ws_ref[...]
        both[:, hid:] = wn_ref[...]
        core, x = lax.rem(at[0], 2), lax.div(at[0], 2)
        piece = both[pl.ds(pl.multiple_of(core * share, share), share), pl.ds(pl.multiple_of(x * TILE, TILE), TILE)]
        for c in range(nfeat):
            for q in range(per_owner):
                tile = c * per_owner + q
                o_ref[c, q * fcols : (q + 1) * fcols, :] = x_ref[:, tile * TILE : (tile + 1) * TILE]
            o_ref[c, per_owner * fcols :, :] = piece

    return pl.pallas_call(
        kernel,
        grid=(1,),
        in_specs=[
            pl.BlockSpec(memory_space=pltpu.SMEM),
            pl.BlockSpec((fcols, nfeat * rows_dev), lambda i: (0, 0)),
            pl.BlockSpec((fcols, hid), lambda i: (0, 0)),
            pl.BlockSpec((fcols, hid), lambda i: (0, 0)),
        ],
        out_specs=pl.BlockSpec((nfeat, per_owner * fcols + share, TILE), lambda i: (0, 0, 0)),
        out_shape=jax.ShapeDtypeStruct((nfeat, per_owner * fcols + share, TILE), BF16),
        scratch_shapes=[pltpu.VMEM((fcols, 2 * hid), BF16)],
        name="pack",
        compiler_params=pltpu.CompilerParams(vmem_limit_bytes=16 << 20),
        cost_estimate=pl.CostEstimate(flops=0, bytes_accessed=3 << 20, transcendentals=0),
    )(place, feats, w_self, w_neigh)


def contract_rows(a, b):
    return lax.dot_general(a, b, (((0,), (0,)), ((), ())), preferred_element_type=F32)


def row_tile(ref, q, fcols):
    return ref[:, q * fcols : (q + 1) * fcols, :].reshape(ref.shape[0] * fcols, TILE)


def own_part(place, same_core, other_core, x_rows, bias, tiles):
    nx, nfeat, share, _ = same_core.shape
    hid = bias.shape[1]
    fcols = 2 * share

    def kernel(at, w0, w1, x_ref, b_ref, pre_ref, wn_ref, both):
        for k in range(nx):
            x = lax.bitwise_xor(lax.div(at[0], 2), k)
            lanes = pl.ds(pl.multiple_of(x * TILE, TILE), TILE)
            for r, ref in enumerate((w0, w1)):
                core = lax.bitwise_xor(lax.rem(at[0], 2), r)
                both[:, pl.ds(pl.multiple_of(core * share, share), share), lanes] = ref[k]
        ws = both[:, :, :hid].reshape(nfeat * fcols, hid)
        wn_ref[...] = both[:, :, hid:].reshape(nfeat * fcols, hid)
        for q in range(tiles):
            pre_ref[q] = contract_rows(row_tile(x_ref, q, fcols), ws) + b_ref[...]

    return pl.pallas_call(
        kernel,
        in_specs=[pl.BlockSpec(memory_space=pltpu.SMEM)] + in_vmem(4),
        out_specs=in_vmem(2),
        out_shape=[
            jax.ShapeDtypeStruct((tiles, TILE, hid), F32),
            jax.ShapeDtypeStruct((nfeat * fcols, hid), BF16),
        ],
        scratch_shapes=[pltpu.VMEM((nfeat, fcols, 2 * hid), BF16)],
        name="own_part",
        compiler_params=pltpu.CompilerParams(vmem_limit_bytes=16 << 20),
        cost_estimate=pl.CostEstimate(
            flops=2 * nfeat * fcols * tiles * TILE * hid, bytes_accessed=4 << 20, transcendentals=0
        ),
    )(place, same_core, other_core, x_rows, bias)


def layer(place, pre_own, a_rows, w_neigh, x_rows, upstream):
    nfeat = x_rows.shape[0]
    feats, hid = w_neigh.shape
    fcols = feats // nfeat
    rows = upstream.shape[0]
    tiles = rows // TILE
    halves = hid // TILE
    out_rows = halves * fcols + 8

    def kernel(at, pre_hbm, a_ref, wn_hbm, x_ref, up_ref, hid_ref, g_ref, pre, wn, deltas, sem):
        get_wn = pltpu.make_async_copy(wn_hbm, wn, sem.at[0])
        get_pre = pltpu.make_async_copy(pre_hbm, pre, sem.at[1])
        get_wn.start()
        get_pre.start()
        get_wn.wait()
        get_pre.wait()
        gb = jnp.zeros((1, hid), F32)
        for q in range(tiles):
            here = slice(q * TILE, (q + 1) * TILE)
            v = pre[q] + contract_rows(row_tile(a_ref, q, fcols), wn[...])
            sq = v * v
            t = jnp.tanh(GELU_A * (v + GELU_B * sq * v))
            half = 0.5 * (1.0 + t)
            hid_ref[here, :] = (v * half).astype(BF16)
            slope = half + 0.5 * v * (1.0 - t * t) * (GELU_A * (1.0 + 3.0 * GELU_B * sq))
            delta = (up_ref[here, :].astype(F32) * slope).astype(BF16)
            deltas[here, :] = delta
            gb = gb + jnp.sum(delta.astype(F32), axis=0, keepdims=True)
        core = lax.rem(at[0], 2)
        for slot, ref in ((core, x_ref), (1 - core, a_ref)):
            left = jnp.concatenate([row_tile(ref, q, fcols) for q in range(tiles)], axis=1)
            grad = jnp.dot(left, deltas[...], preferred_element_type=F32).astype(BF16)
            for h in range(halves):
                g_ref[slot, :, h * fcols : (h + 1) * fcols, :] = grad[:, h * TILE : (h + 1) * TILE].reshape(
                    nfeat, fcols, TILE
                )
        high = gb.astype(BF16).astype(F32)
        mid = (gb - high).astype(BF16).astype(F32)
        low = gb - high - mid
        lines = [part[:, h * TILE : (h + 1) * TILE] for part in (high, mid, low) for h in range(halves)]
        lines = jnp.concatenate(lines + [jnp.zeros((8 - len(lines), TILE), F32)], axis=0).astype(BF16)
        g_ref[0, :, halves * fcols :, :] = jnp.broadcast_to(lines[None], (nfeat, 8, TILE))
        g_ref[1, :, halves * fcols :, :] = jnp.zeros((nfeat, 8, TILE), BF16)

    return pl.pallas_call(
        kernel,
        in_specs=[
            pl.BlockSpec(memory_space=pltpu.SMEM),
            pl.BlockSpec(memory_space=pl.ANY),
            *in_vmem(1),
            pl.BlockSpec(memory_space=pl.ANY),
            *in_vmem(2),
        ],
        out_specs=in_vmem(2),
        out_shape=[
            jax.ShapeDtypeStruct((rows, hid), BF16),
            jax.ShapeDtypeStruct((2, nfeat, out_rows, TILE), BF16),
        ],
        scratch_shapes=[
            pltpu.VMEM((tiles, TILE, hid), F32),
            pltpu.VMEM((feats, hid), BF16),
            pltpu.VMEM((rows, hid), BF16),
            pltpu.SemaphoreType.DMA((2,)),
        ],
        name="layer",
        compiler_params=pltpu.CompilerParams(vmem_limit_bytes=24 << 20),
        cost_estimate=pl.CostEstimate(
            flops=6 * feats * rows * hid, bytes_accessed=6 << 20, transcendentals=rows * hid
        ),
    )(place, pre_own, a_rows, w_neigh, x_rows, upstream)


def finish(place, terms, fcols, hid):
    halves = hid // TILE

    def kernel(at, *refs):
        ins, (gs_ref, gn_ref, gb_ref) = refs[: len(terms)], refs[len(terms) :]
        mine = sum(ref[...] for ref in ins[0::2])
        other = sum(ref[...] for ref in ins[1::2])
        first = lax.rem(at[0], 2) == 0
        both = mine + other
        for h in range(halves):
            lanes, rows = slice(h * TILE, (h + 1) * TILE), slice(h * fcols, (h + 1) * fcols)
            gs_ref[:, lanes] = jnp.where(first, mine[rows], other[rows])
            gn_ref[:, lanes] = jnp.where(first, other[rows], mine[rows])
            at_row = halves * fcols + h
            gb_ref[:, lanes] = sum(both[at_row + halves * p : at_row + halves * p + 1] for p in range(3))

    return pl.pallas_call(
        kernel,
        in_specs=[pl.BlockSpec(memory_space=pltpu.SMEM)] + in_vmem(len(terms)),
        out_specs=in_vmem(3),
        out_shape=[
            jax.ShapeDtypeStruct((fcols, hid), F32),
            jax.ShapeDtypeStruct((fcols, hid), F32),
            jax.ShapeDtypeStruct((1, hid), F32),
        ],
        name="finish",
        compiler_params=pltpu.CompilerParams(vmem_limit_bytes=8 << 20),
    )(place, *terms)


def body(features_t, tile_weights, tile_dst, tile_src, tile_count, w_self, w_neigh, bias, grad_hidden):
    feats = features_t[0]
    fcols = feats.shape[0]
    nv = lax.axis_size("vgroup")
    nfeat = lax.axis_size("feat")
    rows_dev, hid = grad_hidden.shape
    tiles = rows_dev // TILE
    place = lax.axis_index("vgroup")[None].astype(jnp.int32)

    def direct(value, bits):
        return [lax.ppermute(value, "vgroup", [(a, a ^ bit) for a in range(nv)]) for bit in bits]

    with jax.named_scope("send_features"):
        outgoing = pack(place, feats, w_self, w_neigh, nfeat, rows_dev)
        x_rows = lax.all_to_all(outgoing, "feat", 0, 0, tiled=True)

    agg = aggregate(tile_dst[0], tile_src[0], tile_count, feats, tile_weights[0], nfeat)
    x_rows, agg = lax.optimization_barrier((x_rows, agg))
    with jax.named_scope("send_aggregated"):
        a_rows = lax.all_to_all(agg, "feat", 0, 0, tiled=True)

    with jax.named_scope("weights_over_vgroup"):
        piece = x_rows[:, tiles * fcols :, :]
        same_core = jnp.stack([piece] + direct(piece, (2, 4, 6)))
        [other_core] = direct(same_core, (1,))

    pre_own, wn = own_part(place, same_core, other_core, x_rows, bias[None, :], tiles)
    hidden, grads = layer(place, pre_own, a_rows, wn, x_rows, grad_hidden)

    with jax.named_scope("reduce_grads"):
        [got] = direct(grads[1], (1,))
        pair = (grads[0].astype(F32) + got.astype(F32)).astype(BF16)
        arrived = lax.all_to_all(pair, "feat", 0, 0, tiled=True)
        total = jnp.sum(arrived.astype(F32), axis=0)
        terms = [total] + direct(total, range(1, nv))
        grad_self, grad_neigh, grad_bias = finish(place, terms, fcols, hid)
    return (hidden, grad_self, grad_neigh, grad_bias[0])


def solution(mesh):
    return jax.shard_map(
        body,
        mesh=mesh,
        in_specs=(
            P("vgroup", "feat", None),
            P("vgroup", None, None, None),
            P("vgroup", None),
            P("vgroup", None),
            P("vgroup"),
            P("feat", None),
            P("feat", None),
            P(),
            P(("vgroup", "feat"), None),
        ),
        out_specs=(P(("vgroup", "feat"), None), P("feat", None), P("feat", None), P()),
        check_vma=False,
    )
```

time: 130 us -> 122 us (0.938)
  starting transfers between devices: 48.7 us -> 39.2 us
  waiting for transfers between devices: 27.2 us -> 30.1 us
  local copies, waits for them, and re-layouts: 3.58 us -> 5.13 us
  other arithmetic: 1.79 us -> 0.32 us
    all_to_all x2, waiting for transfers between devices: 1.29 us -> 18.5 us  [the longest x1 10.5 us: body(): a_rows = lax.all_to_all(agg, 'feat', 0, 0, tiled=True)]
    ppermute x17 -> x12, waiting for transfers between devices: 25.9 us -> 11.6 us  [direct(): lax.ppermute(value, 'vgroup', [(a, a ^ bit) for a in range(nv)])]
    ppermute x17 -> x12, starting transfers between devices: 30.1 us -> 20.5 us  [direct(): lax.ppermute(value, 'vgroup', [(a, a ^ bit) for a in range(nv)])]
    unnamed x23 -> x20, local copies, waits for them, and re-layouts: 1 us -> 5.04 us
    pallas_call x1 -> x3, Pallas kernels: 2.93 us -> 2.82 us  [the longest x1 1.91 us: layer(): pl.pallas_call(kernel, in_specs=[pl.BlockSpec(memory_space=pltpu.SMEM), p...]
  transfers between devices with their start and end apart: 19 -> 14, of which waited for: 10 -> 9; matrix products, arithmetic and copies ran while one was open for 1% -> 0% of each run, Pallas kernels for 15% -> 16%
where the time goes in v2:
time: 122 us; the launch traced here: 121 us
  starting transfers between devices  39.2 us (32%)
  waiting for transfers between devices  30.1 us (25%)
  blocking collectives  22.7 us (19%)
  Pallas kernels  22.4 us (18%)
  local copies, waits for them, and re-layouts  5.13 us (4%)
  between operations  1.43 us (1%)
    all_to_all x1, blocking collectives, body(): arrived = lax.all_to_all(pair, 'feat', 0, 0, tiled=True)  22.7 us
    ppermute x12, starting transfers between devices, direct(): lax.ppermute(value, 'vgroup', [(a, a ^ bit) for a in range(nv)])  20.5 us
    pallas_call x1, Pallas kernels, aggregate(): pl.pallas_call(kernel, grid_spec=pltpu.PrefetchScalarGridSpec(num_scalar_...  18.9 us
    all_to_all x1, starting transfers between devices, body(): x_rows = lax.all_to_all(outgoing, 'feat', 0, 0, tiled=True)  12.2 us
    ppermute x12, waiting for transfers between devices, direct(): lax.ppermute(value, 'vgroup', [(a, a ^ bit) for a in range(nv)])  11.6 us
    all_to_all x1, waiting for transfers between devices, body(): a_rows = lax.all_to_all(agg, 'feat', 0, 0, tiled=True)  10.5 us
    all_to_all x1, waiting for transfers between devices, body(): x_rows = lax.all_to_all(outgoing, 'feat', 0, 0, tiled=True)  8.07 us
    all_to_all x1, starting transfers between devices, body(): a_rows = lax.all_to_all(agg, 'feat', 0, 0, tiled=True)  6.6 us
  transfers between devices with their start and end apart: 14, of which 9 were waited for; matrix products, arithmetic and copies ran while one was open for 0% of the time, Pallas kernels for 16%

profile of v2, /device:TPU:1, one launch (start us, length us, event | category | flops | bytes accessed | tf_op | source)
XLA Modules:
  0.0 121.4 jit_solution(8820593130887291672)
XLA Ops:
  0.6 1.6 %copy-done = bf16[1,32,32768]{2,1,0:T(8,128)(2,1)S(1)} copy-done((bf16[1,32,32768]{2,1,0:T(8,128)(2,1)S(1)}, bf16[1,32,32768]{2,1,0:T(8,128)(2,1)}, u32[]{:S(2)}) %copy-start) | copy-done | bytes 2097176
  2.2 0.7 copy-done.5
  3.0 0.7 copy-done.6
  3.9 1.0 copy-done.2
  5.0 12.2 %all-to-all-start = ((bf16[32,144,128]{2,1,0:T(8,128)(2,1)}), bf16[32,144,128]{2,1,0:T(8,128)(2,1)S(1)}, u32[]{:S(2)}, u32[]{:S(2)}) async-start(bf16[32,144,128]{2,1,0:T(8,128)(2,1)} %copy-done.2), calls=%async_computation | async-start | bytes 2359296 | tf_op jit(solution)/shard_map/send_features/all_to_all | solution.py:306
  17.8 18.9 %aggregate.1 = bf16[32,128,128]{2,1,0:T(8,128)(2,1)S(1)} custom-call(s32[1024]{0:T(1024)S(1)} %bitcast.19, s32[1024]{0:T(1024)S(1)} %bitcast.20, s32[1]{0:T(128)S(6)} %copy.13.cnt, bf16[32,32768]{1,0:T(8,128)(2,1)S(1)} %bitcast.18, bf16[1024,128,128]{2,1,0:T(8,128)(2,1)} %bitcast.22), custom_call_target="tpu_custom_call" | custom-call | flops 1073741824 | bytes 35651584 | tf_op jit(solution)/shard_map/aggregate/pallas_call | solution.py:78
  36.8 1.0 copy-done.3
  37.7 8.1 %all-to-all-done.x_ref = bf16[32,144,128]{2,1,0:T(8,128)(2,1)S(1)} async-done(((bf16[32,144,128]{2,1,0:T(8,128)(2,1)}), bf16[32,144,128]{2,1,0:T(8,128)(2,1)S(1)}, u32[]{:S(2)}, u32[]{:S(2)}) %all-to-all-start) | async-done | bytes 1179680 | tf_op jit(solution)/shard_map/send_features/all_to_all | solution.py:306
  45.8 6.6 %all-to-all-start.1 = ((bf16[32,128,128]{2,1,0:T(8,128)(2,1)}), bf16[32,128,128]{2,1,0:T(8,128)(2,1)S(1)}, u32[]{:S(2)}, u32[]{:S(2)}) async-start(bf16[32,128,128]{2,1,0:T(8,128)(2,1)} %copy-done.3), calls=%async_computation.1 | async-start | bytes 2097152 | tf_op jit(solution)/shard_map/send_aggregated/all_to_all | solution.py:311
  52.5 2.8 %collective-permute-start.1 = (bf16[32,16,128]{2,1,0:T(8,128)(2,1)S(1)}, bf16[32,16,128]{2,1,0:T(8,128)(2,1)S(1)}, u32[]{:S(2)}, u32[]{:S(2)}) collective-permute-start(bf16[32,16,128]{2,1,0:T(8,128)(2,1)S(1)} %get-tuple-element.23), channel_id=1, source_target_pairs={{0,128},{32,160},{64,192},{96,224},{128,0},{160,32},{192,64},{224,... | collective-permute-start | bytes 393224 | tf_op jit(solution)/shard_map/weights_over_vgroup/ppermute | solution.py:302
  55.3 0.3 collective-permute-start
  55.6 0.6 collective-permute-start.2
  56.1 1.7 %collective-permute-done.1 = bf16[32,16,128]{2,1,0:T(8,128)(2,1)S(1)} collective-permute-done((bf16[32,16,128]{2,1,0:T(8,128)(2,1)S(1)}, bf16[32,16,128]{2,1,0:T(8,128)(2,1)S(1)}, u32[]{:S(2)}, u32[]{:S(2)}) %collective-permute-start.1) | collective-permute-done | bytes 131104 | tf_op jit(solution)/shard_map/weights_over_vgroup/ppermute | solution.py:302
  57.9 1.9 %collective-permute-done = bf16[32,16,128]{2,1,0:T(8,128)(2,1)S(1)} collective-permute-done((bf16[32,16,128]{2,1,0:T(8,128)(2,1)S(1)}, bf16[32,16,128]{2,1,0:T(8,128)(2,1)S(1)}, u32[]{:S(2)}, u32[]{:S(2)}) %collective-permute-start) | collective-permute-done | bytes 131104 | tf_op jit(solution)/shard_map/weights_over_vgroup/ppermute | solution.py:302
  59.8 2.5 %collective-permute-done.2 = bf16[32,16,128]{2,1,0:T(8,128)(2,1)S(1)} collective-permute-done((bf16[32,16,128]{2,1,0:T(8,128)(2,1)S(1)}, bf16[32,16,128]{2,1,0:T(8,128)(2,1)S(1)}, u32[]{:S(2)}, u32[]{:S(2)}) %collective-permute-start.2) | collective-permute-done | bytes 131104 | tf_op jit(solution)/shard_map/weights_over_vgroup/ppermute | solution.py:302
  62.3 2.3 %collective-permute-start.3 = (bf16[4,32,16,128]{3,2,1,0:T(8,128)(2,1)S(1)}, bf16[4,32,16,128]{3,2,1,0:T(8,128)(2,1)S(1)}, u32[]{:S(2)}, u32[]{:S(2)}) collective-permute-start(bf16[4,32,16,128]{3,2,1,0:T(8,128)(2,1)S(1)} %pad_maximum_fusion.w0), channel_id=1, source_target_pairs={{0,32},{32,0},{64,96},{96,64},{128,160},{160,128},{192,224},{224,1... | collective-permute-start | bytes 1572872 | tf_op jit(solution)/shard_map/weights_over_vgroup/ppermute | solution.py:302
  64.7 1.5 %collective-permute-done.3.w1 = bf16[4,32,16,128]{3,2,1,0:T(8,128)(2,1)S(1)} collective-permute-done((bf16[4,32,16,128]{3,2,1,0:T(8,128)(2,1)S(1)}, bf16[4,32,16,128]{3,2,1,0:T(8,128)(2,1)S(1)}, u32[]{:S(2)}, u32[]{:S(2)}) %collective-permute-start.3) | collective-permute-done | bytes 524320 | tf_op jit(solution)/shard_map/weights_over_vgroup/ppermute | solution.py:302
  66.2 0.7 own_part.1
  66.9 10.5 %all-to-all-done.1.a_ref = bf16[32,128,128]{2,1,0:T(8,128)(2,1)S(1)} async-done(((bf16[32,128,128]{2,1,0:T(8,128)(2,1)}), bf16[32,128,128]{2,1,0:T(8,128)(2,1)S(1)}, u32[]{:S(2)}, u32[]{:S(2)}) %all-to-all-start.1) | async-done | bytes 1048608 | tf_op jit(solution)/shard_map/send_aggregated/all_to_all | solution.py:311
  77.4 1.9 %layer.1 = (bf16[512,256]{1,0:T(8,128)(2,1)}, bf16[2,32,72,128]{3,2,1,0:T(8,128)(2,1)S(1)}) custom-call(s32[1]{0:T(128)} %bitcast.at, f32[4,128,256]{2,1,0:T(8,128)S(1)} %get-tuple-element.14.pre_hbm, bf16[32,128,128]{2,1,0:T(8,128)(2,1)S(1)} %all-to-all-done.1.a_ref, bf16[1024,256]{1,0:T(8,128)(2,1)S(1)} %get-tuple-element.16.wn_hbm, ...), custom_call_target="tpu_custom_call" | custom-call | flops 805306368 | bytes 6291456 | tf_op jit(solution)/shard_map/layer/pallas_call | solution.py:234
  79.3 4.1 %collective-permute-start.4 = (bf16[32,72,128]{2,1,0:T(8,128)(2,1)S(1)}, bf16[32,72,128]{2,1,0:T(8,128)(2,1)S(1)}, u32[]{:S(2)}, u32[]{:S(2)}) collective-permute-start(bf16[32,72,128]{2,1,0:T(8,128)(2,1)S(1)} %slice_bitcast_fusion), channel_id=1, source_target_pairs={{0,32},{32,0},{64,96},{96,64},{128,160},{160,128},{192,224},{224,1... | collective-permute-start | bytes 1769480 | tf_op jit(solution)/shard_map/reduce_grads/ppermute | solution.py:302
  83.5 1.6 %collective-permute-done.4 = bf16[32,72,128]{2,1,0:T(8,128)(2,1)S(1)} collective-permute-done((bf16[32,72,128]{2,1,0:T(8,128)(2,1)S(1)}, bf16[32,72,128]{2,1,0:T(8,128)(2,1)S(1)}, u32[]{:S(2)}, u32[]{:S(2)}) %collective-permute-start.4) | collective-permute-done | bytes 589856 | tf_op jit(solution)/shard_map/reduce_grads/ppermute | solution.py:302
  85.3 22.7 %all_to_all.15 = bf16[32,72,128]{2,1,0:T(8,128)(2,1)S(1)} all-to-all(bf16[32,72,128]{2,1,0:T(8,128)(2,1)S(1)} %fusion), channel_id=1, replica_groups=mesh['vgroup'=8,'feat'=32] {'feat'}, dimensions={0} | all-to-all | bytes 1179648 | tf_op jit(solution)/shard_map/reduce_grads/all_to_all | solution.py:324
  108.1 4.8 %collective-permute-start.11 = (f32[72,128]{1,0:T(8,128)S(1)}, f32[72,128]{1,0:T(8,128)S(1)}, u32[]{:S(2)}, u32[]{:S(2)}) collective-permute-start(f32[72,128]{1,0:T(8,128)S(1)} %convert_reduce_fusion.refs_0_), channel_id=1, source_target_pairs={{0,224},{32,192},{64,160},{96,128},{128,96},{160,64},{192,32},{224... | collective-permute-start | bytes 110600 | tf_op jit(solution)/shard_map/reduce_grads/ppermute | solution.py:302
  113.1 0.7 collective-permute-start.9
  113.8 2.4 %collective-permute-start.8 = (f32[72,128]{1,0:T(8,128)S(1)}, f32[72,128]{1,0:T(8,128)S(1)}, u32[]{:S(2)}, u32[]{:S(2)}) collective-permute-start(f32[72,128]{1,0:T(8,128)S(1)} %convert_reduce_fusion.refs_0_), channel_id=1, source_target_pairs={{0,128},{32,160},{64,192},{96,224},{128,0},{160,32},{192,64},{224,... | collective-permute-start | bytes 110600 | tf_op jit(solution)/shard_map/reduce_grads/ppermute | solution.py:302
  116.2 0.4 collective-permute-start.7
  116.6 1.5 %collective-permute-start.6 = (f32[72,128]{1,0:T(8,128)S(1)}, f32[72,128]{1,0:T(8,128)S(1)}, u32[]{:S(2)}, u32[]{:S(2)}) collective-permute-start(f32[72,128]{1,0:T(8,128)S(1)} %convert_reduce_fusion.refs_0_), channel_id=1, source_target_pairs={{0,64},{32,96},{64,0},{96,32},{128,192},{160,224},{192,128},{224,1... | collective-permute-start | bytes 110600 | tf_op jit(solution)/shard_map/reduce_grads/ppermute | solution.py:302
  118.1 0.3 collective-permute-start.5
  118.4 1.7 %collective-permute-done.7.refs_3_ = f32[72,128]{1,0:T(8,128)S(1)} collective-permute-done((f32[72,128]{1,0:T(8,128)S(1)}, f32[72,128]{1,0:T(8,128)S(1)}, u32[]{:S(2)}, u32[]{:S(2)}) %collective-permute-start.7) | collective-permute-done | bytes 36896 | tf_op jit(solution)/shard_map/reduce_grads/ppermute | solution.py:302
  120.1 0.6 collective-permute-done.6.refs_2_
  120.7 0.6 finish.1
  (27 shorter events, 0.9 us)
Async XLA Ops:
  0.6 1.6 %copy-start = (bf16[1,32,32768]{2,1,0:T(8,128)(2,1)S(1)}, bf16[1,32,32768]{2,1,0:T(8,128)(2,1)}, u32[]{:S(2)}) copy-start(bf16[1,32,32768]{2,1,0:T(8,128)(2,1)} %param.9) | copy-start | bytes 6291460
  2.2 0.7 copy-start.5
  2.9 0.7 copy-start.6
  3.9 1.0 copy-start.2
  5.0 12.8 %copy-start.1 = (bf16[1,32,32768]{2,1,0:T(8,128)(2,1)S(1)}, bf16[1,32,32768]{2,1,0:T(8,128)(2,1)}, u32[]{:S(2)}) copy-start(bf16[1,32,32768]{2,1,0:T(8,128)(2,1)} %param.9) | copy-start | bytes 6291460
  5.0 12.8 %copy-start.7 = (s32[1,1024]{1,0:T(1,128)S(1)}, s32[1,1024]{1,0:T(1,128)}, u32[]{:S(2)}) copy-start(s32[1,1024]{1,0:T(1,128)} %param.11) | copy-start | bytes 12292
  5.0 12.8 %copy-start.8 = (s32[1,1024]{1,0:T(1,128)S(1)}, s32[1,1024]{1,0:T(1,128)}, u32[]{:S(2)}) copy-start(s32[1,1024]{1,0:T(1,128)} %param.12) | copy-start | bytes 12292
  5.0 40.8 %all-to-all-start = ((bf16[32,144,128]{2,1,0:T(8,128)(2,1)}), bf16[32,144,128]{2,1,0:T(8,128)(2,1)S(1)}, u32[]{:S(2)}, u32[]{:S(2)}) async-start(bf16[32,144,128]{2,1,0:T(8,128)(2,1)} %copy-done.2), calls=%async_computation | async-start | bytes 2359296 | tf_op jit(solution)/shard_map/send_features/all_to_all | solution.py:306
  36.8 1.0 copy-start.3
  45.8 31.6 %all-to-all-start.1 = ((bf16[32,128,128]{2,1,0:T(8,128)(2,1)}), bf16[32,128,128]{2,1,0:T(8,128)(2,1)S(1)}, u32[]{:S(2)}, u32[]{:S(2)}) async-start(bf16[32,128,128]{2,1,0:T(8,128)(2,1)} %copy-done.3), calls=%async_computation.1 | async-start | bytes 2097152 | tf_op jit(solution)/shard_map/send_aggregated/all_to_all | solution.py:311
  52.4 13.8 %copy-start.9 = (f32[256]{0:T(256)S(1)}, f32[256]{0:T(256)}, u32[]{:S(2)}) copy-start(f32[256]{0:T(256)} %param.16) | copy-start | bytes 3076
  52.5 5.4 %collective-permute-start.1 = (bf16[32,16,128]{2,1,0:T(8,128)(2,1)S(1)}, bf16[32,16,128]{2,1,0:T(8,128)(2,1)S(1)}, u32[]{:S(2)}, u32[]{:S(2)}) collective-permute-start(bf16[32,16,128]{2,1,0:T(8,128)(2,1)S(1)} %get-tuple-element.23), channel_id=1, source_target_pairs={{0,128},{32,160},{64,192},{96,224},{128,0},{160,32},{192,64},{224,... | collective-permute-start | bytes 393224 | tf_op jit(solution)/shard_map/weights_over_vgroup/ppermute | solution.py:302
  55.3 4.5 %collective-permute-start = (bf16[32,16,128]{2,1,0:T(8,128)(2,1)S(1)}, bf16[32,16,128]{2,1,0:T(8,128)(2,1)S(1)}, u32[]{:S(2)}, u32[]{:S(2)}) collective-permute-start(bf16[32,16,128]{2,1,0:T(8,128)(2,1)S(1)} %get-tuple-element.23), channel_id=1, source_target_pairs={{0,64},{32,96},{64,0},{96,32},{128,192},{160,224},{192,128},{224,1... | collective-permute-start | bytes 393224 | tf_op jit(solution)/shard_map/weights_over_vgroup/ppermute | solution.py:302
  55.6 6.6 %collective-permute-start.2 = (bf16[32,16,128]{2,1,0:T(8,128)(2,1)S(1)}, bf16[32,16,128]{2,1,0:T(8,128)(2,1)S(1)}, u32[]{:S(2)}, u32[]{:S(2)}) collective-permute-start(bf16[32,16,128]{2,1,0:T(8,128)(2,1)S(1)} %get-tuple-element.23), channel_id=1, source_target_pairs={{0,192},{32,224},{64,128},{96,160},{128,64},{160,96},{192,0},{224,... | collective-permute-start | bytes 393224 | tf_op jit(solution)/shard_map/weights_over_vgroup/ppermute | solution.py:302
  62.3 15.1 %copy-start.4 = (bf16[512,256]{1,0:T(8,128)(2,1)S(1)}, bf16[512,256]{1,0:T(8,128)(2,1)}, u32[]{:S(2)}) copy-start(bf16[512,256]{1,0:T(8,128)(2,1)} %up_ref.1) | copy-start | bytes 786436
  62.3 3.9 %collective-permute-start.3 = (bf16[4,32,16,128]{3,2,1,0:T(8,128)(2,1)S(1)}, bf16[4,32,16,128]{3,2,1,0:T(8,128)(2,1)S(1)}, u32[]{:S(2)}, u32[]{:S(2)}) collective-permute-start(bf16[4,32,16,128]{3,2,1,0:T(8,128)(2,1)S(1)} %pad_maximum_fusion.w0), channel_id=1, source_target_pairs={{0,32},{32,0},{64,96},{96,64},{128,160},{160,128},{192,224},{224,1... | collective-permute-start | bytes 1572872 | tf_op jit(solution)/shard_map/weights_over_vgroup/ppermute | solution.py:302
  79.3 5.7 %collective-permute-start.4 = (bf16[32,72,128]{2,1,0:T(8,128)(2,1)S(1)}, bf16[32,72,128]{2,1,0:T(8,128)(2,1)S(1)}, u32[]{:S(2)}, u32[]{:S(2)}) collective-permute-start(bf16[32,72,128]{2,1,0:T(8,128)(2,1)S(1)} %slice_bitcast_fusion), channel_id=1, source_target_pairs={{0,32},{32,0},{64,96},{96,64},{128,160},{160,128},{192,224},{224,1... | collective-permute-start | bytes 1769480 | tf_op jit(solution)/shard_map/reduce_grads/ppermute | solution.py:302
  108.1 8.5 %collective-permute-start.11 = (f32[72,128]{1,0:T(8,128)S(1)}, f32[72,128]{1,0:T(8,128)S(1)}, u32[]{:S(2)}, u32[]{:S(2)}) collective-permute-start(f32[72,128]{1,0:T(8,128)S(1)} %convert_reduce_fusion.refs_0_), channel_id=1, source_target_pairs={{0,224},{32,192},{64,160},{96,128},{128,96},{160,64},{192,32},{224... | collective-permute-start | bytes 110600 | tf_op jit(solution)/shard_map/reduce_grads/ppermute | solution.py:302
  112.9 5.2 %collective-permute-start.10 = (f32[72,128]{1,0:T(8,128)S(1)}, f32[72,128]{1,0:T(8,128)S(1)}, u32[]{:S(2)}, u32[]{:S(2)}) collective-permute-start(f32[72,128]{1,0:T(8,128)S(1)} %convert_reduce_fusion.refs_0_), channel_id=1, source_target_pairs={{0,192},{32,224},{64,128},{96,160},{128,64},{160,96},{192,0},{224,... | collective-permute-start | bytes 110600 | tf_op jit(solution)/shard_map/reduce_grads/ppermute | solution.py:302
  113.1 5.3 %collective-permute-start.9 = (f32[72,128]{1,0:T(8,128)S(1)}, f32[72,128]{1,0:T(8,128)S(1)}, u32[]{:S(2)}, u32[]{:S(2)}) collective-permute-start(f32[72,128]{1,0:T(8,128)S(1)} %convert_reduce_fusion.refs_0_), channel_id=1, source_target_pairs={{0,160},{32,128},{64,224},{96,192},{128,32},{160,0},{192,96},{224,... | collective-permute-start | bytes 110600 | tf_op jit(solution)/shard_map/reduce_grads/ppermute | solution.py:302
  113.8 4.6 %collective-permute-start.8 = (f32[72,128]{1,0:T(8,128)S(1)}, f32[72,128]{1,0:T(8,128)S(1)}, u32[]{:S(2)}, u32[]{:S(2)}) collective-permute-start(f32[72,128]{1,0:T(8,128)S(1)} %convert_reduce_fusion.refs_0_), channel_id=1, source_target_pairs={{0,128},{32,160},{64,192},{96,224},{128,0},{160,32},{192,64},{224,... | collective-permute-start | bytes 110600 | tf_op jit(solution)/shard_map/reduce_grads/ppermute | solution.py:302
  116.2 3.8 %collective-permute-start.7 = (f32[72,128]{1,0:T(8,128)S(1)}, f32[72,128]{1,0:T(8,128)S(1)}, u32[]{:S(2)}, u32[]{:S(2)}) collective-permute-start(f32[72,128]{1,0:T(8,128)S(1)} %convert_reduce_fusion.refs_0_), channel_id=1, source_target_pairs={{0,96},{32,64},{64,32},{96,0},{128,224},{160,192},{192,160},{224,1... | collective-permute-start | bytes 110600 | tf_op jit(solution)/shard_map/reduce_grads/ppermute | solution.py:302
  116.6 4.1 %collective-permute-start.6 = (f32[72,128]{1,0:T(8,128)S(1)}, f32[72,128]{1,0:T(8,128)S(1)}, u32[]{:S(2)}, u32[]{:S(2)}) collective-permute-start(f32[72,128]{1,0:T(8,128)S(1)} %convert_reduce_fusion.refs_0_), channel_id=1, source_target_pairs={{0,64},{32,96},{64,0},{96,32},{128,192},{160,224},{192,128},{224,1... | collective-permute-start | bytes 110600 | tf_op jit(solution)/shard_map/reduce_grads/ppermute | solution.py:302
  118.1 2.6 %collective-permute-start.5 = (f32[72,128]{1,0:T(8,128)S(1)}, f32[72,128]{1,0:T(8,128)S(1)}, u32[]{:S(2)}, u32[]{:S(2)}) collective-permute-start(f32[72,128]{1,0:T(8,128)S(1)} %convert_reduce_fusion.refs_0_), channel_id=1, source_target_pairs={{0,32},{32,0},{64,96},{96,64},{128,160},{160,128},{192,224},{224,1... | collective-permute-start | bytes 110600 | tf_op jit(solution)/shard_map/reduce_grads/ppermute | solution.py:302

commit v3 on v2

--- a/solution.py
+++ b/solution.py
@@ -116,31 +116,60 @@
     per_owner = rows_dev // TILE
     share = fcols // 2
 
-    def kernel(at, x_ref, ws_ref, wn_ref, o_ref, both):
-        both[:, :hid] = ws_ref[...]
-        both[:, hid:] = wn_ref[...]
+    parts = 4
+    owners = nfeat // parts
+
+    def kernel(at, x_hbm, ws_hbm, wn_hbm, o_hbm, x_ref, o_ref, both, sem_x, sem_o, sem_w):
+        get_w = [
+            pltpu.make_async_copy(ws_hbm, both.at[:, pl.ds(0, hid)], sem_w.at[0]),
+            pltpu.make_async_copy(wn_hbm, both.at[:, pl.ds(hid, hid)], sem_w.at[1]),
+        ]
+        width = owners * rows_dev
+        get_x = [
+            pltpu.make_async_copy(
+                x_hbm.at[:, pl.ds(p * width, width)], x_ref.at[:, pl.ds(p * width, width)], sem_x.at[p]
+            )
+            for p in range(parts)
+        ]
+        put = [
+            pltpu.make_async_copy(
+                o_ref.at[pl.ds(p * owners, owners)], o_hbm.at[pl.ds(p * owners, owners)], sem_o.at[p]
+            )
+            for p in range(parts)
+        ]
+        for c in get_w + get_x:
+            c.start()
+        for c in get_w:
+            c.wait()
         core, x = lax.rem(at[0], 2), lax.div(at[0], 2)
         piece = both[pl.ds(pl.multiple_of(core * share, share), share), pl.ds(pl.multiple_of(x * TILE, TILE), TILE)]
-        for c in range(nfeat):
-            for q in range(per_owner):
-                tile = c * per_owner + q
-                o_ref[c, q * fcols : (q + 1) * fcols, :] = x_ref[:, tile * TILE : (tile + 1) * TILE]
-            o_ref[c, per_owner * fcols :, :] = piece
-
-    return pl.pallas_call(
-        kernel,
-        grid=(1,),
-        in_specs=[
-            pl.BlockSpec(memory_space=pltpu.SMEM),
-            pl.BlockSpec((fcols, nfeat * rows_dev), lambda i: (0, 0)),
-            pl.BlockSpec((fcols, hid), lambda i: (0, 0)),
-            pl.BlockSpec((fcols, hid), lambda i: (0, 0)),
+        for p in range(parts):
+            get_x[p].wait()
+            for c in range(p * owners, (p + 1) * owners):
+                for q in range(per_owner):
+                    tile = c * per_owner + q
+                    o_ref[c, q * fcols : (q + 1) * fcols, :] = x_ref[:, tile * TILE : (tile + 1) * TILE]
+                o_ref[c, per_owner * fcols :, :] = piece
+            put[p].start()
+        for c in put:
+            c.wait()
+
+    out = (nfeat, per_owner * fcols + share, TILE)
+    return pl.pallas_call(
+        kernel,
+        in_specs=[pl.BlockSpec(memory_space=pltpu.SMEM)] + [pl.BlockSpec(memory_space=pl.ANY)] * 3,
+        out_specs=pl.BlockSpec(memory_space=pl.ANY),
+        out_shape=jax.ShapeDtypeStruct(out, BF16),
+        scratch_shapes=[
+            pltpu.VMEM((fcols, nfeat * rows_dev), BF16),
+            pltpu.VMEM(out, BF16),
+            pltpu.VMEM((fcols, 2 * hid), BF16),
+            pltpu.SemaphoreType.DMA((parts,)),
+            pltpu.SemaphoreType.DMA((parts,)),
+            pltpu.SemaphoreType.DMA((2,)),
         ],
-        out_specs=pl.BlockSpec((nfeat, per_owner * fcols + share, TILE), lambda i: (0, 0, 0)),
-        out_shape=jax.ShapeDtypeStruct((nfeat, per_owner * fcols + share, TILE), BF16),
-        scratch_shapes=[pltpu.VMEM((fcols, 2 * hid), BF16)],
         name="pack",
-        compiler_params=pltpu.CompilerParams(vmem_limit_bytes=16 << 20),
+        compiler_params=pltpu.CompilerParams(vmem_limit_bytes=60 << 20),
         cost_estimate=pl.CostEstimate(flops=0, bytes_accessed=3 << 20, transcendentals=0),
     )(place, feats, w_self, w_neigh)
 
@@ -196,13 +225,7 @@
     halves = hid // TILE
     out_rows = halves * fcols + 8
 
-    def kernel(at, pre_hbm, a_ref, wn_hbm, x_ref, up_ref, hid_ref, g_ref, pre, wn, deltas, sem):
-        get_wn = pltpu.make_async_copy(wn_hbm, wn, sem.at[0])
-        get_pre = pltpu.make_async_copy(pre_hbm, pre, sem.at[1])
-        get_wn.start()
-        get_pre.start()
-        get_wn.wait()
-        get_pre.wait()
+    def kernel(at, pre, a_ref, wn, x_ref, up_ref, hid_ref, g_ref, deltas):
         gb = jnp.zeros((1, hid), F32)
         for q in range(tiles):
             here = slice(q * TILE, (q + 1) * TILE)
@@ -233,24 +256,13 @@
 
     return pl.pallas_call(
         kernel,
-        in_specs=[
-            pl.BlockSpec(memory_space=pltpu.SMEM),
-            pl.BlockSpec(memory_space=pl.ANY),
-            *in_vmem(1),
-            pl.BlockSpec(memory_space=pl.ANY),
-            *in_vmem(2),
-        ],
+        in_specs=[pl.BlockSpec(memory_space=pltpu.SMEM)] + in_vmem(5),
         out_specs=in_vmem(2),
         out_shape=[
             jax.ShapeDtypeStruct((rows, hid), BF16),
             jax.ShapeDtypeStruct((2, nfeat, out_rows, TILE), BF16),
         ],
-        scratch_shapes=[
-            pltpu.VMEM((tiles, TILE, hid), F32),
-            pltpu.VMEM((feats, hid), BF16),
-            pltpu.VMEM((rows, hid), BF16),
-            pltpu.SemaphoreType.DMA((2,)),
-        ],
+        scratch_shapes=[pltpu.VMEM((rows, hid), BF16)],
         name="layer",
         compiler_params=pltpu.CompilerParams(vmem_limit_bytes=24 << 20),
         cost_estimate=pl.CostEstimate(
@@ -259,25 +271,24 @@
     )(place, pre_own, a_rows, w_neigh, x_rows, upstream)
 
 
-def finish(place, terms, fcols, hid):
-    halves = hid // TILE
-
-    def kernel(at, *refs):
-        ins, (gs_ref, gn_ref, gb_ref) = refs[: len(terms)], refs[len(terms) :]
-        mine = sum(ref[...] for ref in ins[0::2])
-        other = sum(ref[...] for ref in ins[1::2])
+def finish(place, mine, other, fcols):
+    halves = (mine.shape[0] - 8) // fcols
+    hid = halves * TILE
+
+    def kernel(at, m_ref, o_ref, gs_ref, gn_ref, gb_ref):
         first = lax.rem(at[0], 2) == 0
-        both = mine + other
         for h in range(halves):
             lanes, rows = slice(h * TILE, (h + 1) * TILE), slice(h * fcols, (h + 1) * fcols)
-            gs_ref[:, lanes] = jnp.where(first, mine[rows], other[rows])
-            gn_ref[:, lanes] = jnp.where(first, other[rows], mine[rows])
-            at_row = halves * fcols + h
-            gb_ref[:, lanes] = sum(both[at_row + halves * p : at_row + halves * p + 1] for p in range(3))
-
-    return pl.pallas_call(
-        kernel,
-        in_specs=[pl.BlockSpec(memory_space=pltpu.SMEM)] + in_vmem(len(terms)),
+            gs_ref[:, lanes] = jnp.where(first, m_ref[rows], o_ref[rows])
+            gn_ref[:, lanes] = jnp.where(first, o_ref[rows], m_ref[rows])
+        both = m_ref[halves * fcols :] + o_ref[halves * fcols :]
+        for h in range(halves):
+            parts = [both[halves * p + h : halves * p + h + 1] for p in range(3)]
+            gb_ref[:, h * TILE : (h + 1) * TILE] = parts[0] + parts[1] + parts[2]
+
+    return pl.pallas_call(
+        kernel,
+        in_specs=[pl.BlockSpec(memory_space=pltpu.SMEM)] + in_vmem(2),
         out_specs=in_vmem(3),
         out_shape=[
             jax.ShapeDtypeStruct((fcols, hid), F32),
@@ -286,7 +297,7 @@
         ],
         name="finish",
         compiler_params=pltpu.CompilerParams(vmem_limit_bytes=8 << 20),
-    )(place, *terms)
+    )(place, mine, other)
 
 
 def body(features_t, tile_weights, tile_dst, tile_src, tile_count, w_self, w_neigh, bias, grad_hidden):
@@ -323,8 +334,9 @@
         pair = (grads[0].astype(F32) + got.astype(F32)).astype(BF16)
         arrived = lax.all_to_all(pair, "feat", 0, 0, tiled=True)
         total = jnp.sum(arrived.astype(F32), axis=0)
-        terms = [total] + direct(total, range(1, nv))
-        grad_self, grad_neigh, grad_bias = finish(place, terms, fcols, hid)
+        total = sum(direct(total, (2, 4, 6)), total)
+        [other] = direct(total, (1,))
+        grad_self, grad_neigh, grad_bias = finish(place, total, other, fcols)
     return (hidden, grad_self, grad_neigh, grad_bias[0])
 
 

time: 122 us -> 118 us (0.967)
  local copies, waits for them, and re-layouts: 5.13 us -> 1.07 us
  starting transfers between devices: 39.2 us -> 36.1 us
  Pallas kernels: 22.4 us -> 24.8 us
    unnamed x20 -> x12, local copies, waits for them, and re-layouts: 5.04 us -> 0.98 us
    ppermute x12 -> x9, starting transfers between devices: 20.5 us -> 17.3 us  [direct(): lax.ppermute(value, 'vgroup', [(a, a ^ bit) for a in range(nv)])]
    ppermute x12 -> x9, waiting for transfers between devices: 11.6 us -> 13.7 us  [direct(): lax.ppermute(value, 'vgroup', [(a, a ^ bit) for a in range(nv)])]
    pallas_call x2, Pallas kernels: 2.17 us -> 3.62 us  [the longest x1 2.16 us: pack(): pl.pallas_call(kernel, in_specs=[pl.BlockSpec(memory_space=pltpu.SMEM)] +...]
  transfers between devices with their start and end apart: 14 -> 11, of which waited for: 9 -> 10; matrix products, arithmetic and copies ran while one was open for 0% -> 0% of each run, Pallas kernels for 16% -> 17%
where the time goes in v3:
time: 118 us
  starting transfers between devices  36.1 us (31%)
  waiting for transfers between devices  31.3 us (27%)
  Pallas kernels  24.8 us (21%)
  blocking collectives  22.7 us (19%)
  between operations  1.43 us (1%)
    all_to_all x1, blocking collectives, body(): arrived = lax.all_to_all(pair, 'feat', 0, 0, tiled=True)  22.7 us
    pallas_call x1, Pallas kernels, aggregate(): pl.pallas_call(kernel, grid_spec=pltpu.PrefetchScalarGridSpec(num_scalar_...  19.9 us
    ppermute x9, starting transfers between devices, direct(): lax.ppermute(value, 'vgroup', [(a, a ^ bit) for a in range(nv)])  17.3 us
    ppermute x9, waiting for transfers between devices, direct(): lax.ppermute(value, 'vgroup', [(a, a ^ bit) for a in range(nv)])  13.7 us
    all_to_all x1, starting transfers between devices, body(): x_rows = lax.all_to_all(outgoing, 'feat', 0, 0, tiled=True)  12.2 us
    all_to_all x1, waiting for transfers between devices, body(): a_rows = lax.all_to_all(agg, 'feat', 0, 0, tiled=True)  10.5 us
    all_to_all x1, waiting for transfers between devices, body(): x_rows = lax.all_to_all(outgoing, 'feat', 0, 0, tiled=True)  7.1 us
    all_to_all x1, starting transfers between devices, body(): a_rows = lax.all_to_all(agg, 'feat', 0, 0, tiled=True)  6.6 us
  transfers between devices with their start and end apart: 11, of which 10 were waited for; matrix products, arithmetic and copies ran while one was open for 0% of the time, Pallas kernels for 17%

profile of v3, /device:TPU:1, one launch (start us, length us, event | category | flops | bytes accessed | tf_op | source)
XLA Modules:
  0.0 117.8 jit_solution(9937749898659101472)
XLA Ops:
  0.6 2.2 %pack.1 = bf16[32,144,128]{2,1,0:T(8,128)(2,1)} custom-call(s32[1]{0:T(128)} %bitcast.at, bf16[32,32768]{1,0:T(8,128)(2,1)} %bitcast.17, bf16[32,256]{1,0:T(8,128)(2,1)} %ws_hbm.1, bf16[32,256]{1,0:T(8,128)(2,1)} %wn_hbm.1), custom_call_target="tpu_custom_call" | custom-call | bytes 3145728 | tf_op jit(solution)/shard_map/send_features/pack/pallas_call | solution.py:158
  2.8 0.0 copy-start.3
  2.8 12.2 %all-to-all-start = ((bf16[32,144,128]{2,1,0:T(8,128)(2,1)}), bf16[32,144,128]{2,1,0:T(8,128)(2,1)S(1)}, u32[]{:S(2)}, u32[]{:S(2)}) async-start(bf16[32,144,128]{2,1,0:T(8,128)(2,1)} %pack.1), calls=%async_computation | async-start | bytes 2359296 | tf_op jit(solution)/shard_map/send_features/all_to_all | solution.py:317
  15.7 19.9 %aggregate.1 = bf16[32,128,128]{2,1,0:T(8,128)(2,1)S(1)} custom-call(s32[1024]{0:T(1024)S(1)} %bitcast.19, s32[1024]{0:T(1024)S(1)} %bitcast.20, s32[1]{0:T(128)S(6)} %copy.13.cnt, bf16[32,32768]{1,0:T(8,128)(2,1)S(1)} %bitcast.18, bf16[1024,128,128]{2,1,0:T(8,128)(2,1)} %bitcast.22), custom_call_target="tpu_custom_call" | custom-call | flops 1073741824 | bytes 35651584 | tf_op jit(solution)/shard_map/aggregate/pallas_call | solution.py:78
  35.6 0.9 copy-done.1
  36.6 7.1 %all-to-all-done.x_ref = bf16[32,144,128]{2,1,0:T(8,128)(2,1)S(1)} async-done(((bf16[32,144,128]{2,1,0:T(8,128)(2,1)}), bf16[32,144,128]{2,1,0:T(8,128)(2,1)S(1)}, u32[]{:S(2)}, u32[]{:S(2)}) %all-to-all-start) | async-done | bytes 1179680 | tf_op jit(solution)/shard_map/send_features/all_to_all | solution.py:317
  43.7 6.6 %all-to-all-start.1 = ((bf16[32,128,128]{2,1,0:T(8,128)(2,1)}), bf16[32,128,128]{2,1,0:T(8,128)(2,1)S(1)}, u32[]{:S(2)}, u32[]{:S(2)}) async-start(bf16[32,128,128]{2,1,0:T(8,128)(2,1)} %copy-done.1), calls=%async_computation.1 | async-start | bytes 2097152 | tf_op jit(solution)/shard_map/send_aggregated/all_to_all | solution.py:322
  50.3 2.8 %collective-permute-start.1 = (bf16[32,16,128]{2,1,0:T(8,128)(2,1)S(1)}, bf16[32,16,128]{2,1,0:T(8,128)(2,1)S(1)}, u32[]{:S(2)}, u32[]{:S(2)}) collective-permute-start(bf16[32,16,128]{2,1,0:T(8,128)(2,1)S(1)} %get-tuple-element.23), channel_id=1, source_target_pairs={{0,128},{32,160},{64,192},{96,224},{128,0},{160,32},{192,64},{224,... | collective-permute-start | bytes 393224 | tf_op jit(solution)/shard_map/weights_over_vgroup/ppermute | solution.py:313
  53.1 0.3 collective-permute-start
  53.5 0.6 collective-permute-start.2
  54.0 1.7 %collective-permute-done.1 = bf16[32,16,128]{2,1,0:T(8,128)(2,1)S(1)} collective-permute-done((bf16[32,16,128]{2,1,0:T(8,128)(2,1)S(1)}, bf16[32,16,128]{2,1,0:T(8,128)(2,1)S(1)}, u32[]{:S(2)}, u32[]{:S(2)}) %collective-permute-start.1) | collective-permute-done | bytes 131104 | tf_op jit(solution)/shard_map/weights_over_vgroup/ppermute | solution.py:313
  55.7 1.9 %collective-permute-done = bf16[32,16,128]{2,1,0:T(8,128)(2,1)S(1)} collective-permute-done((bf16[32,16,128]{2,1,0:T(8,128)(2,1)S(1)}, bf16[32,16,128]{2,1,0:T(8,128)(2,1)S(1)}, u32[]{:S(2)}, u32[]{:S(2)}) %collective-permute-start) | collective-permute-done | bytes 131104 | tf_op jit(solution)/shard_map/weights_over_vgroup/ppermute | solution.py:313
  57.6 2.5 %collective-permute-done.2 = bf16[32,16,128]{2,1,0:T(8,128)(2,1)S(1)} collective-permute-done((bf16[32,16,128]{2,1,0:T(8,128)(2,1)S(1)}, bf16[32,16,128]{2,1,0:T(8,128)(2,1)S(1)}, u32[]{:S(2)}, u32[]{:S(2)}) %collective-permute-start.2) | collective-permute-done | bytes 131104 | tf_op jit(solution)/shard_map/weights_over_vgroup/ppermute | solution.py:313
  60.1 0.1 pad_maximum_fusion.w0
  60.2 2.3 %collective-permute-start.3 = (bf16[4,32,16,128]{3,2,1,0:T(8,128)(2,1)S(1)}, bf16[4,32,16,128]{3,2,1,0:T(8,128)(2,1)S(1)}, u32[]{:S(2)}, u32[]{:S(2)}) collective-permute-start(bf16[4,32,16,128]{3,2,1,0:T(8,128)(2,1)S(1)} %pad_maximum_fusion.w0), channel_id=1, source_target_pairs={{0,32},{32,0},{64,96},{96,64},{128,160},{160,128},{192,224},{224,1... | collective-permute-start | bytes 1572872 | tf_op jit(solution)/shard_map/weights_over_vgroup/ppermute | solution.py:313
  62.5 1.5 %collective-permute-done.3.w1 = bf16[4,32,16,128]{3,2,1,0:T(8,128)(2,1)S(1)} collective-permute-done((bf16[4,32,16,128]{3,2,1,0:T(8,128)(2,1)S(1)}, bf16[4,32,16,128]{3,2,1,0:T(8,128)(2,1)S(1)}, u32[]{:S(2)}, u32[]{:S(2)}) %collective-permute-start.3) | collective-permute-done | bytes 524320 | tf_op jit(solution)/shard_map/weights_over_vgroup/ppermute | solution.py:313
  64.1 0.7 own_part.1
  64.8 10.5 %all-to-all-done.1.a_ref = bf16[32,128,128]{2,1,0:T(8,128)(2,1)S(1)} async-done(((bf16[32,128,128]{2,1,0:T(8,128)(2,1)}), bf16[32,128,128]{2,1,0:T(8,128)(2,1)S(1)}, u32[]{:S(2)}, u32[]{:S(2)}) %all-to-all-start.1) | async-done | bytes 1048608 | tf_op jit(solution)/shard_map/send_aggregated/all_to_all | solution.py:322
  75.2 1.5 %layer.1 = (bf16[512,256]{1,0:T(8,128)(2,1)}, bf16[2,32,72,128]{3,2,1,0:T(8,128)(2,1)S(1)}) custom-call(s32[1]{0:T(128)} %bitcast.at, f32[4,128,256]{2,1,0:T(8,128)S(1)} %get-tuple-element.14.pre, bf16[32,128,128]{2,1,0:T(8,128)(2,1)S(1)} %all-to-all-done.1.a_ref, bf16[1024,256]{1,0:T(8,128)(2,1)S(1)} %get-tuple-element.16.wn, ...), custom_call_target="tpu_custom_call" | custom-call | flops 805306368 | bytes 6291456 | tf_op jit(solution)/shard_map/layer/pallas_call | solution.py:257
  76.8 4.1 %collective-permute-start.4 = (bf16[32,72,128]{2,1,0:T(8,128)(2,1)S(1)}, bf16[32,72,128]{2,1,0:T(8,128)(2,1)S(1)}, u32[]{:S(2)}, u32[]{:S(2)}) collective-permute-start(bf16[32,72,128]{2,1,0:T(8,128)(2,1)S(1)} %slice_bitcast_fusion), channel_id=1, source_target_pairs={{0,32},{32,0},{64,96},{96,64},{128,160},{160,128},{192,224},{224,1... | collective-permute-start | bytes 1769480 | tf_op jit(solution)/shard_map/reduce_grads/ppermute | solution.py:313
  80.9 1.6 %collective-permute-done.4 = bf16[32,72,128]{2,1,0:T(8,128)(2,1)S(1)} collective-permute-done((bf16[32,72,128]{2,1,0:T(8,128)(2,1)S(1)}, bf16[32,72,128]{2,1,0:T(8,128)(2,1)S(1)}, u32[]{:S(2)}, u32[]{:S(2)}) %collective-permute-start.4) | collective-permute-done | bytes 589856 | tf_op jit(solution)/shard_map/reduce_grads/ppermute | solution.py:313
  82.5 0.2 fusion
  82.6 22.7 %all_to_all.15 = bf16[32,72,128]{2,1,0:T(8,128)(2,1)S(1)} all-to-all(bf16[32,72,128]{2,1,0:T(8,128)(2,1)S(1)} %fusion), channel_id=1, replica_groups=mesh['vgroup'=8,'feat'=32] {'feat'}, dimensions={0} | all-to-all | bytes 1179648 | tf_op jit(solution)/shard_map/reduce_grads/all_to_all | solution.py:335
  105.4 0.1 convert_reduce_fusion
  105.5 2.6 %collective-permute-start.7 = (f32[72,128]{1,0:T(8,128)S(1)}, f32[72,128]{1,0:T(8,128)S(1)}, u32[]{:S(2)}, u32[]{:S(2)}) collective-permute-start(f32[72,128]{1,0:T(8,128)S(1)} %convert_reduce_fusion), channel_id=1, source_target_pairs={{0,192},{32,224},{64,128},{96,160},{128,64},{160,96},{192,0},{224,... | collective-permute-start | bytes 110600 | tf_op jit(solution)/shard_map/reduce_grads/ppermute | solution.py:313
  108.0 0.5 collective-permute-start.6
  108.6 0.3 collective-permute-start.5
  108.8 0.8 collective-permute-done.7
  109.6 2.8 %collective-permute-done.6 = f32[72,128]{1,0:T(8,128)S(1)} collective-permute-done((f32[72,128]{1,0:T(8,128)S(1)}, f32[72,128]{1,0:T(8,128)S(1)}, u32[]{:S(2)}, u32[]{:S(2)}) %collective-permute-start.6) | collective-permute-done | bytes 36896 | tf_op jit(solution)/shard_map/reduce_grads/ppermute | solution.py:313
  112.4 3.8 %collective-permute-start.8 = (f32[72,128]{1,0:T(8,128)S(1)}, f32[72,128]{1,0:T(8,128)S(1)}, u32[]{:S(2)}, u32[]{:S(2)}) collective-permute-start(f32[72,128]{1,0:T(8,128)S(1)} %add_add_fusion.m_ref), channel_id=1, source_target_pairs={{0,32},{32,0},{64,96},{96,64},{128,160},{160,128},{192,224},{224,1... | collective-permute-start | bytes 110600 | tf_op jit(solution)/shard_map/reduce_grads/ppermute | solution.py:313
  116.3 0.9 collective-permute-done.8.o_ref
  117.1 0.6 finish.1
  (14 shorter events, 0.1 us)
Async XLA Ops:
  2.8 12.9 %copy-start = (bf16[1,32,32768]{2,1,0:T(8,128)(2,1)S(1)}, bf16[1,32,32768]{2,1,0:T(8,128)(2,1)}, u32[]{:S(2)}) copy-start(bf16[1,32,32768]{2,1,0:T(8,128)(2,1)} %param.9) | copy-start | bytes 6291460
  2.8 12.9 %copy-start.3 = (s32[1,1024]{1,0:T(1,128)S(1)}, s32[1,1024]{1,0:T(1,128)}, u32[]{:S(2)}) copy-start(s32[1,1024]{1,0:T(1,128)} %param.11) | copy-start | bytes 12292
  2.8 12.9 %copy-start.4 = (s32[1,1024]{1,0:T(1,128)S(1)}, s32[1,1024]{1,0:T(1,128)}, u32[]{:S(2)}) copy-start(s32[1,1024]{1,0:T(1,128)} %param.12) | copy-start | bytes 12292
  2.8 40.8 %all-to-all-start = ((bf16[32,144,128]{2,1,0:T(8,128)(2,1)}), bf16[32,144,128]{2,1,0:T(8,128)(2,1)S(1)}, u32[]{:S(2)}, u32[]{:S(2)}) async-start(bf16[32,144,128]{2,1,0:T(8,128)(2,1)} %pack.1), calls=%async_computation | async-start | bytes 2359296 | tf_op jit(solution)/shard_map/send_features/all_to_all | solution.py:317
  35.6 1.0 copy-start.1
  43.7 31.6 %all-to-all-start.1 = ((bf16[32,128,128]{2,1,0:T(8,128)(2,1)}), bf16[32,128,128]{2,1,0:T(8,128)(2,1)S(1)}, u32[]{:S(2)}, u32[]{:S(2)}) async-start(bf16[32,128,128]{2,1,0:T(8,128)(2,1)} %copy-done.1), calls=%async_computation.1 | async-start | bytes 2097152 | tf_op jit(solution)/shard_map/send_aggregated/all_to_all | solution.py:322
  50.3 13.8 %copy-start.5 = (f32[256]{0:T(256)S(1)}, f32[256]{0:T(256)}, u32[]{:S(2)}) copy-start(f32[256]{0:T(256)} %param.16) | copy-start | bytes 3076
  50.3 5.4 %collective-permute-start.1 = (bf16[32,16,128]{2,1,0:T(8,128)(2,1)S(1)}, bf16[32,16,128]{2,1,0:T(8,128)(2,1)S(1)}, u32[]{:S(2)}, u32[]{:S(2)}) collective-permute-start(bf16[32,16,128]{2,1,0:T(8,128)(2,1)S(1)} %get-tuple-element.23), channel_id=1, source_target_pairs={{0,128},{32,160},{64,192},{96,224},{128,0},{160,32},{192,64},{224,... | collective-permute-start | bytes 393224 | tf_op jit(solution)/shard_map/weights_over_vgroup/ppermute | solution.py:313
  53.1 4.5 %collective-permute-start = (bf16[32,16,128]{2,1,0:T(8,128)(2,1)S(1)}, bf16[32,16,128]{2,1,0:T(8,128)(2,1)S(1)}, u32[]{:S(2)}, u32[]{:S(2)}) collective-permute-start(bf16[32,16,128]{2,1,0:T(8,128)(2,1)S(1)} %get-tuple-element.23), channel_id=1, source_target_pairs={{0,64},{32,96},{64,0},{96,32},{128,192},{160,224},{192,128},{224,1... | collective-permute-start | bytes 393224 | tf_op jit(solution)/shard_map/weights_over_vgroup/ppermute | solution.py:313
  53.5 6.6 %collective-permute-start.2 = (bf16[32,16,128]{2,1,0:T(8,128)(2,1)S(1)}, bf16[32,16,128]{2,1,0:T(8,128)(2,1)S(1)}, u32[]{:S(2)}, u32[]{:S(2)}) collective-permute-start(bf16[32,16,128]{2,1,0:T(8,128)(2,1)S(1)} %get-tuple-element.23), channel_id=1, source_target_pairs={{0,192},{32,224},{64,128},{96,160},{128,64},{160,96},{192,0},{224,... | collective-permute-start | bytes 393224 | tf_op jit(solution)/shard_map/weights_over_vgroup/ppermute | solution.py:313
  60.2 15.1 %copy-start.2 = (bf16[512,256]{1,0:T(8,128)(2,1)S(1)}, bf16[512,256]{1,0:T(8,128)(2,1)}, u32[]{:S(2)}) copy-start(bf16[512,256]{1,0:T(8,128)(2,1)} %up_ref.1) | copy-start | bytes 786436
  60.2 3.9 %collective-permute-start.3 = (bf16[4,32,16,128]{3,2,1,0:T(8,128)(2,1)S(1)}, bf16[4,32,16,128]{3,2,1,0:T(8,128)(2,1)S(1)}, u32[]{:S(2)}, u32[]{:S(2)}) collective-permute-start(bf16[4,32,16,128]{3,2,1,0:T(8,128)(2,1)S(1)} %pad_maximum_fusion.w0), channel_id=1, source_target_pairs={{0,32},{32,0},{64,96},{96,64},{128,160},{160,128},{192,224},{224,1... | collective-permute-start | bytes 1572872 | tf_op jit(solution)/shard_map/weights_over_vgroup/ppermute | solution.py:313
  76.8 5.7 %collective-permute-start.4 = (bf16[32,72,128]{2,1,0:T(8,128)(2,1)S(1)}, bf16[32,72,128]{2,1,0:T(8,128)(2,1)S(1)}, u32[]{:S(2)}, u32[]{:S(2)}) collective-permute-start(bf16[32,72,128]{2,1,0:T(8,128)(2,1)S(1)} %slice_bitcast_fusion), channel_id=1, source_target_pairs={{0,32},{32,0},{64,96},{96,64},{128,160},{160,128},{192,224},{224,1... | collective-permute-start | bytes 1769480 | tf_op jit(solution)/shard_map/reduce_grads/ppermute | solution.py:313
  105.5 4.1 %collective-permute-start.7 = (f32[72,128]{1,0:T(8,128)S(1)}, f32[72,128]{1,0:T(8,128)S(1)}, u32[]{:S(2)}, u32[]{:S(2)}) collective-permute-start(f32[72,128]{1,0:T(8,128)S(1)} %convert_reduce_fusion), channel_id=1, source_target_pairs={{0,192},{32,224},{64,128},{96,160},{128,64},{160,96},{192,0},{224,... | collective-permute-start | bytes 110600 | tf_op jit(solution)/shard_map/reduce_grads/ppermute | solution.py:313
  108.0 4.3 %collective-permute-start.6 = (f32[72,128]{1,0:T(8,128)S(1)}, f32[72,128]{1,0:T(8,128)S(1)}, u32[]{:S(2)}, u32[]{:S(2)}) collective-permute-start(f32[72,128]{1,0:T(8,128)S(1)} %convert_reduce_fusion), channel_id=1, source_target_pairs={{0,128},{32,160},{64,192},{96,224},{128,0},{160,32},{192,64},{224,... | collective-permute-start | bytes 110600 | tf_op jit(solution)/shard_map/reduce_grads/ppermute | solution.py:313
  108.6 3.8 %collective-permute-start.5 = (f32[72,128]{1,0:T(8,128)S(1)}, f32[72,128]{1,0:T(8,128)S(1)}, u32[]{:S(2)}, u32[]{:S(2)}) collective-permute-start(f32[72,128]{1,0:T(8,128)S(1)} %convert_reduce_fusion), channel_id=1, source_target_pairs={{0,64},{32,96},{64,0},{96,32},{128,192},{160,224},{192,128},{224,1... | collective-permute-start | bytes 110600 | tf_op jit(solution)/shard_map/reduce_grads/ppermute | solution.py:313
  112.4 4.7 %collective-permute-start.8 = (f32[72,128]{1,0:T(8,128)S(1)}, f32[72,128]{1,0:T(8,128)S(1)}, u32[]{:S(2)}, u32[]{:S(2)}) collective-permute-start(f32[72,128]{1,0:T(8,128)S(1)} %add_add_fusion.m_ref), channel_id=1, source_target_pairs={{0,32},{32,0},{64,96},{96,64},{128,160},{160,128},{192,224},{224,1... | collective-permute-start | bytes 110600 | tf_op jit(solution)/shard_map/reduce_grads/ppermute | solution.py:313

commit v4 on v3

--- a/solution.py
+++ b/solution.py
@@ -6,8 +6,8 @@
 from jax.sharding import PartitionSpec as P
 
 TILE = 128
-SLOTS_STEP = 128
-UNROLL = 32
+SLOTS_STEP = 64
+BUFFERS = 4
 GELU_A = 0.7978845608
 GELU_B = 0.044715
 BF16 = jnp.bfloat16
@@ -19,81 +19,84 @@
     slots = weights.shape[0]
     dtiles = nsrc // TILE // 2
     per_owner = dtiles // nfeat
-    steps = slots // SLOTS_STEP
-
-    def kernel(dst, src, cnt, x_ref, w_ref, o_ref, acc, out, sem):
-        i = pl.program_id(0)
-
-        @pl.when(i == 0)
-        def _():
-            acc[...] = jnp.zeros_like(acc)
-
-        base = i * SLOTS_STEP
-        live = jnp.clip(cnt[0] - base, 0, SLOTS_STEP)
+    parts = 4
+    owners = nfeat // parts
+
+    def kernel(dst, src, cnt, x_ref, w_hbm, o_hbm, acc, out, buf, sem_w, sem_o):
+        steps = pl.cdiv(cnt[0], SLOTS_STEP)
+
+        def fetch(i):
+            place = lax.rem(i, BUFFERS)
+            return pltpu.make_async_copy(
+                w_hbm.at[pl.ds(i * SLOTS_STEP, SLOTS_STEP)], buf.at[place], sem_w.at[place]
+            )
+
+        for i in range(BUFFERS - 1):
+
+            @pl.when(i < steps)
+            def _():
+                fetch(i).start()
+
+        acc[...] = jnp.zeros_like(acc)
         zero = jnp.zeros((fcols, TILE), BF16)
 
         def source(slot):
             return x_ref[:, pl.ds(pl.multiple_of(src[slot] * TILE, TILE), TILE)]
 
-        def group(g, carry):
-            first = g * UNROLL
+        def step(i, carry):
+            @pl.when(i + BUFFERS - 1 < steps)
+            def _():
+                fetch(i + BUFFERS - 1).start()
+
+            fetch(i).wait()
+            w_ref = buf.at[lax.rem(i, BUFFERS)]
+            first = i * SLOTS_STEP
             products = []
-            for u in range(0, UNROLL, 2):
-                slot = base + first + u
+            for u in range(0, SLOTS_STEP, 2):
                 left = jnp.concatenate(
                     [
-                        jnp.concatenate([source(slot), zero], 1),
-                        jnp.concatenate([zero, source(slot + 1)], 1),
+                        jnp.concatenate([source(first + u), zero], 1),
+                        jnp.concatenate([zero, source(first + u + 1)], 1),
                     ],
                     0,
                 )
-                right = jnp.concatenate([w_ref[first + u], w_ref[first + u + 1]], 1)
-                both = lax.dot_general(
-                    left, right, (((1,), (1,)), ((), ())), preferred_element_type=F32
+                right = jnp.concatenate([w_ref[u], w_ref[u + 1]], 1)
+                both = lax.dot_general(left, right, (((1,), (1,)), ((), ())), preferred_element_type=F32)
+                products += [both[:fcols], both[fcols:]]
+            for u in range(SLOTS_STEP):
+                acc[dst[first + u]] += jnp.where(first + u < cnt[0], products[u], 0.0)
+            return carry
+
+        lax.fori_loop(0, steps, step, 0)
+        put = []
+        for p in range(parts):
+            tiles = acc[p * owners * per_owner : (p + 1) * owners * per_owner]
+            out[p * owners : (p + 1) * owners] = tiles.reshape(owners, per_owner * fcols, TILE).astype(BF16)
+            put.append(
+                pltpu.make_async_copy(
+                    out.at[pl.ds(p * owners, owners)], o_hbm.at[pl.ds(p * owners, owners)], sem_o.at[p]
                 )
-                products += [both[:fcols], both[fcols:]]
-            for u in range(UNROLL):
-                slot = base + first + u
-                acc[dst[slot]] += jnp.where(slot < cnt[0], products[u], 0.0)
-            return carry
-
-        lax.fori_loop(0, pl.cdiv(live, UNROLL), group, 0)
-
-        @pl.when(i == steps - 1)
-        def _():
-            part = nfeat // 4
-            copies = []
-            for p in range(4):
-                tiles = acc[p * part * per_owner : (p + 1) * part * per_owner]
-                out[p * part : (p + 1) * part] = tiles.reshape(part, per_owner * fcols, TILE).astype(BF16)
-                copies.append(
-                    pltpu.make_async_copy(
-                        out.at[pl.ds(p * part, part)], o_ref.at[pl.ds(p * part, part)], sem.at[p]
-                    )
-                )
-                copies[-1].start()
-            for c in copies:
-                c.wait()
-
-    return pl.pallas_call(
-        kernel,
-        grid_spec=pltpu.PrefetchScalarGridSpec(
-            num_scalar_prefetch=3,
-            grid=(steps,),
-            in_specs=[
-                pl.BlockSpec((fcols, nsrc), lambda i, *_: (0, 0)),
-                pl.BlockSpec((SLOTS_STEP, TILE, TILE), lambda i, *_: (i, 0, 0)),
-            ],
-            out_specs=pl.BlockSpec(memory_space=pltpu.HBM),
-            scratch_shapes=[
-                pltpu.VMEM((dtiles, fcols, TILE), F32),
-                pltpu.VMEM((nfeat, per_owner * fcols, TILE), BF16),
-                pltpu.SemaphoreType.DMA((4,)),
-            ],
-        ),
-        out_shape=jax.ShapeDtypeStruct((nfeat, per_owner * fcols, TILE), BF16),
+            )
+            put[-1].start()
+        for c in put:
+            c.wait()
+
+    shape = (nfeat, per_owner * fcols, TILE)
+    return pl.pallas_call(
+        kernel,
+        in_specs=[pl.BlockSpec(memory_space=pltpu.SMEM)] * 3
+        + [pl.BlockSpec(memory_space=pltpu.VMEM), pl.BlockSpec(memory_space=pl.ANY)],
+        out_specs=pl.BlockSpec(memory_space=pl.ANY),
+        scratch_shapes=[
+            pltpu.VMEM((dtiles, fcols, TILE), F32),
+            pltpu.VMEM(shape, BF16),
+            pltpu.VMEM((BUFFERS, SLOTS_STEP, TILE, TILE), BF16),
+            pltpu.SemaphoreType.DMA((BUFFERS,)),
+            pltpu.SemaphoreType.DMA((parts,)),
+        ],
+        out_shape=jax.ShapeDtypeStruct(shape, BF16),
         name="aggregate",
-        compiler_params=pltpu.CompilerParams(vmem_limit_bytes=40 << 20),
+        compiler_params=pltpu.CompilerParams(vmem_limit_bytes=56 << 20),
         cost_estimate=pl.CostEstimate(
             flops=2 * slots * fcols * TILE * TILE,
             bytes_accessed=slots * TILE * TILE * 2 + fcols * nsrc * 2,
@@ -115,7 +118,7 @@
     hid = w_self.shape[1]
     per_owner = rows_dev // TILE
     share = fcols // 2
-
+    part_rows = share // 2
     parts = 4
     owners = nfeat // parts
 
@@ -149,12 +152,13 @@
                 for q in range(per_owner):
                     tile = c * per_owner + q
                     o_ref[c, q * fcols : (q + 1) * fcols, :] = x_ref[:, tile * TILE : (tile + 1) * TILE]
-                o_ref[c, per_owner * fcols :, :] = piece
+                first = c % 2 * part_rows
+                o_ref[c, per_owner * fcols :, :] = piece[first : first + part_rows]
             put[p].start()
         for c in put:
             c.wait()
 
-    out = (nfeat, per_owner * fcols + share, TILE)
+    out = (nfeat, per_owner * fcols + part_rows, TILE)
     return pl.pallas_call(
         kernel,
         in_specs=[pl.BlockSpec(memory_space=pltpu.SMEM)] + [pl.BlockSpec(memory_space=pl.ANY)] * 3,
@@ -322,7 +326,10 @@
         a_rows = lax.all_to_all(agg, "feat", 0, 0, tiled=True)
 
     with jax.named_scope("weights_over_vgroup"):
-        piece = x_rows[:, tiles * fcols :, :]
+        part = x_rows[:, tiles * fcols :, :]
+        other = lax.ppermute(part, "feat", [(a, a ^ 1) for a in range(nfeat)])
+        even = lax.axis_index("feat") % 2 == 0
+        piece = jnp.concatenate([jnp.where(even, part, other), jnp.where(even, other, part)], axis=1)
         same_core = jnp.stack([piece] + direct(piece, (2, 4, 6)))
         [other_core] = direct(same_core, (1,))
 

time: 118 us -> 117 us (level)
  starting transfers between devices: 36.1 us -> 41.8 us
  waiting for transfers between devices: 31.3 us -> 26.8 us
  Pallas kernels: 24.8 us -> 23.1 us
    all_to_all x1, waiting for transfers between devices: 10.5 us -> 3.49 us  [body(): a_rows = lax.all_to_all(agg, 'feat', 0, 0, tiled=True)]
    ppermute x9, starting transfers between devices: 17.3 us -> 21.9 us  [direct(): lax.ppermute(value, 'vgroup', [(a, a ^ bit) for a in range(nv)])]
    ppermute x0 -> x1, waiting for transfers between devices: none -> 2.34 us  [body(): other = lax.ppermute(part, 'feat', [(a, a ^ 1) for a in range(nfeat)])]
    pallas_call x1, Pallas kernels: 19.9 us -> 18.1 us  [aggregate(): pl.pallas_call(kernel, in_specs=[pl.BlockSpec(memory_space=pltpu.SMEM)] *...]
    all_to_all x1, waiting for transfers between devices: 7.1 us -> 8.56 us  [body(): x_rows = lax.all_to_all(outgoing, 'feat', 0, 0, tiled=True)]
    ppermute x0 -> x1, starting transfers between devices: none -> 1.32 us  [body(): other = lax.ppermute(part, 'feat', [(a, a ^ 1) for a in range(nfeat)])]
    ppermute x9, waiting for transfers between devices: 13.7 us -> 12.4 us  [direct(): lax.ppermute(value, 'vgroup', [(a, a ^ bit) for a in range(nv)])]
  transfers between devices with their start and end apart: 11 -> 12, of which waited for: 10 -> 11; matrix products, arithmetic and copies ran while one was open for 0% -> 0% of each run, Pallas kernels for 17% -> 16%
where the time goes in v4:
time: 117 us; the launch traced here: 116 us
  starting transfers between devices  41.8 us (36%)
  waiting for transfers between devices  26.8 us (23%)
  Pallas kernels  23.1 us (20%)
  blocking collectives  22.7 us (19%)
  between operations  1.38 us (1%)
    all_to_all x1, blocking collectives, body(): arrived = lax.all_to_all(pair, 'feat', 0, 0, tiled=True)  22.7 us
    ppermute x9, starting transfers between devices, direct(): lax.ppermute(value, 'vgroup', [(a, a ^ bit) for a in range(nv)])  21.9 us
    pallas_call x1, Pallas kernels, aggregate(): pl.pallas_call(kernel, in_specs=[pl.BlockSpec(memory_space=pltpu.SMEM)] *...  18.1 us
    ppermute x9, waiting for transfers between devices, direct(): lax.ppermute(value, 'vgroup', [(a, a ^ bit) for a in range(nv)])  12.4 us
    all_to_all x1, starting transfers between devices, body(): x_rows = lax.all_to_all(outgoing, 'feat', 0, 0, tiled=True)  12 us
    all_to_all x1, waiting for transfers between devices, body(): x_rows = lax.all_to_all(outgoing, 'feat', 0, 0, tiled=True)  8.56 us
    all_to_all x1, starting transfers between devices, body(): a_rows = lax.all_to_all(agg, 'feat', 0, 0, tiled=True)  6.48 us
    all_to_all x1, waiting for transfers between devices, body(): a_rows = lax.all_to_all(agg, 'feat', 0, 0, tiled=True)  3.49 us
  transfers between devices with their start and end apart: 12, of which 11 were waited for; matrix products, arithmetic and copies ran while one was open for 0% of the time, Pallas kernels for 16%

profile of v4, /device:TPU:1, one launch (start us, length us, event | category | flops | bytes accessed | tf_op | source)
XLA Modules:
  0.0 116.2 jit_solution(15312959363577722094)
XLA Ops:
  0.6 2.1 %pack.1 = bf16[32,136,128]{2,1,0:T(8,128)(2,1)} custom-call(s32[1]{0:T(128)} %bitcast.at, bf16[32,32768]{1,0:T(8,128)(2,1)} %bitcast.19, bf16[32,256]{1,0:T(8,128)(2,1)} %ws_hbm.1, bf16[32,256]{1,0:T(8,128)(2,1)} %wn_hbm.1), custom_call_target="tpu_custom_call" | custom-call | bytes 3145728 | tf_op jit(solution)/shard_map/send_features/pack/pallas_call | solution.py:162
  2.8 12.0 %all-to-all-start = ((bf16[32,136,128]{2,1,0:T(8,128)(2,1)}), bf16[32,136,128]{2,1,0:T(8,128)(2,1)S(1)}, u32[]{:S(2)}, u32[]{:S(2)}) async-start(bf16[32,136,128]{2,1,0:T(8,128)(2,1)} %pack.1), calls=%async_computation | async-start | bytes 2228224 | tf_op jit(solution)/shard_map/send_features/all_to_all | solution.py:321
  15.5 18.1 %aggregate.1 = bf16[32,128,128]{2,1,0:T(8,128)(2,1)} custom-call(s32[1024]{0:T(1024)} %bitcast.24, s32[1024]{0:T(1024)} %bitcast.25, s32[1]{0:T(128)S(6)} %copy.13.cnt, bf16[32,32768]{1,0:T(8,128)(2,1)} %bitcast.20, bf16[1024,128,128]{2,1,0:T(8,128)(2,1)} %bitcast.18), custom_call_target="tpu_custom_call" | custom-call | flops 1073741824 | bytes 35651584 | tf_op jit(solution)/shard_map/aggregate/pallas_call | solution.py:85
  33.6 8.6 %all-to-all-done.x_ref = bf16[32,136,128]{2,1,0:T(8,128)(2,1)S(1)} async-done(((bf16[32,136,128]{2,1,0:T(8,128)(2,1)}), bf16[32,136,128]{2,1,0:T(8,128)(2,1)S(1)}, u32[]{:S(2)}, u32[]{:S(2)}) %all-to-all-start) | async-done | bytes 1114144 | tf_op jit(solution)/shard_map/send_features/all_to_all | solution.py:321
  42.2 6.5 %all-to-all-start.1 = ((bf16[32,128,128]{2,1,0:T(8,128)(2,1)}), bf16[32,128,128]{2,1,0:T(8,128)(2,1)S(1)}, u32[]{:S(2)}, u32[]{:S(2)}) async-start(bf16[32,128,128]{2,1,0:T(8,128)(2,1)} %aggregate.1), calls=%async_computation.1 | async-start | bytes 2097152 | tf_op jit(solution)/shard_map/send_aggregated/all_to_all | solution.py:326
  48.7 1.3 %collective-permute-start = (bf16[32,8,128]{2,1,0:T(8,128)(2,1)S(1)}, bf16[32,8,128]{2,1,0:T(8,128)(2,1)S(1)}, u32[]{:S(2)}, u32[]{:S(2)}) collective-permute-start(bf16[32,8,128]{2,1,0:T(8,128)(2,1)S(1)} %slice.9), channel_id=1, source_target_pairs={{0,1},{1,0},{2,3},{3,2},{4,5},{5,4},{6,7},{7,6},{8,9},{9,8},{10,11... | collective-permute-start | bytes 196616 | tf_op jit(solution)/shard_map/weights_over_vgroup/ppermute | solution.py:330
  50.0 2.3 %collective-permute-done = bf16[32,8,128]{2,1,0:T(8,128)(2,1)S(1)} collective-permute-done((bf16[32,8,128]{2,1,0:T(8,128)(2,1)S(1)}, bf16[32,8,128]{2,1,0:T(8,128)(2,1)S(1)}, u32[]{:S(2)}, u32[]{:S(2)}) %collective-permute-start) | collective-permute-done | bytes 65568 | tf_op jit(solution)/shard_map/weights_over_vgroup/ppermute | solution.py:330
  52.4 2.8 %collective-permute-start.2 = (bf16[32,16,128]{2,1,0:T(8,128)(2,1)S(1)}, bf16[32,16,128]{2,1,0:T(8,128)(2,1)S(1)}, u32[]{:S(2)}, u32[]{:S(2)}) collective-permute-start(bf16[32,16,128]{2,1,0:T(8,128)(2,1)S(1)} %get-tuple-element.25), channel_id=1, source_target_pairs={{0,128},{32,160},{64,192},{96,224},{128,0},{160,32},{192,64},{224,... | collective-permute-start | bytes 393224 | tf_op jit(solution)/shard_map/weights_over_vgroup/ppermute | solution.py:317
  55.3 0.3 collective-permute-start.1
  55.6 0.6 collective-permute-start.3
  56.1 1.7 %collective-permute-done.2 = bf16[32,16,128]{2,1,0:T(8,128)(2,1)S(1)} collective-permute-done((bf16[32,16,128]{2,1,0:T(8,128)(2,1)S(1)}, bf16[32,16,128]{2,1,0:T(8,128)(2,1)S(1)}, u32[]{:S(2)}, u32[]{:S(2)}) %collective-permute-start.2) | collective-permute-done | bytes 131104 | tf_op jit(solution)/shard_map/weights_over_vgroup/ppermute | solution.py:317
  57.8 1.8 %collective-permute-done.1 = bf16[32,16,128]{2,1,0:T(8,128)(2,1)S(1)} collective-permute-done((bf16[32,16,128]{2,1,0:T(8,128)(2,1)S(1)}, bf16[32,16,128]{2,1,0:T(8,128)(2,1)S(1)}, u32[]{:S(2)}, u32[]{:S(2)}) %collective-permute-start.1) | collective-permute-done | bytes 131104 | tf_op jit(solution)/shard_map/weights_over_vgroup/ppermute | solution.py:317
  59.6 1.3 %collective-permute-done.3 = bf16[32,16,128]{2,1,0:T(8,128)(2,1)S(1)} collective-permute-done((bf16[32,16,128]{2,1,0:T(8,128)(2,1)S(1)}, bf16[32,16,128]{2,1,0:T(8,128)(2,1)S(1)}, u32[]{:S(2)}, u32[]{:S(2)}) %collective-permute-start.3) | collective-permute-done | bytes 131104 | tf_op jit(solution)/shard_map/weights_over_vgroup/ppermute | solution.py:317
  60.9 0.1 pad_maximum_fusion.w0
  61.0 7.0 %collective-permute-start.4 = (bf16[4,32,16,128]{3,2,1,0:T(8,128)(2,1)S(1)}, bf16[4,32,16,128]{3,2,1,0:T(8,128)(2,1)S(1)}, u32[]{:S(2)}, u32[]{:S(2)}) collective-permute-start(bf16[4,32,16,128]{3,2,1,0:T(8,128)(2,1)S(1)} %pad_maximum_fusion.w0), channel_id=1, source_target_pairs={{0,32},{32,0},{64,96},{96,64},{128,160},{160,128},{192,224},{224,1... | collective-permute-start | bytes 1572872 | tf_op jit(solution)/shard_map/weights_over_vgroup/ppermute | solution.py:317
  68.0 1.5 %collective-permute-done.4.w1 = bf16[4,32,16,128]{3,2,1,0:T(8,128)(2,1)S(1)} collective-permute-done((bf16[4,32,16,128]{3,2,1,0:T(8,128)(2,1)S(1)}, bf16[4,32,16,128]{3,2,1,0:T(8,128)(2,1)S(1)}, u32[]{:S(2)}, u32[]{:S(2)}) %collective-permute-start.4) | collective-permute-done | bytes 524320 | tf_op jit(solution)/shard_map/weights_over_vgroup/ppermute | solution.py:317
  69.5 0.7 own_part.1
  70.2 3.5 %all-to-all-done.1.a_ref = bf16[32,128,128]{2,1,0:T(8,128)(2,1)S(1)} async-done(((bf16[32,128,128]{2,1,0:T(8,128)(2,1)}), bf16[32,128,128]{2,1,0:T(8,128)(2,1)S(1)}, u32[]{:S(2)}, u32[]{:S(2)}) %all-to-all-start.1) | async-done | bytes 1048608 | tf_op jit(solution)/shard_map/send_aggregated/all_to_all | solution.py:326
  73.7 1.5 %layer.1 = (bf16[512,256]{1,0:T(8,128)(2,1)}, bf16[2,32,72,128]{3,2,1,0:T(8,128)(2,1)S(1)}) custom-call(s32[1]{0:T(128)} %bitcast.at, f32[4,128,256]{2,1,0:T(8,128)S(1)} %get-tuple-element.14.pre, bf16[32,128,128]{2,1,0:T(8,128)(2,1)S(1)} %all-to-all-done.1.a_ref, bf16[1024,256]{1,0:T(8,128)(2,1)S(1)} %get-tuple-element.16.wn, ...), custom_call_target="tpu_custom_call" | custom-call | flops 805306368 | bytes 6291456 | tf_op jit(solution)/shard_map/layer/pallas_call | solution.py:261
  75.2 4.1 %collective-permute-start.5 = (bf16[32,72,128]{2,1,0:T(8,128)(2,1)S(1)}, bf16[32,72,128]{2,1,0:T(8,128)(2,1)S(1)}, u32[]{:S(2)}, u32[]{:S(2)}) collective-permute-start(bf16[32,72,128]{2,1,0:T(8,128)(2,1)S(1)} %slice_bitcast_fusion), channel_id=1, source_target_pairs={{0,32},{32,0},{64,96},{96,64},{128,160},{160,128},{192,224},{224,1... | collective-permute-start | bytes 1769480 | tf_op jit(solution)/shard_map/reduce_grads/ppermute | solution.py:317
  79.3 1.6 %collective-permute-done.5 = bf16[32,72,128]{2,1,0:T(8,128)(2,1)S(1)} collective-permute-done((bf16[32,72,128]{2,1,0:T(8,128)(2,1)S(1)}, bf16[32,72,128]{2,1,0:T(8,128)(2,1)S(1)}, u32[]{:S(2)}, u32[]{:S(2)}) %collective-permute-start.5) | collective-permute-done | bytes 589856 | tf_op jit(solution)/shard_map/reduce_grads/ppermute | solution.py:317
  80.9 0.2 fusion
  81.1 22.7 %all_to_all.15 = bf16[32,72,128]{2,1,0:T(8,128)(2,1)S(1)} all-to-all(bf16[32,72,128]{2,1,0:T(8,128)(2,1)S(1)} %fusion), channel_id=1, replica_groups=mesh['vgroup'=8,'feat'=32] {'feat'}, dimensions={0} | all-to-all | bytes 1179648 | tf_op jit(solution)/shard_map/reduce_grads/all_to_all | solution.py:342
  103.8 0.1 convert_reduce_fusion
  103.9 2.6 %collective-permute-start.8 = (f32[72,128]{1,0:T(8,128)S(1)}, f32[72,128]{1,0:T(8,128)S(1)}, u32[]{:S(2)}, u32[]{:S(2)}) collective-permute-start(f32[72,128]{1,0:T(8,128)S(1)} %convert_reduce_fusion), channel_id=1, source_target_pairs={{0,192},{32,224},{64,128},{96,160},{128,64},{160,96},{192,0},{224,... | collective-permute-start | bytes 110600 | tf_op jit(solution)/shard_map/reduce_grads/ppermute | solution.py:317
  106.5 0.5 collective-permute-start.7
  107.0 0.3 collective-permute-start.6
  107.3 0.8 collective-permute-done.8
  108.0 2.8 %collective-permute-done.7 = f32[72,128]{1,0:T(8,128)S(1)} collective-permute-done((f32[72,128]{1,0:T(8,128)S(1)}, f32[72,128]{1,0:T(8,128)S(1)}, u32[]{:S(2)}, u32[]{:S(2)}) %collective-permute-start.7) | collective-permute-done | bytes 36896 | tf_op jit(solution)/shard_map/reduce_grads/ppermute | solution.py:317
  110.8 3.8 %collective-permute-start.9 = (f32[72,128]{1,0:T(8,128)S(1)}, f32[72,128]{1,0:T(8,128)S(1)}, u32[]{:S(2)}, u32[]{:S(2)}) collective-permute-start(f32[72,128]{1,0:T(8,128)S(1)} %add_add_fusion.m_ref), channel_id=1, source_target_pairs={{0,32},{32,0},{64,96},{96,64},{128,160},{160,128},{192,224},{224,1... | collective-permute-start | bytes 110600 | tf_op jit(solution)/shard_map/reduce_grads/ppermute | solution.py:317
  114.7 0.9 collective-permute-done.9.o_ref
  115.6 0.6 finish.1
  (10 shorter events, 0.1 us)
Async XLA Ops:
  2.8 39.4 %all-to-all-start = ((bf16[32,136,128]{2,1,0:T(8,128)(2,1)}), bf16[32,136,128]{2,1,0:T(8,128)(2,1)S(1)}, u32[]{:S(2)}, u32[]{:S(2)}) async-start(bf16[32,136,128]{2,1,0:T(8,128)(2,1)} %pack.1), calls=%async_computation | async-start | bytes 2228224 | tf_op jit(solution)/shard_map/send_features/all_to_all | solution.py:321
  42.2 31.5 %all-to-all-start.1 = ((bf16[32,128,128]{2,1,0:T(8,128)(2,1)}), bf16[32,128,128]{2,1,0:T(8,128)(2,1)S(1)}, u32[]{:S(2)}, u32[]{:S(2)}) async-start(bf16[32,128,128]{2,1,0:T(8,128)(2,1)} %aggregate.1), calls=%async_computation.1 | async-start | bytes 2097152 | tf_op jit(solution)/shard_map/send_aggregated/all_to_all | solution.py:326
  48.7 20.8 %copy-start.1 = (f32[256]{0:T(256)S(1)}, f32[256]{0:T(256)}, u32[]{:S(2)}) copy-start(f32[256]{0:T(256)} %param.16) | copy-start | bytes 3076
  48.7 3.7 %collective-permute-start = (bf16[32,8,128]{2,1,0:T(8,128)(2,1)S(1)}, bf16[32,8,128]{2,1,0:T(8,128)(2,1)S(1)}, u32[]{:S(2)}, u32[]{:S(2)}) collective-permute-start(bf16[32,8,128]{2,1,0:T(8,128)(2,1)S(1)} %slice.9), channel_id=1, source_target_pairs={{0,1},{1,0},{2,3},{3,2},{4,5},{5,4},{6,7},{7,6},{8,9},{9,8},{10,11... | collective-permute-start | bytes 196616 | tf_op jit(solution)/shard_map/weights_over_vgroup/ppermute | solution.py:330
  52.4 5.4 %collective-permute-start.2 = (bf16[32,16,128]{2,1,0:T(8,128)(2,1)S(1)}, bf16[32,16,128]{2,1,0:T(8,128)(2,1)S(1)}, u32[]{:S(2)}, u32[]{:S(2)}) collective-permute-start(bf16[32,16,128]{2,1,0:T(8,128)(2,1)S(1)} %get-tuple-element.25), channel_id=1, source_target_pairs={{0,128},{32,160},{64,192},{96,224},{128,0},{160,32},{192,64},{224,... | collective-permute-start | bytes 393224 | tf_op jit(solution)/shard_map/weights_over_vgroup/ppermute | solution.py:317
  55.3 4.4 %collective-permute-start.1 = (bf16[32,16,128]{2,1,0:T(8,128)(2,1)S(1)}, bf16[32,16,128]{2,1,0:T(8,128)(2,1)S(1)}, u32[]{:S(2)}, u32[]{:S(2)}) collective-permute-start(bf16[32,16,128]{2,1,0:T(8,128)(2,1)S(1)} %get-tuple-element.25), channel_id=1, source_target_pairs={{0,64},{32,96},{64,0},{96,32},{128,192},{160,224},{192,128},{224,1... | collective-permute-start | bytes 393224 | tf_op jit(solution)/shard_map/weights_over_vgroup/ppermute | solution.py:317
  55.6 5.3 %collective-permute-start.3 = (bf16[32,16,128]{2,1,0:T(8,128)(2,1)S(1)}, bf16[32,16,128]{2,1,0:T(8,128)(2,1)S(1)}, u32[]{:S(2)}, u32[]{:S(2)}) collective-permute-start(bf16[32,16,128]{2,1,0:T(8,128)(2,1)S(1)} %get-tuple-element.25), channel_id=1, source_target_pairs={{0,192},{32,224},{64,128},{96,160},{128,64},{160,96},{192,0},{224,... | collective-permute-start | bytes 393224 | tf_op jit(solution)/shard_map/weights_over_vgroup/ppermute | solution.py:317
  61.0 12.7 %copy-start = (bf16[512,256]{1,0:T(8,128)(2,1)S(1)}, bf16[512,256]{1,0:T(8,128)(2,1)}, u32[]{:S(2)}) copy-start(bf16[512,256]{1,0:T(8,128)(2,1)} %up_ref.1) | copy-start | bytes 786436
  61.0 8.5 %collective-permute-start.4 = (bf16[4,32,16,128]{3,2,1,0:T(8,128)(2,1)S(1)}, bf16[4,32,16,128]{3,2,1,0:T(8,128)(2,1)S(1)}, u32[]{:S(2)}, u32[]{:S(2)}) collective-permute-start(bf16[4,32,16,128]{3,2,1,0:T(8,128)(2,1)S(1)} %pad_maximum_fusion.w0), channel_id=1, source_target_pairs={{0,32},{32,0},{64,96},{96,64},{128,160},{160,128},{192,224},{224,1... | collective-permute-start | bytes 1572872 | tf_op jit(solution)/shard_map/weights_over_vgroup/ppermute | solution.py:317
  75.2 5.7 %collective-permute-start.5 = (bf16[32,72,128]{2,1,0:T(8,128)(2,1)S(1)}, bf16[32,72,128]{2,1,0:T(8,128)(2,1)S(1)}, u32[]{:S(2)}, u32[]{:S(2)}) collective-permute-start(bf16[32,72,128]{2,1,0:T(8,128)(2,1)S(1)} %slice_bitcast_fusion), channel_id=1, source_target_pairs={{0,32},{32,0},{64,96},{96,64},{128,160},{160,128},{192,224},{224,1... | collective-permute-start | bytes 1769480 | tf_op jit(solution)/shard_map/reduce_grads/ppermute | solution.py:317
  103.9 4.1 %collective-permute-start.8 = (f32[72,128]{1,0:T(8,128)S(1)}, f32[72,128]{1,0:T(8,128)S(1)}, u32[]{:S(2)}, u32[]{:S(2)}) collective-permute-start(f32[72,128]{1,0:T(8,128)S(1)} %convert_reduce_fusion), channel_id=1, source_target_pairs={{0,192},{32,224},{64,128},{96,160},{128,64},{160,96},{192,0},{224,... | collective-permute-start | bytes 110600 | tf_op jit(solution)/shard_map/reduce_grads/ppermute | solution.py:317
  106.5 4.3 %collective-permute-start.7 = (f32[72,128]{1,0:T(8,128)S(1)}, f32[72,128]{1,0:T(8,128)S(1)}, u32[]{:S(2)}, u32[]{:S(2)}) collective-permute-start(f32[72,128]{1,0:T(8,128)S(1)} %convert_reduce_fusion), channel_id=1, source_target_pairs={{0,128},{32,160},{64,192},{96,224},{128,0},{160,32},{192,64},{224,... | collective-permute-start | bytes 110600 | tf_op jit(solution)/shard_map/reduce_grads/ppermute | solution.py:317
  107.0 3.8 %collective-permute-start.6 = (f32[72,128]{1,0:T(8,128)S(1)}, f32[72,128]{1,0:T(8,128)S(1)}, u32[]{:S(2)}, u32[]{:S(2)}) collective-permute-start(f32[72,128]{1,0:T(8,128)S(1)} %convert_reduce_fusion), channel_id=1, source_target_pairs={{0,64},{32,96},{64,0},{96,32},{128,192},{160,224},{192,128},{224,1... | collective-permute-start | bytes 110600 | tf_op jit(solution)/shard_map/reduce_grads/ppermute | solution.py:317
  110.8 4.7 %collective-permute-start.9 = (f32[72,128]{1,0:T(8,128)S(1)}, f32[72,128]{1,0:T(8,128)S(1)}, u32[]{:S(2)}, u32[]{:S(2)}) collective-permute-start(f32[72,128]{1,0:T(8,128)S(1)} %add_add_fusion.m_ref), channel_id=1, source_target_pairs={{0,32},{32,0},{64,96},{96,64},{128,160},{160,128},{192,224},{224,1... | collective-permute-start | bytes 110600 | tf_op jit(solution)/shard_map/reduce_grads/ppermute | solution.py:317

commit v5 on v4

--- a/solution.py
+++ b/solution.py
@@ -341,7 +341,7 @@
         pair = (grads[0].astype(F32) + got.astype(F32)).astype(BF16)
         arrived = lax.all_to_all(pair, "feat", 0, 0, tiled=True)
         total = jnp.sum(arrived.astype(F32), axis=0)
-        total = sum(direct(total, (2, 4, 6)), total)
+        total = sum(direct(total, (2, 6, 4)), total)
         [other] = direct(total, (1,))
         grad_self, grad_neigh, grad_bias = finish(place, total, other, fcols)
     return (hidden, grad_self, grad_neigh, grad_bias[0])

time: 117 us -> 117 us (level)
  Pallas kernels: 23.1 us -> 18.7 us
  waiting for transfers between devices: 26.8 us -> 31 us
    all_to_all x1, waiting for transfers between devices: 8.56 us -> 12.9 us  [body(): x_rows = lax.all_to_all(outgoing, 'feat', 0, 0, tiled=True)]
    pallas_call x1, Pallas kernels: 18.1 us -> 13.8 us  [aggregate(): pl.pallas_call(kernel, in_specs=[pl.BlockSpec(memory_space=pltpu.SMEM)] *...]
  transfers between devices with their start and end apart: 12 -> 12, of which waited for: 11 -> 11; matrix products, arithmetic and copies ran while one was open for 0% -> 0% of each run, Pallas kernels for 16% -> 12%
where the time goes in v5:
time: 117 us; the launch traced here: 116 us
  starting transfers between devices  41.9 us (36%)
  waiting for transfers between devices  31 us (26%)
  blocking collectives  22.7 us (19%)
  Pallas kernels  18.7 us (16%)
  between operations  1.38 us (1%)
    all_to_all x1, blocking collectives, body(): arrived = lax.all_to_all(pair, 'feat', 0, 0, tiled=True)  22.7 us
    ppermute x9, starting transfers between devices, direct(): lax.ppermute(value, 'vgroup', [(a, a ^ bit) for a in range(nv)])  22 us
    pallas_call x1, Pallas kernels, aggregate(): pl.pallas_call(kernel, in_specs=[pl.BlockSpec(memory_space=pltpu.SMEM)] *...  13.8 us
    all_to_all x1, waiting for transfers between devices, body(): x_rows = lax.all_to_all(outgoing, 'feat', 0, 0, tiled=True)  12.9 us
    ppermute x9, waiting for transfers between devices, direct(): lax.ppermute(value, 'vgroup', [(a, a ^ bit) for a in range(nv)])  12.3 us
    all_to_all x1, starting transfers between devices, body(): x_rows = lax.all_to_all(outgoing, 'feat', 0, 0, tiled=True)  12 us
    all_to_all x1, starting transfers between devices, body(): a_rows = lax.all_to_all(agg, 'feat', 0, 0, tiled=True)  6.48 us
    all_to_all x1, waiting for transfers between devices, body(): a_rows = lax.all_to_all(agg, 'feat', 0, 0, tiled=True)  3.49 us
  transfers between devices with their start and end apart: 12, of which 11 were waited for; matrix products, arithmetic and copies ran while one was open for 0% of the time, Pallas kernels for 12%

profile of v5, /device:TPU:1, one launch (start us, length us, event | category | flops | bytes accessed | tf_op | source)
XLA Modules:
  0.0 116.2 jit_solution(10272009017417157601)
XLA Ops:
  0.6 2.1 %pack.1 = bf16[32,136,128]{2,1,0:T(8,128)(2,1)} custom-call(s32[1]{0:T(128)} %bitcast.at, bf16[32,32768]{1,0:T(8,128)(2,1)} %bitcast.19, bf16[32,256]{1,0:T(8,128)(2,1)} %ws_hbm.1, bf16[32,256]{1,0:T(8,128)(2,1)} %wn_hbm.1), custom_call_target="tpu_custom_call" | custom-call | bytes 3145728 | tf_op jit(solution)/shard_map/send_features/pack/pallas_call | solution.py:162
  2.8 12.0 %all-to-all-start = ((bf16[32,136,128]{2,1,0:T(8,128)(2,1)}), bf16[32,136,128]{2,1,0:T(8,128)(2,1)S(1)}, u32[]{:S(2)}, u32[]{:S(2)}) async-start(bf16[32,136,128]{2,1,0:T(8,128)(2,1)} %pack.1), calls=%async_computation | async-start | bytes 2228224 | tf_op jit(solution)/shard_map/send_features/all_to_all | solution.py:321
  15.5 13.8 %aggregate.1 = bf16[32,128,128]{2,1,0:T(8,128)(2,1)} custom-call(s32[1024]{0:T(1024)} %bitcast.24, s32[1024]{0:T(1024)} %bitcast.25, s32[1]{0:T(128)S(6)} %copy.13.cnt, bf16[32,32768]{1,0:T(8,128)(2,1)} %bitcast.20, bf16[1024,128,128]{2,1,0:T(8,128)(2,1)} %bitcast.18), custom_call_target="tpu_custom_call" | custom-call | flops 1073741824 | bytes 35651584 | tf_op jit(solution)/shard_map/aggregate/pallas_call | solution.py:85
  29.3 12.9 %all-to-all-done.x_ref = bf16[32,136,128]{2,1,0:T(8,128)(2,1)S(1)} async-done(((bf16[32,136,128]{2,1,0:T(8,128)(2,1)}), bf16[32,136,128]{2,1,0:T(8,128)(2,1)S(1)}, u32[]{:S(2)}, u32[]{:S(2)}) %all-to-all-start) | async-done | bytes 1114144 | tf_op jit(solution)/shard_map/send_features/all_to_all | solution.py:321
  42.2 6.5 %all-to-all-start.1 = ((bf16[32,128,128]{2,1,0:T(8,128)(2,1)}), bf16[32,128,128]{2,1,0:T(8,128)(2,1)S(1)}, u32[]{:S(2)}, u32[]{:S(2)}) async-start(bf16[32,128,128]{2,1,0:T(8,128)(2,1)} %aggregate.1), calls=%async_computation.1 | async-start | bytes 2097152 | tf_op jit(solution)/shard_map/send_aggregated/all_to_all | solution.py:326
  48.7 0.0 copy-start.1
  48.7 1.3 %collective-permute-start = (bf16[32,8,128]{2,1,0:T(8,128)(2,1)S(1)}, bf16[32,8,128]{2,1,0:T(8,128)(2,1)S(1)}, u32[]{:S(2)}, u32[]{:S(2)}) collective-permute-start(bf16[32,8,128]{2,1,0:T(8,128)(2,1)S(1)} %slice.9), channel_id=1, source_target_pairs={{0,1},{1,0},{2,3},{3,2},{4,5},{5,4},{6,7},{7,6},{8,9},{9,8},{10,11... | collective-permute-start | bytes 196616 | tf_op jit(solution)/shard_map/weights_over_vgroup/ppermute | solution.py:330
  50.0 2.3 %collective-permute-done = bf16[32,8,128]{2,1,0:T(8,128)(2,1)S(1)} collective-permute-done((bf16[32,8,128]{2,1,0:T(8,128)(2,1)S(1)}, bf16[32,8,128]{2,1,0:T(8,128)(2,1)S(1)}, u32[]{:S(2)}, u32[]{:S(2)}) %collective-permute-start) | collective-permute-done | bytes 65568 | tf_op jit(solution)/shard_map/weights_over_vgroup/ppermute | solution.py:330
  52.4 2.8 %collective-permute-start.2 = (bf16[32,16,128]{2,1,0:T(8,128)(2,1)S(1)}, bf16[32,16,128]{2,1,0:T(8,128)(2,1)S(1)}, u32[]{:S(2)}, u32[]{:S(2)}) collective-permute-start(bf16[32,16,128]{2,1,0:T(8,128)(2,1)S(1)} %get-tuple-element.25), channel_id=1, source_target_pairs={{0,128},{32,160},{64,192},{96,224},{128,0},{160,32},{192,64},{224,... | collective-permute-start | bytes 393224 | tf_op jit(solution)/shard_map/weights_over_vgroup/ppermute | solution.py:317
  55.3 0.3 collective-permute-start.1
  55.6 0.6 collective-permute-start.3
  56.1 1.7 %collective-permute-done.2 = bf16[32,16,128]{2,1,0:T(8,128)(2,1)S(1)} collective-permute-done((bf16[32,16,128]{2,1,0:T(8,128)(2,1)S(1)}, bf16[32,16,128]{2,1,0:T(8,128)(2,1)S(1)}, u32[]{:S(2)}, u32[]{:S(2)}) %collective-permute-start.2) | collective-permute-done | bytes 131104 | tf_op jit(solution)/shard_map/weights_over_vgroup/ppermute | solution.py:317
  57.8 1.8 %collective-permute-done.1 = bf16[32,16,128]{2,1,0:T(8,128)(2,1)S(1)} collective-permute-done((bf16[32,16,128]{2,1,0:T(8,128)(2,1)S(1)}, bf16[32,16,128]{2,1,0:T(8,128)(2,1)S(1)}, u32[]{:S(2)}, u32[]{:S(2)}) %collective-permute-start.1) | collective-permute-done | bytes 131104 | tf_op jit(solution)/shard_map/weights_over_vgroup/ppermute | solution.py:317
  59.6 1.3 %collective-permute-done.3 = bf16[32,16,128]{2,1,0:T(8,128)(2,1)S(1)} collective-permute-done((bf16[32,16,128]{2,1,0:T(8,128)(2,1)S(1)}, bf16[32,16,128]{2,1,0:T(8,128)(2,1)S(1)}, u32[]{:S(2)}, u32[]{:S(2)}) %collective-permute-start.3) | collective-permute-done | bytes 131104 | tf_op jit(solution)/shard_map/weights_over_vgroup/ppermute | solution.py:317
  60.9 0.1 pad_maximum_fusion.w0
  61.0 7.0 %collective-permute-start.4 = (bf16[4,32,16,128]{3,2,1,0:T(8,128)(2,1)S(1)}, bf16[4,32,16,128]{3,2,1,0:T(8,128)(2,1)S(1)}, u32[]{:S(2)}, u32[]{:S(2)}) collective-permute-start(bf16[4,32,16,128]{3,2,1,0:T(8,128)(2,1)S(1)} %pad_maximum_fusion.w0), channel_id=1, source_target_pairs={{0,32},{32,0},{64,96},{96,64},{128,160},{160,128},{192,224},{224,1... | collective-permute-start | bytes 1572872 | tf_op jit(solution)/shard_map/weights_over_vgroup/ppermute | solution.py:317
  68.0 1.5 %collective-permute-done.4.w1 = bf16[4,32,16,128]{3,2,1,0:T(8,128)(2,1)S(1)} collective-permute-done((bf16[4,32,16,128]{3,2,1,0:T(8,128)(2,1)S(1)}, bf16[4,32,16,128]{3,2,1,0:T(8,128)(2,1)S(1)}, u32[]{:S(2)}, u32[]{:S(2)}) %collective-permute-start.4) | collective-permute-done | bytes 524320 | tf_op jit(solution)/shard_map/weights_over_vgroup/ppermute | solution.py:317
  69.5 0.7 own_part.1
  70.2 3.5 %all-to-all-done.1.a_ref = bf16[32,128,128]{2,1,0:T(8,128)(2,1)S(1)} async-done(((bf16[32,128,128]{2,1,0:T(8,128)(2,1)}), bf16[32,128,128]{2,1,0:T(8,128)(2,1)S(1)}, u32[]{:S(2)}, u32[]{:S(2)}) %all-to-all-start.1) | async-done | bytes 1048608 | tf_op jit(solution)/shard_map/send_aggregated/all_to_all | solution.py:326
  73.7 1.5 %layer.1 = (bf16[512,256]{1,0:T(8,128)(2,1)}, bf16[2,32,72,128]{3,2,1,0:T(8,128)(2,1)S(1)}) custom-call(s32[1]{0:T(128)} %bitcast.at, f32[4,128,256]{2,1,0:T(8,128)S(1)} %get-tuple-element.14.pre, bf16[32,128,128]{2,1,0:T(8,128)(2,1)S(1)} %all-to-all-done.1.a_ref, bf16[1024,256]{1,0:T(8,128)(2,1)S(1)} %get-tuple-element.16.wn, ...), custom_call_target="tpu_custom_call" | custom-call | flops 805306368 | bytes 6291456 | tf_op jit(solution)/shard_map/layer/pallas_call | solution.py:261
  75.2 4.1 %collective-permute-start.5 = (bf16[32,72,128]{2,1,0:T(8,128)(2,1)S(1)}, bf16[32,72,128]{2,1,0:T(8,128)(2,1)S(1)}, u32[]{:S(2)}, u32[]{:S(2)}) collective-permute-start(bf16[32,72,128]{2,1,0:T(8,128)(2,1)S(1)} %slice_bitcast_fusion), channel_id=1, source_target_pairs={{0,32},{32,0},{64,96},{96,64},{128,160},{160,128},{192,224},{224,1... | collective-permute-start | bytes 1769480 | tf_op jit(solution)/shard_map/reduce_grads/ppermute | solution.py:317
  79.3 1.6 %collective-permute-done.5 = bf16[32,72,128]{2,1,0:T(8,128)(2,1)S(1)} collective-permute-done((bf16[32,72,128]{2,1,0:T(8,128)(2,1)S(1)}, bf16[32,72,128]{2,1,0:T(8,128)(2,1)S(1)}, u32[]{:S(2)}, u32[]{:S(2)}) %collective-permute-start.5) | collective-permute-done | bytes 589856 | tf_op jit(solution)/shard_map/reduce_grads/ppermute | solution.py:317
  80.9 0.2 fusion
  81.1 22.7 %all_to_all.15 = bf16[32,72,128]{2,1,0:T(8,128)(2,1)S(1)} all-to-all(bf16[32,72,128]{2,1,0:T(8,128)(2,1)S(1)} %fusion), channel_id=1, replica_groups=mesh['vgroup'=8,'feat'=32] {'feat'}, dimensions={0} | all-to-all | bytes 1179648 | tf_op jit(solution)/shard_map/reduce_grads/all_to_all | solution.py:342
  103.8 0.1 convert_reduce_fusion
  103.9 2.8 %collective-permute-start.8 = (f32[72,128]{1,0:T(8,128)S(1)}, f32[72,128]{1,0:T(8,128)S(1)}, u32[]{:S(2)}, u32[]{:S(2)}) collective-permute-start(f32[72,128]{1,0:T(8,128)S(1)} %convert_reduce_fusion), channel_id=1, source_target_pairs={{0,128},{32,160},{64,192},{96,224},{128,0},{160,32},{192,64},{224,... | collective-permute-start | bytes 110600 | tf_op jit(solution)/shard_map/reduce_grads/ppermute | solution.py:317
  106.7 0.9 collective-permute-start.7
  107.6 0.7 collective-permute-done.8
  108.3 2.8 %collective-permute-done.7 = f32[72,128]{1,0:T(8,128)S(1)} collective-permute-done((f32[72,128]{1,0:T(8,128)S(1)}, f32[72,128]{1,0:T(8,128)S(1)}, u32[]{:S(2)}, u32[]{:S(2)}) %collective-permute-start.7) | collective-permute-done | bytes 36896 | tf_op jit(solution)/shard_map/reduce_grads/ppermute | solution.py:317
  111.1 3.6 %collective-permute-start.9 = (f32[72,128]{1,0:T(8,128)S(1)}, f32[72,128]{1,0:T(8,128)S(1)}, u32[]{:S(2)}, u32[]{:S(2)}) collective-permute-start(f32[72,128]{1,0:T(8,128)S(1)} %add_add_fusion.m_ref), channel_id=1, source_target_pairs={{0,32},{32,0},{64,96},{96,64},{128,160},{160,128},{192,224},{224,1... | collective-permute-start | bytes 110600 | tf_op jit(solution)/shard_map/reduce_grads/ppermute | solution.py:317
  114.7 0.9 collective-permute-done.9.o_ref
  115.5 0.6 finish.1
  (10 shorter events, 0.1 us)
Async XLA Ops:
  2.8 39.4 %all-to-all-start = ((bf16[32,136,128]{2,1,0:T(8,128)(2,1)}), bf16[32,136,128]{2,1,0:T(8,128)(2,1)S(1)}, u32[]{:S(2)}, u32[]{:S(2)}) async-start(bf16[32,136,128]{2,1,0:T(8,128)(2,1)} %pack.1), calls=%async_computation | async-start | bytes 2228224 | tf_op jit(solution)/shard_map/send_features/all_to_all | solution.py:321
  42.2 31.5 %all-to-all-start.1 = ((bf16[32,128,128]{2,1,0:T(8,128)(2,1)}), bf16[32,128,128]{2,1,0:T(8,128)(2,1)S(1)}, u32[]{:S(2)}, u32[]{:S(2)}) async-start(bf16[32,128,128]{2,1,0:T(8,128)(2,1)} %aggregate.1), calls=%async_computation.1 | async-start | bytes 2097152 | tf_op jit(solution)/shard_map/send_aggregated/all_to_all | solution.py:326
  48.7 20.8 %copy-start.1 = (f32[256]{0:T(256)S(1)}, f32[256]{0:T(256)}, u32[]{:S(2)}) copy-start(f32[256]{0:T(256)} %param.16) | copy-start | bytes 3076
  48.7 3.7 %collective-permute-start = (bf16[32,8,128]{2,1,0:T(8,128)(2,1)S(1)}, bf16[32,8,128]{2,1,0:T(8,128)(2,1)S(1)}, u32[]{:S(2)}, u32[]{:S(2)}) collective-permute-start(bf16[32,8,128]{2,1,0:T(8,128)(2,1)S(1)} %slice.9), channel_id=1, source_target_pairs={{0,1},{1,0},{2,3},{3,2},{4,5},{5,4},{6,7},{7,6},{8,9},{9,8},{10,11... | collective-permute-start | bytes 196616 | tf_op jit(solution)/shard_map/weights_over_vgroup/ppermute | solution.py:330
  52.4 5.4 %collective-permute-start.2 = (bf16[32,16,128]{2,1,0:T(8,128)(2,1)S(1)}, bf16[32,16,128]{2,1,0:T(8,128)(2,1)S(1)}, u32[]{:S(2)}, u32[]{:S(2)}) collective-permute-start(bf16[32,16,128]{2,1,0:T(8,128)(2,1)S(1)} %get-tuple-element.25), channel_id=1, source_target_pairs={{0,128},{32,160},{64,192},{96,224},{128,0},{160,32},{192,64},{224,... | collective-permute-start | bytes 393224 | tf_op jit(solution)/shard_map/weights_over_vgroup/ppermute | solution.py:317
  55.3 4.4 %collective-permute-start.1 = (bf16[32,16,128]{2,1,0:T(8,128)(2,1)S(1)}, bf16[32,16,128]{2,1,0:T(8,128)(2,1)S(1)}, u32[]{:S(2)}, u32[]{:S(2)}) collective-permute-start(bf16[32,16,128]{2,1,0:T(8,128)(2,1)S(1)} %get-tuple-element.25), channel_id=1, source_target_pairs={{0,64},{32,96},{64,0},{96,32},{128,192},{160,224},{192,128},{224,1... | collective-permute-start | bytes 393224 | tf_op jit(solution)/shard_map/weights_over_vgroup/ppermute | solution.py:317
  55.6 5.3 %collective-permute-start.3 = (bf16[32,16,128]{2,1,0:T(8,128)(2,1)S(1)}, bf16[32,16,128]{2,1,0:T(8,128)(2,1)S(1)}, u32[]{:S(2)}, u32[]{:S(2)}) collective-permute-start(bf16[32,16,128]{2,1,0:T(8,128)(2,1)S(1)} %get-tuple-element.25), channel_id=1, source_target_pairs={{0,192},{32,224},{64,128},{96,160},{128,64},{160,96},{192,0},{224,... | collective-permute-start | bytes 393224 | tf_op jit(solution)/shard_map/weights_over_vgroup/ppermute | solution.py:317
  61.0 12.7 %copy-start = (bf16[512,256]{1,0:T(8,128)(2,1)S(1)}, bf16[512,256]{1,0:T(8,128)(2,1)}, u32[]{:S(2)}) copy-start(bf16[512,256]{1,0:T(8,128)(2,1)} %up_ref.1) | copy-start | bytes 786436
  61.0 8.5 %collective-permute-start.4 = (bf16[4,32,16,128]{3,2,1,0:T(8,128)(2,1)S(1)}, bf16[4,32,16,128]{3,2,1,0:T(8,128)(2,1)S(1)}, u32[]{:S(2)}, u32[]{:S(2)}) collective-permute-start(bf16[4,32,16,128]{3,2,1,0:T(8,128)(2,1)S(1)} %pad_maximum_fusion.w0), channel_id=1, source_target_pairs={{0,32},{32,0},{64,96},{96,64},{128,160},{160,128},{192,224},{224,1... | collective-permute-start | bytes 1572872 | tf_op jit(solution)/shard_map/weights_over_vgroup/ppermute | solution.py:317
  75.2 5.7 %collective-permute-start.5 = (bf16[32,72,128]{2,1,0:T(8,128)(2,1)S(1)}, bf16[32,72,128]{2,1,0:T(8,128)(2,1)S(1)}, u32[]{:S(2)}, u32[]{:S(2)}) collective-permute-start(bf16[32,72,128]{2,1,0:T(8,128)(2,1)S(1)} %slice_bitcast_fusion), channel_id=1, source_target_pairs={{0,32},{32,0},{64,96},{96,64},{128,160},{160,128},{192,224},{224,1... | collective-permute-start | bytes 1769480 | tf_op jit(solution)/shard_map/reduce_grads/ppermute | solution.py:317
  103.9 4.4 %collective-permute-start.8 = (f32[72,128]{1,0:T(8,128)S(1)}, f32[72,128]{1,0:T(8,128)S(1)}, u32[]{:S(2)}, u32[]{:S(2)}) collective-permute-start(f32[72,128]{1,0:T(8,128)S(1)} %convert_reduce_fusion), channel_id=1, source_target_pairs={{0,128},{32,160},{64,192},{96,224},{128,0},{160,32},{192,64},{224,... | collective-permute-start | bytes 110600 | tf_op jit(solution)/shard_map/reduce_grads/ppermute | solution.py:317
  106.7 4.3 %collective-permute-start.7 = (f32[72,128]{1,0:T(8,128)S(1)}, f32[72,128]{1,0:T(8,128)S(1)}, u32[]{:S(2)}, u32[]{:S(2)}) collective-permute-start(f32[72,128]{1,0:T(8,128)S(1)} %convert_reduce_fusion), channel_id=1, source_target_pairs={{0,192},{32,224},{64,128},{96,160},{128,64},{160,96},{192,0},{224,... | collective-permute-start | bytes 110600 | tf_op jit(solution)/shard_map/reduce_grads/ppermute | solution.py:317
  107.6 3.5 %collective-permute-start.6 = (f32[72,128]{1,0:T(8,128)S(1)}, f32[72,128]{1,0:T(8,128)S(1)}, u32[]{:S(2)}, u32[]{:S(2)}) collective-permute-start(f32[72,128]{1,0:T(8,128)S(1)} %convert_reduce_fusion), channel_id=1, source_target_pairs={{0,64},{32,96},{64,0},{96,32},{128,192},{160,224},{192,128},{224,1... | collective-permute-start | bytes 110600 | tf_op jit(solution)/shard_map/reduce_grads/ppermute | solution.py:317
  111.1 4.4 %collective-permute-start.9 = (f32[72,128]{1,0:T(8,128)S(1)}, f32[72,128]{1,0:T(8,128)S(1)}, u32[]{:S(2)}, u32[]{:S(2)}) collective-permute-start(f32[72,128]{1,0:T(8,128)S(1)} %add_add_fusion.m_ref), channel_id=1, source_target_pairs={{0,32},{32,0},{64,96},{96,64},{128,160},{160,128},{192,224},{224,1... | collective-permute-start | bytes 110600 | tf_op jit(solution)/shard_map/reduce_grads/ppermute | solution.py:317

commit v6 on v5

--- a/solution.py
+++ b/solution.py
@@ -330,7 +330,8 @@
         other = lax.ppermute(part, "feat", [(a, a ^ 1) for a in range(nfeat)])
         even = lax.axis_index("feat") % 2 == 0
         piece = jnp.concatenate([jnp.where(even, part, other), jnp.where(even, other, part)], axis=1)
-        same_core = jnp.stack([piece] + direct(piece, (2, 4, 6)))
+        near, side, far = direct(piece, (2, 6, 4))
+        same_core = jnp.stack([piece, near, far, side])
         [other_core] = direct(same_core, (1,))
 
     pre_own, wn = own_part(place, same_core, other_core, x_rows, bias[None, :], tiles)

time: 117 us -> 117 us (level)
  Pallas kernels: 18.7 us -> 23 us
  waiting for transfers between devices: 31 us -> 26.7 us
    all_to_all x1, waiting for transfers between devices: 12.9 us -> 8.58 us  [body(): x_rows = lax.all_to_all(outgoing, 'feat', 0, 0, tiled=True)]
    pallas_call x1, Pallas kernels: 13.8 us -> 18.1 us  [aggregate(): pl.pallas_call(kernel, in_specs=[pl.BlockSpec(memory_space=pltpu.SMEM)] *...]
  transfers between devices with their start and end apart: 12 -> 12, of which waited for: 11 -> 11; matrix products, arithmetic and copies ran while one was open for 0% -> 0% of each run, Pallas kernels for 12% -> 16%
where the time goes in v6:
time: 117 us; the launch traced here: 116 us
  starting transfers between devices  41.9 us (36%)
  waiting for transfers between devices  26.7 us (23%)
  Pallas kernels  23 us (20%)
  blocking collectives  22.7 us (19%)
  between operations  1.38 us (1%)
    all_to_all x1, blocking collectives, body(): arrived = lax.all_to_all(pair, 'feat', 0, 0, tiled=True)  22.7 us
    ppermute x9, starting transfers between devices, direct(): lax.ppermute(value, 'vgroup', [(a, a ^ bit) for a in range(nv)])  22 us
    pallas_call x1, Pallas kernels, aggregate(): pl.pallas_call(kernel, in_specs=[pl.BlockSpec(memory_space=pltpu.SMEM)] *...  18.1 us
    ppermute x9, waiting for transfers between devices, direct(): lax.ppermute(value, 'vgroup', [(a, a ^ bit) for a in range(nv)])  12.3 us
    all_to_all x1, starting transfers between devices, body(): x_rows = lax.all_to_all(outgoing, 'feat', 0, 0, tiled=True)  12 us
    all_to_all x1, waiting for transfers between devices, body(): x_rows = lax.all_to_all(outgoing, 'feat', 0, 0, tiled=True)  8.58 us
    all_to_all x1, starting transfers between devices, body(): a_rows = lax.all_to_all(agg, 'feat', 0, 0, tiled=True)  6.48 us
    all_to_all x1, waiting for transfers between devices, body(): a_rows = lax.all_to_all(agg, 'feat', 0, 0, tiled=True)  3.49 us
  transfers between devices with their start and end apart: 12, of which 11 were waited for; matrix products, arithmetic and copies ran while one was open for 0% of the time, Pallas kernels for 16%

profile of v6, /device:TPU:1, one launch (start us, length us, event | category | flops | bytes accessed | tf_op | source)
XLA Modules:
  0.0 116.2 jit_solution(10272009017417157601)
XLA Ops:
  0.6 2.1 %pack.1 = bf16[32,136,128]{2,1,0:T(8,128)(2,1)} custom-call(s32[1]{0:T(128)} %bitcast.at, bf16[32,32768]{1,0:T(8,128)(2,1)} %bitcast.19, bf16[32,256]{1,0:T(8,128)(2,1)} %ws_hbm.1, bf16[32,256]{1,0:T(8,128)(2,1)} %wn_hbm.1), custom_call_target="tpu_custom_call" | custom-call | bytes 3145728 | tf_op jit(solution)/shard_map/send_features/pack/pallas_call | solution.py:162
  2.8 12.0 %all-to-all-start = ((bf16[32,136,128]{2,1,0:T(8,128)(2,1)}), bf16[32,136,128]{2,1,0:T(8,128)(2,1)S(1)}, u32[]{:S(2)}, u32[]{:S(2)}) async-start(bf16[32,136,128]{2,1,0:T(8,128)(2,1)} %pack.1), calls=%async_computation | async-start | bytes 2228224 | tf_op jit(solution)/shard_map/send_features/all_to_all | solution.py:321
  15.5 18.1 %aggregate.1 = bf16[32,128,128]{2,1,0:T(8,128)(2,1)} custom-call(s32[1024]{0:T(1024)} %bitcast.24, s32[1024]{0:T(1024)} %bitcast.25, s32[1]{0:T(128)S(6)} %copy.13.cnt, bf16[32,32768]{1,0:T(8,128)(2,1)} %bitcast.20, bf16[1024,128,128]{2,1,0:T(8,128)(2,1)} %bitcast.18), custom_call_target="tpu_custom_call" | custom-call | flops 1073741824 | bytes 35651584 | tf_op jit(solution)/shard_map/aggregate/pallas_call | solution.py:85
  33.6 8.6 %all-to-all-done.x_ref = bf16[32,136,128]{2,1,0:T(8,128)(2,1)S(1)} async-done(((bf16[32,136,128]{2,1,0:T(8,128)(2,1)}), bf16[32,136,128]{2,1,0:T(8,128)(2,1)S(1)}, u32[]{:S(2)}, u32[]{:S(2)}) %all-to-all-start) | async-done | bytes 1114144 | tf_op jit(solution)/shard_map/send_features/all_to_all | solution.py:321
  42.2 6.5 %all-to-all-start.1 = ((bf16[32,128,128]{2,1,0:T(8,128)(2,1)}), bf16[32,128,128]{2,1,0:T(8,128)(2,1)S(1)}, u32[]{:S(2)}, u32[]{:S(2)}) async-start(bf16[32,128,128]{2,1,0:T(8,128)(2,1)} %aggregate.1), calls=%async_computation.1 | async-start | bytes 2097152 | tf_op jit(solution)/shard_map/send_aggregated/all_to_all | solution.py:326
  48.7 0.0 copy-start.1
  48.7 1.3 %collective-permute-start = (bf16[32,8,128]{2,1,0:T(8,128)(2,1)S(1)}, bf16[32,8,128]{2,1,0:T(8,128)(2,1)S(1)}, u32[]{:S(2)}, u32[]{:S(2)}) collective-permute-start(bf16[32,8,128]{2,1,0:T(8,128)(2,1)S(1)} %slice.9), channel_id=1, source_target_pairs={{0,1},{1,0},{2,3},{3,2},{4,5},{5,4},{6,7},{7,6},{8,9},{9,8},{10,11... | collective-permute-start | bytes 196616 | tf_op jit(solution)/shard_map/weights_over_vgroup/ppermute | solution.py:330
  50.0 2.3 %collective-permute-done = bf16[32,8,128]{2,1,0:T(8,128)(2,1)S(1)} collective-permute-done((bf16[32,8,128]{2,1,0:T(8,128)(2,1)S(1)}, bf16[32,8,128]{2,1,0:T(8,128)(2,1)S(1)}, u32[]{:S(2)}, u32[]{:S(2)}) %collective-permute-start) | collective-permute-done | bytes 65568 | tf_op jit(solution)/shard_map/weights_over_vgroup/ppermute | solution.py:330
  52.4 2.8 %collective-permute-start.2 = (bf16[32,16,128]{2,1,0:T(8,128)(2,1)S(1)}, bf16[32,16,128]{2,1,0:T(8,128)(2,1)S(1)}, u32[]{:S(2)}, u32[]{:S(2)}) collective-permute-start(bf16[32,16,128]{2,1,0:T(8,128)(2,1)S(1)} %get-tuple-element.25), channel_id=1, source_target_pairs={{0,128},{32,160},{64,192},{96,224},{128,0},{160,32},{192,64},{224,... | collective-permute-start | bytes 393224 | tf_op jit(solution)/shard_map/weights_over_vgroup/ppermute | solution.py:317
  55.3 0.3 collective-permute-start.1
  55.6 0.6 collective-permute-start.3
  56.1 1.7 %collective-permute-done.2 = bf16[32,16,128]{2,1,0:T(8,128)(2,1)S(1)} collective-permute-done((bf16[32,16,128]{2,1,0:T(8,128)(2,1)S(1)}, bf16[32,16,128]{2,1,0:T(8,128)(2,1)S(1)}, u32[]{:S(2)}, u32[]{:S(2)}) %collective-permute-start.2) | collective-permute-done | bytes 131104 | tf_op jit(solution)/shard_map/weights_over_vgroup/ppermute | solution.py:317
  57.8 1.8 %collective-permute-done.1 = bf16[32,16,128]{2,1,0:T(8,128)(2,1)S(1)} collective-permute-done((bf16[32,16,128]{2,1,0:T(8,128)(2,1)S(1)}, bf16[32,16,128]{2,1,0:T(8,128)(2,1)S(1)}, u32[]{:S(2)}, u32[]{:S(2)}) %collective-permute-start.1) | collective-permute-done | bytes 131104 | tf_op jit(solution)/shard_map/weights_over_vgroup/ppermute | solution.py:317
  59.6 1.3 %collective-permute-done.3 = bf16[32,16,128]{2,1,0:T(8,128)(2,1)S(1)} collective-permute-done((bf16[32,16,128]{2,1,0:T(8,128)(2,1)S(1)}, bf16[32,16,128]{2,1,0:T(8,128)(2,1)S(1)}, u32[]{:S(2)}, u32[]{:S(2)}) %collective-permute-start.3) | collective-permute-done | bytes 131104 | tf_op jit(solution)/shard_map/weights_over_vgroup/ppermute | solution.py:317
  60.9 0.1 pad_maximum_fusion.w0
  61.0 7.0 %collective-permute-start.4 = (bf16[4,32,16,128]{3,2,1,0:T(8,128)(2,1)S(1)}, bf16[4,32,16,128]{3,2,1,0:T(8,128)(2,1)S(1)}, u32[]{:S(2)}, u32[]{:S(2)}) collective-permute-start(bf16[4,32,16,128]{3,2,1,0:T(8,128)(2,1)S(1)} %pad_maximum_fusion.w0), channel_id=1, source_target_pairs={{0,32},{32,0},{64,96},{96,64},{128,160},{160,128},{192,224},{224,1... | collective-permute-start | bytes 1572872 | tf_op jit(solution)/shard_map/weights_over_vgroup/ppermute | solution.py:317
  68.0 1.5 %collective-permute-done.4.w1 = bf16[4,32,16,128]{3,2,1,0:T(8,128)(2,1)S(1)} collective-permute-done((bf16[4,32,16,128]{3,2,1,0:T(8,128)(2,1)S(1)}, bf16[4,32,16,128]{3,2,1,0:T(8,128)(2,1)S(1)}, u32[]{:S(2)}, u32[]{:S(2)}) %collective-permute-start.4) | collective-permute-done | bytes 524320 | tf_op jit(solution)/shard_map/weights_over_vgroup/ppermute | solution.py:317
  69.5 0.7 own_part.1
  70.2 3.5 %all-to-all-done.1.a_ref = bf16[32,128,128]{2,1,0:T(8,128)(2,1)S(1)} async-done(((bf16[32,128,128]{2,1,0:T(8,128)(2,1)}), bf16[32,128,128]{2,1,0:T(8,128)(2,1)S(1)}, u32[]{:S(2)}, u32[]{:S(2)}) %all-to-all-start.1) | async-done | bytes 1048608 | tf_op jit(solution)/shard_map/send_aggregated/all_to_all | solution.py:326
  73.7 1.5 %layer.1 = (bf16[512,256]{1,0:T(8,128)(2,1)}, bf16[2,32,72,128]{3,2,1,0:T(8,128)(2,1)S(1)}) custom-call(s32[1]{0:T(128)} %bitcast.at, f32[4,128,256]{2,1,0:T(8,128)S(1)} %get-tuple-element.14.pre, bf16[32,128,128]{2,1,0:T(8,128)(2,1)S(1)} %all-to-all-done.1.a_ref, bf16[1024,256]{1,0:T(8,128)(2,1)S(1)} %get-tuple-element.16.wn, ...), custom_call_target="tpu_custom_call" | custom-call | flops 805306368 | bytes 6291456 | tf_op jit(solution)/shard_map/layer/pallas_call | solution.py:261
  75.2 4.1 %collective-permute-start.5 = (bf16[32,72,128]{2,1,0:T(8,128)(2,1)S(1)}, bf16[32,72,128]{2,1,0:T(8,128)(2,1)S(1)}, u32[]{:S(2)}, u32[]{:S(2)}) collective-permute-start(bf16[32,72,128]{2,1,0:T(8,128)(2,1)S(1)} %slice_bitcast_fusion), channel_id=1, source_target_pairs={{0,32},{32,0},{64,96},{96,64},{128,160},{160,128},{192,224},{224,1... | collective-permute-start | bytes 1769480 | tf_op jit(solution)/shard_map/reduce_grads/ppermute | solution.py:317
  79.3 1.6 %collective-permute-done.5 = bf16[32,72,128]{2,1,0:T(8,128)(2,1)S(1)} collective-permute-done((bf16[32,72,128]{2,1,0:T(8,128)(2,1)S(1)}, bf16[32,72,128]{2,1,0:T(8,128)(2,1)S(1)}, u32[]{:S(2)}, u32[]{:S(2)}) %collective-permute-start.5) | collective-permute-done | bytes 589856 | tf_op jit(solution)/shard_map/reduce_grads/ppermute | solution.py:317
  80.9 0.2 fusion
  81.1 22.7 %all_to_all.15 = bf16[32,72,128]{2,1,0:T(8,128)(2,1)S(1)} all-to-all(bf16[32,72,128]{2,1,0:T(8,128)(2,1)S(1)} %fusion), channel_id=1, replica_groups=mesh['vgroup'=8,'feat'=32] {'feat'}, dimensions={0} | all-to-all | bytes 1179648 | tf_op jit(solution)/shard_map/reduce_grads/all_to_all | solution.py:343
  103.8 0.1 convert_reduce_fusion
  103.9 2.8 %collective-permute-start.8 = (f32[72,128]{1,0:T(8,128)S(1)}, f32[72,128]{1,0:T(8,128)S(1)}, u32[]{:S(2)}, u32[]{:S(2)}) collective-permute-start(f32[72,128]{1,0:T(8,128)S(1)} %convert_reduce_fusion), channel_id=1, source_target_pairs={{0,128},{32,160},{64,192},{96,224},{128,0},{160,32},{192,64},{224,... | collective-permute-start | bytes 110600 | tf_op jit(solution)/shard_map/reduce_grads/ppermute | solution.py:317
  106.7 0.9 collective-permute-start.7
  107.6 0.7 collective-permute-done.8
  108.3 2.8 %collective-permute-done.7 = f32[72,128]{1,0:T(8,128)S(1)} collective-permute-done((f32[72,128]{1,0:T(8,128)S(1)}, f32[72,128]{1,0:T(8,128)S(1)}, u32[]{:S(2)}, u32[]{:S(2)}) %collective-permute-start.7) | collective-permute-done | bytes 36896 | tf_op jit(solution)/shard_map/reduce_grads/ppermute | solution.py:317
  111.1 3.6 %collective-permute-start.9 = (f32[72,128]{1,0:T(8,128)S(1)}, f32[72,128]{1,0:T(8,128)S(1)}, u32[]{:S(2)}, u32[]{:S(2)}) collective-permute-start(f32[72,128]{1,0:T(8,128)S(1)} %add_add_fusion.m_ref), channel_id=1, source_target_pairs={{0,32},{32,0},{64,96},{96,64},{128,160},{160,128},{192,224},{224,1... | collective-permute-start | bytes 110600 | tf_op jit(solution)/shard_map/reduce_grads/ppermute | solution.py:317
  114.7 0.9 collective-permute-done.9.o_ref
  115.5 0.6 finish.1
  (10 shorter events, 0.1 us)
Async XLA Ops:
  2.8 39.4 %all-to-all-start = ((bf16[32,136,128]{2,1,0:T(8,128)(2,1)}), bf16[32,136,128]{2,1,0:T(8,128)(2,1)S(1)}, u32[]{:S(2)}, u32[]{:S(2)}) async-start(bf16[32,136,128]{2,1,0:T(8,128)(2,1)} %pack.1), calls=%async_computation | async-start | bytes 2228224 | tf_op jit(solution)/shard_map/send_features/all_to_all | solution.py:321
  42.2 31.5 %all-to-all-start.1 = ((bf16[32,128,128]{2,1,0:T(8,128)(2,1)}), bf16[32,128,128]{2,1,0:T(8,128)(2,1)S(1)}, u32[]{:S(2)}, u32[]{:S(2)}) async-start(bf16[32,128,128]{2,1,0:T(8,128)(2,1)} %aggregate.1), calls=%async_computation.1 | async-start | bytes 2097152 | tf_op jit(solution)/shard_map/send_aggregated/all_to_all | solution.py:326
  48.7 20.8 %copy-start.1 = (f32[256]{0:T(256)S(1)}, f32[256]{0:T(256)}, u32[]{:S(2)}) copy-start(f32[256]{0:T(256)} %param.16) | copy-start | bytes 3076
  48.7 3.7 %collective-permute-start = (bf16[32,8,128]{2,1,0:T(8,128)(2,1)S(1)}, bf16[32,8,128]{2,1,0:T(8,128)(2,1)S(1)}, u32[]{:S(2)}, u32[]{:S(2)}) collective-permute-start(bf16[32,8,128]{2,1,0:T(8,128)(2,1)S(1)} %slice.9), channel_id=1, source_target_pairs={{0,1},{1,0},{2,3},{3,2},{4,5},{5,4},{6,7},{7,6},{8,9},{9,8},{10,11... | collective-permute-start | bytes 196616 | tf_op jit(solution)/shard_map/weights_over_vgroup/ppermute | solution.py:330
  52.4 5.4 %collective-permute-start.2 = (bf16[32,16,128]{2,1,0:T(8,128)(2,1)S(1)}, bf16[32,16,128]{2,1,0:T(8,128)(2,1)S(1)}, u32[]{:S(2)}, u32[]{:S(2)}) collective-permute-start(bf16[32,16,128]{2,1,0:T(8,128)(2,1)S(1)} %get-tuple-element.25), channel_id=1, source_target_pairs={{0,128},{32,160},{64,192},{96,224},{128,0},{160,32},{192,64},{224,... | collective-permute-start | bytes 393224 | tf_op jit(solution)/shard_map/weights_over_vgroup/ppermute | solution.py:317
  55.3 4.4 %collective-permute-start.1 = (bf16[32,16,128]{2,1,0:T(8,128)(2,1)S(1)}, bf16[32,16,128]{2,1,0:T(8,128)(2,1)S(1)}, u32[]{:S(2)}, u32[]{:S(2)}) collective-permute-start(bf16[32,16,128]{2,1,0:T(8,128)(2,1)S(1)} %get-tuple-element.25), channel_id=1, source_target_pairs={{0,64},{32,96},{64,0},{96,32},{128,192},{160,224},{192,128},{224,1... | collective-permute-start | bytes 393224 | tf_op jit(solution)/shard_map/weights_over_vgroup/ppermute | solution.py:317
  55.6 5.3 %collective-permute-start.3 = (bf16[32,16,128]{2,1,0:T(8,128)(2,1)S(1)}, bf16[32,16,128]{2,1,0:T(8,128)(2,1)S(1)}, u32[]{:S(2)}, u32[]{:S(2)}) collective-permute-start(bf16[32,16,128]{2,1,0:T(8,128)(2,1)S(1)} %get-tuple-element.25), channel_id=1, source_target_pairs={{0,192},{32,224},{64,128},{96,160},{128,64},{160,96},{192,0},{224,... | collective-permute-start | bytes 393224 | tf_op jit(solution)/shard_map/weights_over_vgroup/ppermute | solution.py:317
  61.0 12.7 %copy-start = (bf16[512,256]{1,0:T(8,128)(2,1)S(1)}, bf16[512,256]{1,0:T(8,128)(2,1)}, u32[]{:S(2)}) copy-start(bf16[512,256]{1,0:T(8,128)(2,1)} %up_ref.1) | copy-start | bytes 786436
  61.0 8.5 %collective-permute-start.4 = (bf16[4,32,16,128]{3,2,1,0:T(8,128)(2,1)S(1)}, bf16[4,32,16,128]{3,2,1,0:T(8,128)(2,1)S(1)}, u32[]{:S(2)}, u32[]{:S(2)}) collective-permute-start(bf16[4,32,16,128]{3,2,1,0:T(8,128)(2,1)S(1)} %pad_maximum_fusion.w0), channel_id=1, source_target_pairs={{0,32},{32,0},{64,96},{96,64},{128,160},{160,128},{192,224},{224,1... | collective-permute-start | bytes 1572872 | tf_op jit(solution)/shard_map/weights_over_vgroup/ppermute | solution.py:317
  75.2 5.7 %collective-permute-start.5 = (bf16[32,72,128]{2,1,0:T(8,128)(2,1)S(1)}, bf16[32,72,128]{2,1,0:T(8,128)(2,1)S(1)}, u32[]{:S(2)}, u32[]{:S(2)}) collective-permute-start(bf16[32,72,128]{2,1,0:T(8,128)(2,1)S(1)} %slice_bitcast_fusion), channel_id=1, source_target_pairs={{0,32},{32,0},{64,96},{96,64},{128,160},{160,128},{192,224},{224,1... | collective-permute-start | bytes 1769480 | tf_op jit(solution)/shard_map/reduce_grads/ppermute | solution.py:317
  103.9 4.4 %collective-permute-start.8 = (f32[72,128]{1,0:T(8,128)S(1)}, f32[72,128]{1,0:T(8,128)S(1)}, u32[]{:S(2)}, u32[]{:S(2)}) collective-permute-start(f32[72,128]{1,0:T(8,128)S(1)} %convert_reduce_fusion), channel_id=1, source_target_pairs={{0,128},{32,160},{64,192},{96,224},{128,0},{160,32},{192,64},{224,... | collective-permute-start | bytes 110600 | tf_op jit(solution)/shard_map/reduce_grads/ppermute | solution.py:317
  106.7 4.3 %collective-permute-start.7 = (f32[72,128]{1,0:T(8,128)S(1)}, f32[72,128]{1,0:T(8,128)S(1)}, u32[]{:S(2)}, u32[]{:S(2)}) collective-permute-start(f32[72,128]{1,0:T(8,128)S(1)} %convert_reduce_fusion), channel_id=1, source_target_pairs={{0,192},{32,224},{64,128},{96,160},{128,64},{160,96},{192,0},{224,... | collective-permute-start | bytes 110600 | tf_op jit(solution)/shard_map/reduce_grads/ppermute | solution.py:317
  107.6 3.5 %collective-permute-start.6 = (f32[72,128]{1,0:T(8,128)S(1)}, f32[72,128]{1,0:T(8,128)S(1)}, u32[]{:S(2)}, u32[]{:S(2)}) collective-permute-start(f32[72,128]{1,0:T(8,128)S(1)} %convert_reduce_fusion), channel_id=1, source_target_pairs={{0,64},{32,96},{64,0},{96,32},{128,192},{160,224},{192,128},{224,1... | collective-permute-start | bytes 110600 | tf_op jit(solution)/shard_map/reduce_grads/ppermute | solution.py:317
  111.1 4.4 %collective-permute-start.9 = (f32[72,128]{1,0:T(8,128)S(1)}, f32[72,128]{1,0:T(8,128)S(1)}, u32[]{:S(2)}, u32[]{:S(2)}) collective-permute-start(f32[72,128]{1,0:T(8,128)S(1)} %add_add_fusion.m_ref), channel_id=1, source_target_pairs={{0,32},{32,0},{64,96},{96,64},{128,160},{160,128},{192,224},{224,1... | collective-permute-start | bytes 110600 | tf_op jit(solution)/shard_map/reduce_grads/ppermute | solution.py:317
